TPU v7x, 32 devices: a whole 2x2x4 slice. The times are simulated.
32 devices in a mesh: seq: 4 (over x, core), fsdp: 8 (over z, y).
Axes of the slice: x: 2, y: 2, z: 4, core: 2. Of those that a mesh axis runs over, the one named last changes fastest.
Arguments:
- inputs: bfloat16 [16, 1568, 1024], P('fsdp', 'seq'), may hold values from -7 to 7
- cotangent: bfloat16 [16, 1568, 1024], P('fsdp', 'seq'), may hold values from -6 to 6
- valid: int32 [16, 1568], P('fsdp'), may hold values from 0 to 1, as said below
- ln1_gain: bfloat16 [1024], P('fsdp'), may hold values from 0.25 to 1.75
- ln1_bias: bfloat16 [1024], P('fsdp'), may hold values from -1.75 to 1.75
- qkv_weight: bfloat16 [1024, 3072], P('fsdp'), may hold values from -0.1875 to 0.1875
- q_bias: bfloat16 [1024], P('fsdp'), may hold values from -3 to 3
- v_bias: bfloat16 [1024], P('fsdp'), may hold values from -0.3125 to 0.3125
- out_weight: bfloat16 [1024, 1024], P('fsdp'), may hold values from -2 to 2
- out_bias: bfloat16 [1024], P('fsdp'), may hold values from -1.75 to 1.75
- ln2_gain: bfloat16 [1024], P('fsdp'), may hold values from 0.25 to 1.75
- ln2_bias: bfloat16 [1024], P('fsdp'), may hold values from -1.75 to 1.75
- fc1_weight: bfloat16 [1024, 4096], P('fsdp'), may hold values from -0.1875 to 0.1875
- fc1_bias: bfloat16 [4096], P('fsdp'), may hold values from -1.75 to 1.75
- fc2_weight: bfloat16 [4096, 1024], P('fsdp'), may hold values from -0.09375 to 0.09375
- fc2_bias: bfloat16 [1024], P('fsdp'), may hold values from -1.75 to 1.75
Outputs:
- output: bfloat16 [16, 1568, 1024], P('fsdp', 'seq')
- input_grad: bfloat16 [16, 1568, 1024], P('fsdp', 'seq')
- ln1_gain_grad: float32 [1024], P('fsdp')
- ln1_bias_grad: float32 [1024], P('fsdp')
- qkv_weight_grad: float32 [1024, 3072], P('fsdp')
- q_bias_grad: float32 [1024], P('fsdp')
- v_bias_grad: float32 [1024], P('fsdp')
- out_weight_grad: float32 [1024, 1024], P('fsdp')
- out_bias_grad: float32 [1024], P('fsdp')
- ln2_gain_grad: float32 [1024], P('fsdp')
- ln2_bias_grad: float32 [1024], P('fsdp')
- fc1_weight_grad: float32 [1024, 4096], P('fsdp')
- fc1_bias_grad: float32 [4096], P('fsdp')
- fc2_weight_grad: float32 [4096, 1024], P('fsdp')
- fc2_bias_grad: float32 [1024], P('fsdp')
- branch_rms: float32 [3], replicated
Inputs may be any that keep to these rules, and one draw needn't show every extreme that they name: In every clip the valid tokens are a leading run of 392 tokens or more; some clip is valid in all its tokens.
All inputs are finite; a program needn't handle non-finite values.
Results may differ from a plain program's by a relative error of at most 0.015.
Values may be sent and summed in bfloat16 or wider, within the bound.
No kernel may reach another device: no remote copies, remote signals or barrier semaphores. Data moves between devices by JAX's collectives and lax.ppermute only.
A program may use at most 192 MiB of HBM per device.

v0:
```python
from functools import partial

import jax
import jax.numpy as jnp
from jax import lax
from jax.sharding import PartitionSpec as P

HEADS = 16
HEAD = 64


EPS = 1e-06
masked_score = -1e30


def layer_norm(values, gain, bias):
    center = values - jnp.mean(values, axis=-1, keepdims=True)
    spread = jnp.mean(center * center, axis=-1, keepdims=True)
    return center * lax.rsqrt(spread + EPS) * gain + bias


def gelu_exact(values):
    return jax.nn.gelu(values, approximate=False)


def contract_rows(left, right):
    return lax.dot_general(
        left, right, (((0,), (0,)), ((), ())), preferred_element_type=jnp.float32
    )


def times_transpose(left, right):
    return lax.dot_general(
        left, right, (((1,), (1,)), ((), ())), preferred_element_type=jnp.float32
    )


def column_sum(values):
    return jnp.sum(values, axis=0, dtype=jnp.float32)


def head_major(values, heads_here):
    clip_count, length, total_width = values.shape
    return jnp.moveaxis(values.reshape(clip_count, length, heads_here, HEAD), 2, 0)


def token_major(values):
    heads_here, clip_count, length, head_width = values.shape
    return jnp.moveaxis(values, 0, 2).reshape(clip_count, length, heads_here * head_width)


def attend_forward(pieces, keep):
    queries, key_rows, value_rows = pieces
    scores = jnp.einsum("cqd,ckd->cqk", queries, key_rows, preferred_element_type=jnp.float32)
    scores = jnp.where(keep[:, None, :], scores, masked_score)
    highest = jnp.max(scores, axis=-1, keepdims=True)
    weights = jnp.exp(scores - highest)
    totals = jnp.sum(weights, axis=-1, keepdims=True)
    probs_low = (weights / totals).astype(jnp.bfloat16)
    context = jnp.einsum(
        "cqk,ckd->cqd", probs_low, value_rows, preferred_element_type=jnp.float32
    ).astype(jnp.bfloat16)
    return (context, (highest + jnp.log(totals))[..., 0])


def attend_backward(pieces, keep):
    queries, key_rows, value_rows, log_total, grad_context = pieces
    scores = jnp.einsum("cqd,ckd->cqk", queries, key_rows, preferred_element_type=jnp.float32)
    scores = jnp.where(keep[:, None, :], scores, masked_score)
    probs = jnp.exp(scores - log_total[..., None])
    grad_probs = jnp.einsum(
        "cqd,ckd->cqk", grad_context, value_rows, preferred_element_type=jnp.float32
    )
    inner = jnp.sum(grad_probs * probs, axis=-1, keepdims=True)
    grad_scores = (probs * (grad_probs - inner)).astype(jnp.bfloat16)
    grad_queries = jnp.einsum(
        "cqk,ckd->cqd", grad_scores, key_rows, preferred_element_type=jnp.float32
    ).astype(jnp.bfloat16)
    grad_keys = jnp.einsum(
        "cqk,cqd->ckd", grad_scores, queries, preferred_element_type=jnp.float32
    ).astype(jnp.bfloat16)
    grad_values = jnp.einsum(
        "cqk,cqd->ckd", probs.astype(jnp.bfloat16), grad_context, preferred_element_type=jnp.float32
    ).astype(jnp.bfloat16)
    return (grad_queries, grad_keys, grad_values)


def body(
    inputs,
    cotangent,
    valid,
    ln1_gain,
    ln1_bias,
    qkv_weight,
    q_bias,
    v_bias,
    out_weight,
    out_bias,
    ln2_gain,
    ln2_bias,
    fc1_weight,
    fc1_bias,
    fc2_weight,
    fc2_bias,
):
    clip_count, row_count, model_width = inputs.shape
    seq_count = lax.axis_size("seq")
    heads_here = HEADS // seq_count
    scale_factor = HEAD ** (-0.5)
    shaped = (clip_count, row_count, model_width)
    key_valid = valid > 0
    full_ln1_gain, full_ln1_bias, full_qkv, full_q_bias, full_v_bias, full_out, full_out_bias = (
        lax.all_gather(ln1_gain, "fsdp", axis=0, tiled=True),
        lax.all_gather(ln1_bias, "fsdp", axis=0, tiled=True),
        lax.all_gather(qkv_weight, "fsdp", axis=0, tiled=True),
        lax.all_gather(q_bias, "fsdp", axis=0, tiled=True),
        lax.all_gather(v_bias, "fsdp", axis=0, tiled=True),
        lax.all_gather(out_weight, "fsdp", axis=0, tiled=True),
        lax.all_gather(out_bias, "fsdp", axis=0, tiled=True),
    )
    residual_in = inputs.reshape(clip_count * row_count, model_width).astype(jnp.float32)
    h_one, norm_one_pull = jax.vjp(
        layer_norm,
        residual_in,
        full_ln1_gain.astype(jnp.float32),
        full_ln1_bias.astype(jnp.float32),
    )
    h_one_low = h_one.astype(jnp.bfloat16)
    mixed = jnp.dot(h_one_low, full_qkv, preferred_element_type=jnp.float32)
    queries = ((mixed[:, :model_width] + full_q_bias.astype(jnp.float32)) * scale_factor).astype(
        jnp.bfloat16
    )
    key_rows = mixed[:, model_width : 2 * model_width].astype(jnp.bfloat16)
    value_rows = (mixed[:, 2 * model_width :] + full_v_bias.astype(jnp.float32)).astype(
        jnp.bfloat16
    )
    query_heads, key_heads, value_heads = (
        lax.all_to_all(queries.reshape(shaped), "seq", split_axis=2, concat_axis=1, tiled=True),
        lax.all_to_all(key_rows.reshape(shaped), "seq", split_axis=2, concat_axis=1, tiled=True),
        lax.all_to_all(value_rows.reshape(shaped), "seq", split_axis=2, concat_axis=1, tiled=True),
    )
    stacked = (
        head_major(query_heads, heads_here),
        head_major(key_heads, heads_here),
        head_major(value_heads, heads_here),
    )
    context_heads, log_totals = lax.map(partial(attend_forward, keep=key_valid), stacked)
    context_tokens = lax.all_to_all(
        token_major(context_heads), "seq", split_axis=1, concat_axis=2, tiled=True
    )
    context_low = context_tokens.reshape(-1, model_width)
    attn_branch = jnp.dot(
        context_low, full_out, preferred_element_type=jnp.float32
    ) + full_out_bias.astype(jnp.float32)
    residual_mid = residual_in + attn_branch
    full_ln2_gain, full_ln2_bias, full_fc1, full_fc1_bias, full_fc2, full_fc2_bias = (
        lax.all_gather(ln2_gain, "fsdp", axis=0, tiled=True),
        lax.all_gather(ln2_bias, "fsdp", axis=0, tiled=True),
        lax.all_gather(fc1_weight, "fsdp", axis=0, tiled=True),
        lax.all_gather(fc1_bias, "fsdp", axis=0, tiled=True),
        lax.all_gather(fc2_weight, "fsdp", axis=0, tiled=True),
        lax.all_gather(fc2_bias, "fsdp", axis=0, tiled=True),
    )
    h_two, norm_two_pull = jax.vjp(
        layer_norm,
        residual_mid,
        full_ln2_gain.astype(jnp.float32),
        full_ln2_bias.astype(jnp.float32),
    )
    h_two_low = h_two.astype(jnp.bfloat16)
    hidden = jnp.dot(
        h_two_low, full_fc1, preferred_element_type=jnp.float32
    ) + full_fc1_bias.astype(jnp.float32)
    active, gelu_pull = jax.vjp(gelu_exact, hidden)
    active_low = active.astype(jnp.bfloat16)
    mlp_branch = jnp.dot(
        active_low, full_fc2, preferred_element_type=jnp.float32
    ) + full_fc2_bias.astype(jnp.float32)
    residual_out = residual_mid + mlp_branch
    own_valid = (
        lax.dynamic_slice_in_dim(valid, lax.axis_index("seq") * row_count, row_count, 1)
        .reshape(-1, 1)
        .astype(jnp.float32)
    )
    totals = lax.psum(
        (
            jnp.sum(own_valid * residual_out * residual_out),
            jnp.sum(own_valid * attn_branch * attn_branch),
            jnp.sum(own_valid * mlp_branch * mlp_branch),
            jnp.sum(own_valid),
        ),
        ("seq", "fsdp"),
    )
    branch_rms = jnp.sqrt(jnp.stack([totals[0], totals[1], totals[2]]) / (totals[3] * model_width))
    full_qkv, full_out, full_fc1, full_fc2 = (
        lax.all_gather(qkv_weight, "fsdp", axis=0, tiled=True),
        lax.all_gather(out_weight, "fsdp", axis=0, tiled=True),
        lax.all_gather(fc1_weight, "fsdp", axis=0, tiled=True),
        lax.all_gather(fc2_weight, "fsdp", axis=0, tiled=True),
    )
    grad_output = cotangent.reshape(-1, model_width)
    grad_fc2_weight = contract_rows(active_low, grad_output)
    grad_fc2_bias = column_sum(grad_output)
    grad_hidden = gelu_pull(times_transpose(grad_output, full_fc2))[0].astype(jnp.bfloat16)
    grad_fc1_weight = contract_rows(h_two_low, grad_hidden)
    grad_fc1_bias = column_sum(grad_hidden)
    grad_mid, grad_ln2_gain, grad_ln2_bias = norm_two_pull(times_transpose(grad_hidden, full_fc1))
    grad_residual = grad_output.astype(jnp.float32) + grad_mid
    grad_attn = grad_residual.astype(jnp.bfloat16)
    grad_out_weight = contract_rows(context_low, grad_attn)
    grad_out_bias = column_sum(grad_attn)
    grad_context = times_transpose(grad_attn, full_out).astype(jnp.bfloat16).reshape(shaped)
    grad_context_heads = lax.all_to_all(
        grad_context, "seq", split_axis=2, concat_axis=1, tiled=True
    )
    grad_query_heads, grad_key_heads, grad_value_heads = lax.map(
        partial(attend_backward, keep=key_valid),
        stacked + (log_totals, head_major(grad_context_heads, heads_here)),
    )
    grad_queries, grad_keys, grad_values = (
        lax.all_to_all(
            token_major(grad_query_heads), "seq", split_axis=1, concat_axis=2, tiled=True
        ),
        lax.all_to_all(token_major(grad_key_heads), "seq", split_axis=1, concat_axis=2, tiled=True),
        lax.all_to_all(
            token_major(grad_value_heads), "seq", split_axis=1, concat_axis=2, tiled=True
        ),
    )
    grad_mixed = jnp.concatenate(
        [
            (grad_queries * scale_factor).reshape(-1, model_width),
            grad_keys.reshape(-1, model_width),
            grad_values.reshape(-1, model_width),
        ],
        axis=1,
    )
    grad_qkv_weight = contract_rows(h_one_low, grad_mixed)
    grad_q_bias = column_sum(grad_mixed[:, :model_width])
    grad_v_bias = column_sum(grad_mixed[:, 2 * model_width :])
    grad_first, grad_ln1_gain, grad_ln1_bias = norm_one_pull(times_transpose(grad_mixed, full_qkv))
    input_grad = (grad_residual + grad_first).astype(jnp.bfloat16).reshape(shaped)
    output = residual_out.astype(jnp.bfloat16).reshape(shaped)
    attn_part = (
        lax.psum_scatter(grad_ln1_gain, "fsdp", scatter_dimension=0, tiled=True),
        lax.psum_scatter(grad_ln1_bias, "fsdp", scatter_dimension=0, tiled=True),
        lax.psum_scatter(grad_qkv_weight, "fsdp", scatter_dimension=0, tiled=True),
        lax.psum_scatter(grad_q_bias, "fsdp", scatter_dimension=0, tiled=True),
        lax.psum_scatter(grad_v_bias, "fsdp", scatter_dimension=0, tiled=True),
        lax.psum_scatter(grad_out_weight, "fsdp", scatter_dimension=0, tiled=True),
        lax.psum_scatter(grad_out_bias, "fsdp", scatter_dimension=0, tiled=True),
    )
    mlp_part = (
        lax.psum_scatter(grad_ln2_gain, "fsdp", scatter_dimension=0, tiled=True),
        lax.psum_scatter(grad_ln2_bias, "fsdp", scatter_dimension=0, tiled=True),
        lax.psum_scatter(grad_fc1_weight, "fsdp", scatter_dimension=0, tiled=True),
        lax.psum_scatter(grad_fc1_bias, "fsdp", scatter_dimension=0, tiled=True),
        lax.psum_scatter(grad_fc2_weight, "fsdp", scatter_dimension=0, tiled=True),
        lax.psum_scatter(grad_fc2_bias, "fsdp", scatter_dimension=0, tiled=True),
    )
    shards = (
        lax.psum(attn_part[0].astype(jnp.bfloat16), "seq").astype(jnp.float32),
        lax.psum(attn_part[1].astype(jnp.bfloat16), "seq").astype(jnp.float32),
        lax.psum(attn_part[2].astype(jnp.bfloat16), "seq").astype(jnp.float32),
        lax.psum(attn_part[3].astype(jnp.bfloat16), "seq").astype(jnp.float32),
        lax.psum(attn_part[4].astype(jnp.bfloat16), "seq").astype(jnp.float32),
        lax.psum(attn_part[5].astype(jnp.bfloat16), "seq").astype(jnp.float32),
        lax.psum(attn_part[6].astype(jnp.bfloat16), "seq").astype(jnp.float32),
        lax.psum(mlp_part[0].astype(jnp.bfloat16), "seq").astype(jnp.float32),
        lax.psum(mlp_part[1].astype(jnp.bfloat16), "seq").astype(jnp.float32),
        lax.psum(mlp_part[2].astype(jnp.bfloat16), "seq").astype(jnp.float32),
        lax.psum(mlp_part[3].astype(jnp.bfloat16), "seq").astype(jnp.float32),
        lax.psum(mlp_part[4].astype(jnp.bfloat16), "seq").astype(jnp.float32),
        lax.psum(mlp_part[5].astype(jnp.bfloat16), "seq").astype(jnp.float32),
    )
    return (
        output,
        input_grad,
        shards[0],
        shards[1],
        shards[2],
        shards[3],
        shards[4],
        shards[5],
        shards[6],
        shards[7],
        shards[8],
        shards[9],
        shards[10],
        shards[11],
        shards[12],
        branch_rms,
    )


def solution(mesh):
    return jax.shard_map(
        body,
        mesh=mesh,
        in_specs=(
            P("fsdp", "seq", None),
            P("fsdp", "seq", None),
            P("fsdp", None),
            P("fsdp"),
            P("fsdp"),
            P("fsdp", None),
            P("fsdp"),
            P("fsdp"),
            P("fsdp", None),
            P("fsdp"),
            P("fsdp"),
            P("fsdp"),
            P("fsdp", None),
            P("fsdp"),
            P("fsdp", None),
            P("fsdp"),
        ),
        out_specs=(
            P("fsdp", "seq", None),
            P("fsdp", "seq", None),
            P("fsdp"),
            P("fsdp"),
            P("fsdp", None),
            P("fsdp"),
            P("fsdp"),
            P("fsdp", None),
            P("fsdp"),
            P("fsdp"),
            P("fsdp"),
            P("fsdp", None),
            P("fsdp"),
            P("fsdp", None),
            P("fsdp"),
            P(),
        ),
        check_vma=False,
    )
```

profile of v0, /device:TPU:0, one launch (start us, length us, event | category | flops | bytes accessed | tf_op | source)
XLA Modules:
  0.0 1739.1 jit_solution(8141717129016121572)
XLA Ops:
  12.0 22.4 %all-gather = bf16[8,1,128]{2,1,0:T(2,128)(2,1)S(1)} all-gather(bf16[1,1,128]{2,1,0:T(2,128)(2,1)S(1)} %bitcast.283), channel_id=1, replica_groups=mesh['seq'=4,'fsdp'=8] {'fsdp'}, dimensions={0}, use_global_device_ids=true | all-gather | bytes 2304 | tf_op jit(solution)/shard_map/all_gather | solution.py:113
  34.4 16.5 all-gather.1
  50.9 18.4 %all-gather.2 = bf16[8,1,128]{2,1,0:T(2,128)(2,1)S(1)} all-gather(bf16[1,1,128]{2,1,0:T(2,128)(2,1)S(1)} %bitcast.285), channel_id=1, replica_groups=mesh['seq'=4,'fsdp'=8] {'fsdp'}, dimensions={0}, use_global_device_ids=true | all-gather | bytes 2304 | tf_op jit(solution)/shard_map/all_gather | solution.py:116
  69.3 16.5 all-gather.3
  86.5 25.7 %all-gather.14.cloned.1.call-done = bf16[1024,3072]{1,0:T(8,128)(2,1)} async-done(((bf16[128,3072]{1,0:T(8,128)(2,1)}), bf16[1024,3072]{1,0:T(8,128)(2,1)}) %all-gather.14.cloned.1.call-update) | async-done | bytes 6291472 | tf_op jit(solution)/shard_map/all_gather | solution.py:115
  137.6 19.5 %all-to-all-done = bf16[2,392,1024]{1,0,2:T(2,128)(2,1)S(1)} async-done(((bf16[2,392,1024]{1,0,2:T(2,128)(2,1)}), bf16[2,392,1024]{1,0,2:T(2,128)(2,1)S(1)}, u32[]{:S(2)}, u32[]{:S(2)}) %all-to-all-start) | async-done | bytes 1605664 | tf_op jit(solution)/shard_map/all_to_all | solution.py:138
  171.0 16.2 all-to-all-done.2
  229.9 59.0 %while.26 = (s32[]{:T(128)}, bf16[4,2,1568,64]{2,3,1,0:T(8,128)(2,1)}, f32[4,2,1568]{2,1,0:T(2,128)}, pred[2,1568]{1,0:T(4,128)(4,1)S(1)}, bf16[4,2,1568,64]{2,3...) while((s32[]{:T(128)}, ...), condition=%wide.region_5.6_spmd, body=%wide.region_2.5_spmd.sunk | while | flops 1303268352 | bytes 60827604 | solution.py:147
  302.0 18.2 %all-gather.4 = bf16[8,1,128]{2,1,0:T(2,128)(2,1)S(1)} all-gather(bf16[1,1,128]{2,1,0:T(2,128)(2,1)S(1)} %bitcast.287), channel_id=1, replica_groups=mesh['seq'=4,'fsdp'=8] {'fsdp'}, dimensions={0}, use_global_device_ids=true | all-gather | bytes 2304 | tf_op jit(solution)/shard_map/all_gather | solution.py:119
  320.2 16.4 all-gather.5
  336.6 18.4 %all-gather.6 = bf16[8,1,128]{2,1,0:T(2,128)(2,1)S(1)} all-gather(bf16[1,1,128]{2,1,0:T(2,128)(2,1)S(1)} %bitcast.289), channel_id=1, replica_groups=mesh['seq'=4,'fsdp'=8] {'fsdp'}, dimensions={0}, use_global_device_ids=true | all-gather | bytes 2304 | tf_op jit(solution)/shard_map/all_gather | solution.py:158
  355.1 26.5 %all-gather.7 = bf16[8,1,512]{2,1,0:T(2,128)(2,1)S(1)} all-gather(bf16[1,1,512]{2,1,0:T(2,128)(2,1)S(1)} %reshape.266), channel_id=1, replica_groups=mesh['seq'=4,'fsdp'=8] {'fsdp'}, dimensions={0}, use_global_device_ids=true | all-gather | bytes 9216 | tf_op jit(solution)/shard_map/all_gather | solution.py:160
  383.7 16.3 all-gather.8
  410.9 13.7 fusion.67
  424.7 40.7 %convert_reduce_fusion = (f32[4096]{0:T(1024)}, bf16[784,4096]{1,0:T(8,128)(2,1)}, f32[784,4096]{1,0:T(8,128)S(1)}) fusion(f32[784,4096]{1,0:T(8,128)} %fusion.67, f32[4096]{0:T(1024)S(1)} %bitcast.262, bf16[784,1024]{1,0:T(8,128)(2,1)} %bitcast.227, bf16[4096,1024]{1,0:T(8,128)(2,1)} %all-gather.20.cloned.1.call-done), kind=kOutput, calls=%fused_computation.56 | convolution fusion | flops 6817509376 | bytes 42139648 | tf_op jit(solution)/shard_map/dot_general | solution.py:33
  513.2 19.3 %all-to-all-done.4 = bf16[2,392,1024]{1,0,2:T(2,128)(2,1)S(1)} async-done(((bf16[2,392,1024]{1,0,2:T(2,128)(2,1)}), bf16[2,392,1024]{1,0,2:T(2,128)(2,1)S(1)}, u32[]{:S(2)}, u32[]{:S(2)}) %all-to-all-start.4) | async-done | bytes 1605664 | tf_op jit(solution)/shard_map/all_to_all | solution.py:213
  544.8 235.6 %while.27 = (s32[]{:T(128)}, bf16[4,2,1568,64]{2,3,1,0:T(8,128)(2,1)}, bf16[4,2,1568,64]{2,3,1,0:T(8,128)(2,1)}, bf16[4,2,1568,64]{2,3,1,0:T(8,128)(2,1)}, pred[...) while((s32[]{:T(128)}, ...), condition=%wide.region_12.13_spmd, body=%wide.region_10.12_spmd.sunk | while | flops 3186975744 | bytes 154863216 | solution.py:216
  555.8 17.3 multiply_reduce_fusion.8
  573.1 14.1 multiply_convert_fusion.3
  615.2 17.1 multiply_reduce_fusion.8
  632.3 13.7 multiply_convert_fusion.3
  673.8 17.1 multiply_reduce_fusion.8
  732.5 17.1 multiply_reduce_fusion.8
  822.3 15.4 all-to-all-done.6
  846.3 15.3 all-to-all-done.7
  877.6 14.8 fusion.66
  893.8 14.5 fusion.76
  912.6 42.8 %all-reduce.9 = (f32[1]{0:T(128)}, f32[1]{0:T(128)}, f32[1]{0:T(128)}, f32[]{:T(128)}) all-reduce(f32[1]{0:T(128)} %bitcast.74, f32[1]{0:T(128)} %bitcast.73, f32[1]{0:T(128)} %bitcast.72, f32[]{:T(128)} %get-tuple-element.252), channel_id=1, replica_groups=mesh['seq'=4,'fsdp'=8] {'seq','fsdp'}, use_global_device_ids=true, to_apply=%region_56.57 | all-reduce | flops 4 | bytes 32 | tf_op jit(solution)/shard_map/psum | solution.py:185
  971.3 110.5 %reduce-scatter.5.cloned.1.call-done = f32[128,3072]{1,0:T(8,128)} async-done(((f32[1024,3072]{1,0:T(8,128)}), f32[128,3072]{1,0:T(8,128)}) %reduce-scatter.5.cloned.1.call-update) | async-done | bytes 1572880 | tf_op jit(solution)/shard_map/reduce_scatter | solution.py:246
  1084.2 283.7 %reduce-scatter.9.cloned.1.call-done = f32[128,4096]{1,0:T(8,128)} async-done(((f32[1024,4096]{1,0:T(8,128)}), f32[128,4096]{1,0:T(8,128)}) %reduce-scatter.9.cloned.1.call-update) | async-done | bytes 2097168 | tf_op jit(solution)/shard_map/reduce_scatter | solution.py:255
  1370.6 282.8 %reduce-scatter.11.cloned.1.call-done = f32[512,1024]{1,0:T(8,128)} async-done(((f32[4096,1024]{1,0:T(8,128)}), f32[512,1024]{1,0:T(8,128)}) %reduce-scatter.11.cloned.1.call-update) | async-done | bytes 2097168 | tf_op jit(solution)/shard_map/reduce_scatter | solution.py:257
  1659.3 35.7 %all-reduce.10 = (bf16[1024]{0:T(1024)(128)(2,1)S(1)}, bf16[1024]{0:T(1024)(128)(2,1)S(1)}, bf16[1024]{0:T(1024)(128)(2,1)S(1)}, bf16[1024]{0:T(1024)(128)(2,1)S...) all-reduce(f32[1024]{0:T(1024)S(1)} %get-tuple-element.185, ...), channel_id=2, replica_groups=mesh['seq'=4,'fsdp'=8] {'fsdp'}, use_global_device_ids=true, to_apply=%region_16.17.clone | all-reduce | flops 12288 | bytes 73728
  (346 shorter events, 504.8 us)
Async XLA Ops:
  7.2 62.0 %copy-start.66 = (bf16[128]{0:T(256)(128)(2,1)S(1)}, bf16[128]{0:T(256)(128)(2,1)}, u32[]{:S(2)}) copy-start(bf16[128]{0:T(256)(128)(2,1)} %param.27) | copy-start | bytes 772
  7.2 104.9 %all-gather.14.cloned.1.call-start = ((), (), s32[]{:S(2)}) async-start(), calls=%async_computation.12 | async-start | bytes 7077888 | tf_op jit(solution)/shard_map/all_gather | solution.py:115
  8.0 395.0 %all-gather.16.cloned.1.call-start = ((), (), s32[]{:S(2)}) async-start(), calls=%async_computation.13 | async-start | bytes 2359296 | tf_op jit(solution)/shard_map/all_gather | solution.py:118
  8.7 401.1 %all-gather.18.cloned.1.call-start = ((), (), s32[]{:S(2)}) async-start(), calls=%async_computation.14 | async-start | bytes 9437184 | tf_op jit(solution)/shard_map/all_gather | solution.py:159
  11.3 108.1 %copy-start.30 = (f32[784]{0:T(1024)}, f32[784]{0:T(1024)S(1)}, u32[]{:S(2)}) copy-start(f32[784]{0:T(1024)S(1)} %div.53) | copy-start | bytes 9412
  11.9 73.8 %copy-start.43 = (f32[784]{0:T(1024)}, f32[784]{0:T(1024)S(1)}, u32[]{:S(2)}) copy-start(f32[784]{0:T(1024)S(1)} %add.176) | copy-start | bytes 9412
  11.9 73.8 %copy-start.32 = (f32[784]{0:T(1024)}, f32[784]{0:T(1024)S(1)}, u32[]{:S(2)}) copy-start(f32[784]{0:T(1024)S(1)} %rsqrt.20) | copy-start | bytes 9412
  34.4 51.4 %copy-start.34 = (f32[8,1,128]{2,1,0:T(1,128)}, f32[8,1,128]{2,1,0:T(1,128)S(1)}, u32[]{:S(2)}) copy-start(f32[8,1,128]{2,1,0:T(1,128)S(1)} %convert_element_type.259) | copy-start | bytes 12292
  127.8 29.3 %all-to-all-start = ((bf16[2,392,1024]{1,0,2:T(2,128)(2,1)}), bf16[2,392,1024]{1,0,2:T(2,128)(2,1)S(1)}, u32[]{:S(2)}, u32[]{:S(2)}) async-start(bf16[2,392,1024]{1,0,2:T(2,128)(2,1)} %copy.128), calls=%async_computation | async-start | bytes 4194304 | tf_op jit(solution)/shard_map/all_to_all | solution.py:138
  157.0 30.2 %all-to-all-start.2 = ((bf16[2,392,1024]{1,0,2:T(2,128)(2,1)}), bf16[2,392,1024]{1,0,2:T(2,128)(2,1)}, u32[]{:S(2)}, u32[]{:S(2)}) async-start(bf16[2,392,1024]{1,0,2:T(2,128)(2,1)} %copy.134), calls=%async_computation.2 | async-start | bytes 4194304 | tf_op jit(solution)/shard_map/all_to_all | solution.py:140
  187.3 30.2 %all-to-all-start.1 = ((bf16[2,392,1024]{1,0,2:T(2,128)(2,1)}), bf16[2,392,1024]{1,0,2:T(2,128)(2,1)}, u32[]{:S(2)}, u32[]{:S(2)}) async-start(bf16[2,392,1024]{1,0,2:T(2,128)(2,1)} %copy.131), calls=%async_computation.1 | async-start | bytes 4194304 | tf_op jit(solution)/shard_map/all_to_all | solution.py:139
  191.7 232.9 %all-gather.20.cloned.1.call-start = ((), (), s32[]{:S(2)}) async-start(), calls=%async_computation.15 | async-start | bytes 9437184 | tf_op jit(solution)/shard_map/all_gather | solution.py:161
  288.8 114.1 %copy-start.2 = (bf16[4,2,1568,64]{2,3,1,0:T(8,128)(2,1)}, bf16[4,2,1568,64]{2,3,1,0:T(8,128)(2,1)S(1)}, u32[]{:S(2)}) copy-start(bf16[4,2,1568,64]{2,3,1,0:T(8,128)(2,1)S(1)} %get-tuple-element.457) | copy-start | bytes 4816900
  292.9 62.2 %copy-start.62 = (bf16[512]{0:T(512)(128)(2,1)S(1)}, bf16[512]{0:T(512)(128)(2,1)}, u32[]{:S(2)}) copy-start(bf16[512]{0:T(512)(128)(2,1)} %param.33) | copy-start | bytes 3076
  292.9 90.8 %copy-start.70 = (bf16[128]{0:T(256)(128)(2,1)S(1)}, bf16[128]{0:T(256)(128)(2,1)}, u32[]{:S(2)}) copy-start(bf16[128]{0:T(256)(128)(2,1)} %param.35) | copy-start | bytes 772
  298.4 102.2 %all-to-all-start.3 = ((bf16[2,1568,256]{2,0,1:T(2,128)(2,1)}), bf16[2,1568,256]{2,0,1:T(2,128)(2,1)S(1)}, u32[]{:S(2)}, u32[]{:S(2)}) async-start(bf16[2,1568,256]{2,0,1:T(2,128)(2,1)} %copy.141), calls=%async_computation.3 | async-start | bytes 3211264 | tf_op jit(solution)/shard_map/all_to_all | solution.py:148
  320.2 82.7 %copy-start.58 = (f32[8,1,128]{2,1,0:T(1,128)}, f32[8,1,128]{2,1,0:T(1,128)S(1)}, u32[]{:S(2)}) copy-start(f32[8,1,128]{2,1,0:T(1,128)S(1)} %convert_element_type.263) | copy-start | bytes 12292
  336.6 73.2 %copy-start.47 = (f32[8,1,128]{2,1,0:T(1,128)}, f32[8,1,128]{2,1,0:T(1,128)S(1)}, u32[]{:S(2)}) copy-start(f32[8,1,128]{2,1,0:T(1,128)S(1)} %convert_element_type.264) | copy-start | bytes 12292
  355.1 54.8 %copy-start.56 = (f32[8,1,128]{2,1,0:T(1,128)}, f32[8,1,128]{2,1,0:T(1,128)S(1)}, u32[]{:S(2)}) copy-start(f32[8,1,128]{2,1,0:T(1,128)S(1)} %convert_element_type.265) | copy-start | bytes 12292
  503.2 29.3 %all-to-all-start.4 = ((bf16[2,392,1024]{1,0,2:T(2,128)(2,1)}), bf16[2,392,1024]{1,0,2:T(2,128)(2,1)S(1)}, u32[]{:S(2)}, u32[]{:S(2)}) async-start(bf16[2,392,1024]{1,0,2:T(2,128)(2,1)} %copy.144), calls=%async_computation.4 | async-start | bytes 4194304 | tf_op jit(solution)/shard_map/all_to_all | solution.py:213
  506.9 462.7 %reduce-scatter.7.cloned.1.call-start = ((), (), s32[]{:S(2)}) async-start(), calls=%async_computation.17 | async-start | bytes 4718592 | tf_op jit(solution)/shard_map/reduce_scatter | solution.py:249
  788.7 24.1 %all-to-all-start.5 = ((bf16[2,1568,256]{2,0,1:T(2,128)(2,1)}), bf16[2,1568,256]{2,0,1:T(2,128)(2,1)S(1)}, u32[]{:S(2)}, u32[]{:S(2)}) async-start(bf16[2,1568,256]{2,0,1:T(2,128)(2,1)} %copy.152), calls=%async_computation.5 | async-start | bytes 3211264 | tf_op jit(solution)/shard_map/all_to_all | solution.py:221
  812.8 24.9 %all-to-all-start.6 = ((bf16[2,1568,256]{2,0,1:T(2,128)(2,1)}), bf16[2,1568,256]{2,0,1:T(2,128)(2,1)}, u32[]{:S(2)}, u32[]{:S(2)}) async-start(bf16[2,1568,256]{2,0,1:T(2,128)(2,1)} %copy.156), calls=%async_computation.6 | async-start | bytes 3211264 | tf_op jit(solution)/shard_map/all_to_all | solution.py:224
  837.6 24.0 %all-to-all-start.7 = ((bf16[2,1568,256]{2,0,1:T(2,128)(2,1)}), bf16[2,1568,256]{2,0,1:T(2,128)(2,1)S(1)}, u32[]{:S(2)}, u32[]{:S(2)}) async-start(bf16[2,1568,256]{2,0,1:T(2,128)(2,1)} %copy.160), calls=%async_computation.7 | async-start | bytes 3211264 | tf_op jit(solution)/shard_map/all_to_all | solution.py:225
  841.2 240.6 %reduce-scatter.5.cloned.1.call-start = ((), (), s32[]{:S(2)}) async-start(), calls=%async_computation.16 | async-start | bytes 14155776 | tf_op jit(solution)/shard_map/reduce_scatter | solution.py:246
  875.7 492.2 %reduce-scatter.9.cloned.1.call-start = ((), (), s32[]{:S(2)}) async-start(), calls=%async_computation.18 | async-start | bytes 18874368 | tf_op jit(solution)/shard_map/reduce_scatter | solution.py:255
  892.4 761.0 %reduce-scatter.11.cloned.1.call-start = ((), (), s32[]{:S(2)}) async-start(), calls=%async_computation.19 | async-start | bytes 18874368 | tf_op jit(solution)/shard_map/reduce_scatter | solution.py:257
  908.3 50.5 %copy-start.9 = (bf16[2,392,1024]{2,1,0:T(8,128)(2,1)S(1)}, bf16[2,392,1024]{2,1,0:T(8,128)(2,1)}, u32[]{:S(2)}) copy-start(bf16[2,392,1024]{2,1,0:T(8,128)(2,1)} %param.20) | copy-start | bytes 4816900
  908.3 50.5 %copy-start.31 = (f32[784]{0:T(1024)S(1)}, f32[784]{0:T(1024)}, u32[]{:S(2)}) copy-start(f32[784]{0:T(1024)} %copy-done.30) | copy-start | bytes 9412
  908.4 817.3 %all-reduce.15.cloned.1.call-start = ((), (), s32[]{:S(2)}) async-start(), calls=%async_computation.20 | async-start | bytes 6291456 | tf_op jit(solution)/shard_map/psum | solution.py:263
  1370.6 285.6 %copy-start.11 = (bf16[2,1568,256]{2,0,1:T(2,128)(2,1)S(1)}, bf16[2,1568,256]{2,0,1:T(2,128)(2,1)}, u32[]{:S(2)}) copy-start(bf16[2,1568,256]{2,0,1:T(2,128)(2,1)} %copy-done.10) | copy-start | bytes 4816900
  1656.1 50.8 %copy-start.44 = (f32[784]{0:T(1024)S(1)}, f32[784]{0:T(1024)}, u32[]{:S(2)}) copy-start(f32[784]{0:T(1024)} %copy-done.43) | copy-start | bytes 9412
  (60 other events, 710.4 us)
Sparse Core Ops, SparseCore 0:
  10.2 101.8 all-gather.13
  114.3 47.4 all-gather.15
  164.0 123.4 all-gather.17
  289.4 123.5 all-gather.19
  513.3 87.2 reduce-scatter.6
  875.8 205.9 reduce-scatter.4
  1086.1 281.7 reduce-scatter.8
  1371.6 281.6 reduce-scatter.10
  1657.3 68.3 all-reduce.14
where the time goes:
time: 1750 us; the launch traced here: 1740 us
  waiting for transfers between devices  820 us (47%)
  matrix products  365 us (21%)
  blocking collectives  255 us (15%)
  other arithmetic  130 us (7%)
  local copies, waits for them, and re-layouts  121 us (7%)
  starting transfers between devices  32 us (2%)
    reduce_scatter x1, waiting for transfers between devices, body(): lax.psum_scatter(grad_fc1_weight, 'fsdp', scatter_dimension=0, tiled=True)  284 us
    reduce_scatter x1, waiting for transfers between devices, body(): lax.psum_scatter(grad_fc2_weight, 'fsdp', scatter_dimension=0, tiled=True)  283 us
    reduce_scatter x1, waiting for transfers between devices, body(): lax.psum_scatter(grad_qkv_weight, 'fsdp', scatter_dimension=0, tiled=True)  110 us
    dot_general x4, matrix products, attend_backward(): jnp.einsum('cqd,ckd->cqk', grad_context, value_rows, preferred_element_ty...  68.6 us
    dot_general x4, matrix products, times_transpose(): lax.dot_general(left, right, (((1,), (1,)), ((), ())), preferred_element_...  64.6 us
    convert_element_type x4, other arithmetic, attend_backward(): grad_scores = (probs * (grad_probs - inner)).astype(jnp.bfloat16)  55.1 us
    dot_general x4, matrix products, contract_rows(): lax.dot_general(left, right, (((0,), (0,)), ((), ())), preferred_element_...  44.9 us
    psum x1, blocking collectives, body(): lax.psum((jnp.sum(own_valid * residual_out * residual_out), jnp.sum(own_v...  42.8 us
  transfers between devices with their start and end apart: 17, of which 12 were waited for; matrix products, arithmetic and copies ran while one was open for 30% of the time, Pallas kernels for 0%

commit v1 on v0

v1 whole, which is shorter than its diff:
```python
from functools import partial

import jax
import jax.numpy as jnp
from jax import lax
from jax.experimental import pallas as pl
from jax.experimental.pallas import tpu as pltpu
from jax.sharding import PartitionSpec as P

HEADS = 16
HEAD = 64
PAIR = 2 * HEAD
EPS = 1e-06
MASKED = -1e30
VMEM_BYTES = 56 * 2**20
BF16 = jnp.bfloat16
F32 = jnp.float32
NN = (((1,), (0,)), ((), ()))
NT = (((1,), (1,)), ((), ()))
TN = (((0,), (0,)), ((), ()))


def dot(left, right, dims=NN):
    return lax.dot_general(left, right, dims, preferred_element_type=F32)


def lanes_of(shape):
    return lax.broadcasted_iota(jnp.int32, shape, len(shape) - 1)


def three_parts(column):
    high = column.astype(BF16).astype(F32)
    rest = column - high
    middle = rest.astype(BF16).astype(F32)
    return high, middle, rest - middle


def block_rows(length):
    for rows in (224, 112, 16):
        if length % rows == 0:
            return rows
    return length


def attend_kernel(q_ref, k_ref, v_ref, key_base_ref, context_ref, query_ref):
    length = q_ref.shape[0]
    rows = block_rows(length)
    low = lanes_of((length, PAIR)) < HEAD
    keys, values, key_base = k_ref[...], v_ref[...], key_base_ref[...]
    ones = jnp.ones((length, PAIR), BF16)
    keys_of = [jnp.where(low, keys, key_base), jnp.where(low, key_base, keys)]
    values_of = [jnp.where(low, values, ones), jnp.where(low, ones, values)]
    lane = lanes_of((rows, PAIR))
    low_rows = lane < HEAD
    for step in range(length // rows):
        span = slice(step * rows, (step + 1) * rows)
        queries = q_ref[span, :]
        results = []
        for head in range(2):
            base = HEAD * (1 - head)
            own = low_rows if head == 0 else jnp.logical_not(low_rows)
            unit = jnp.where(lane == base, 1.0, 0.0)
            scores = dot(jnp.where(own, queries, unit.astype(BF16)), keys_of[head], NT)
            highest = jnp.max(scores, axis=1, keepdims=True)
            weights = jnp.exp(scores - highest).astype(BF16)
            mixed = dot(weights, values_of[head])
            total = mixed[:, base : base + 1]
            high, middle, rest = three_parts(-(highest + jnp.log(total)))
            extra = jnp.where(lane == base + 3, rest, unit)
            extra = jnp.where(lane == base + 2, middle, extra)
            extra = jnp.where(lane == base + 1, high, extra)
            query_ref[head, span, :] = jnp.where(own, queries, extra.astype(BF16))
            results.append(mixed / total)
        context_ref[span, :] = jnp.where(low_rows, results[0], results[1]).astype(BF16)


def attend(mixed, key_base):
    length, width = mixed.shape
    pairs = width // (3 * PAIR)
    tile = lambda place: pl.BlockSpec((length, PAIR), place)
    scores_size = 2 * pairs * length * length
    return pl.pallas_call(
        attend_kernel,
        grid=(pairs,),
        in_specs=[
            tile(lambda i: (0, i)),
            tile(lambda i: (0, pairs + i)),
            tile(lambda i: (0, 2 * pairs + i)),
            tile(lambda i: (0, 0)),
        ],
        out_specs=[tile(lambda i: (0, i)), pl.BlockSpec((2, length, PAIR), lambda i: (i, 0, 0))],
        out_shape=[
            jax.ShapeDtypeStruct((length, pairs * PAIR), BF16),
            jax.ShapeDtypeStruct((2 * pairs, length, PAIR), BF16),
        ],
        compiler_params=pltpu.CompilerParams(vmem_limit_bytes=VMEM_BYTES),
        cost_estimate=pl.CostEstimate(
            flops=16 * scores_size * HEAD, bytes_accessed=8 * 2**20, transcendentals=scores_size
        ),
        name="attend",
    )(mixed, mixed, mixed, key_base)


def attend_back_kernel(
    query_ref, k_ref, v_ref, grad_ref, context_ref, key_base_ref, grad_q_ref, grad_k_ref, grad_v_ref
):
    length = k_ref.shape[0]
    rows = block_rows(length)
    low = lanes_of((length, PAIR)) < HEAD
    keys, values, key_base = k_ref[...], v_ref[...], key_base_ref[...]
    ones = jnp.ones((length, PAIR), BF16)
    lane = lanes_of((rows, PAIR))
    low_rows = lane < HEAD
    steps = length // rows
    grad_q, grad_k, grad_v = [], [], []
    for head in range(2):
        base = HEAD * (1 - head)
        own = low if head == 0 else jnp.logical_not(low)
        own_rows = low_rows if head == 0 else jnp.logical_not(low_rows)
        head_keys = jnp.where(own, keys, key_base)
        head_values = jnp.where(own, values, ones)
        sum_k = jnp.zeros((length, PAIR), F32)
        sum_v = jnp.zeros((length, PAIR), F32)
        for step in range(steps):
            span = slice(step * rows, (step + 1) * rows)
            queries = query_ref[head, span, :]
            grads = grad_ref[span, :]
            product = grads.astype(F32) * context_ref[span, :].astype(F32)
            inner = jnp.sum(jnp.where(own_rows, product, 0.0), axis=1, keepdims=True)
            high, middle, rest = three_parts(-inner)
            extra = jnp.where(lane == base + 2, rest, 0.0)
            extra = jnp.where(lane == base + 1, middle, extra)
            extra = jnp.where(lane == base, high, extra)
            head_grads = jnp.where(own_rows, grads, extra.astype(BF16))
            probs = jnp.exp(dot(head_keys, queries, NT))
            grad_scores = (probs * dot(head_values, head_grads, NT)).astype(BF16)
            sum_v = sum_v + dot(probs.astype(BF16), grads)
            sum_k = sum_k + dot(grad_scores, queries)
            part = dot(grad_scores, keys, TN)
            if head == 0:
                grad_q.append(part)
            else:
                both = jnp.where(low_rows, grad_q[step], part).astype(BF16)
                grad_q_ref[span, :] = both * (HEAD ** (-0.5))
        grad_k.append(sum_k)
        grad_v.append(sum_v)
    grad_k_ref[...] = jnp.where(low, grad_k[0], grad_k[1]).astype(BF16)
    grad_v_ref[...] = jnp.where(low, grad_v[0], grad_v[1]).astype(BF16)


def attend_back(queries, mixed, grad_context, context, key_base):
    length, width = mixed.shape
    pairs = width // (3 * PAIR)
    tile = lambda place: pl.BlockSpec((length, PAIR), place)
    scores_size = 2 * pairs * length * length
    return pl.pallas_call(
        attend_back_kernel,
        grid=(pairs,),
        in_specs=[
            pl.BlockSpec((2, length, PAIR), lambda i: (i, 0, 0)),
            tile(lambda i: (0, pairs + i)),
            tile(lambda i: (0, 2 * pairs + i)),
            tile(lambda i: (0, i)),
            tile(lambda i: (0, i)),
            tile(lambda i: (0, 0)),
        ],
        out_specs=[tile(lambda i: (0, i))] * 3,
        out_shape=[jax.ShapeDtypeStruct((length, pairs * PAIR), BF16)] * 3,
        compiler_params=pltpu.CompilerParams(vmem_limit_bytes=VMEM_BYTES),
        cost_estimate=pl.CostEstimate(
            flops=40 * scores_size * HEAD, bytes_accessed=12 * 2**20, transcendentals=scores_size
        ),
        name="attend_back",
    )(queries, mixed, mixed, grad_context, context, key_base)


def normalize(values):
    center = values - jnp.mean(values, axis=-1, keepdims=True)
    spread = jnp.mean(center * center, axis=-1, keepdims=True)
    scale = lax.rsqrt(spread + EPS)
    return center * scale, scale


def normalize_back(normal, scale, grad, gain):
    inner = grad * gain
    first = jnp.mean(inner, axis=-1, keepdims=True)
    second = jnp.mean(inner * normal, axis=-1, keepdims=True)
    return scale * (inner - first - normal * second)


def gelu_both(values):
    half = 0.5 * (1.0 + lax.erf(values * (0.5**0.5)))
    density = jnp.exp(-0.5 * values * values) * (0.5 / jnp.pi) ** 0.5
    return values * half, half + values * density


def column_sum(values):
    return jnp.sum(values, axis=0, dtype=F32)


def swap_core(values):
    return lax.ppermute(values, "seq", [(0, 1), (1, 0), (2, 3), (3, 2)])


def swap_chip(values):
    return lax.ppermute(values, "seq", [(0, 2), (2, 0), (1, 3), (3, 1)])


def with_partner(values):
    return jnp.concatenate([values, swap_core(values)], axis=0)


def sum_partner(partial_sums):
    half = partial_sums.shape[0] // 2
    received = swap_core(partial_sums[half:].astype(BF16))
    return partial_sums[:half] + received.astype(F32)


def gather_rows(values):
    return lax.all_gather(values, "fsdp", axis=0, tiled=True)


def scatter_rows(values):
    return lax.psum_scatter(values.astype(BF16), "fsdp", scatter_dimension=0, tiled=True)


def in_core_order(own, other, core, axis):
    first = jnp.where(core == 0, own, other)
    second = jnp.where(core == 0, other, own)
    return first, second


def body(
    inputs,
    cotangent,
    valid,
    ln1_gain,
    ln1_bias,
    qkv_weight,
    q_bias,
    v_bias,
    out_weight,
    out_bias,
    ln2_gain,
    ln2_bias,
    fc1_weight,
    fc1_bias,
    fc2_weight,
    fc2_bias,
):
    clips, rows, width = inputs.shape
    groups = lax.axis_size("fsdp")
    place = lax.axis_index("seq")
    group = lax.axis_index("fsdp")
    chip, core = place // 2, place % 2
    half = width // 2
    hidden_rows = fc2_weight.shape[0]
    half_rows = hidden_rows // 2
    own_rows = clips * rows
    scale_factor = HEAD ** (-0.5)

    def take(values, index):
        return lax.dynamic_index_in_dim(values, index, 0, keepdims=False)

    def own_clip(values):
        mine = take(values, chip)
        return jnp.concatenate([mine, swap_chip(take(values, 1 - chip))], axis=0)

    def all_clips(values):
        mine, back = values[:rows], swap_chip(values[rows:])
        first = jnp.where(chip == 0, mine, back)
        second = jnp.where(chip == 0, back, mine)
        return jnp.stack([first, second])

    vectors = (ln1_gain, ln1_bias, q_bias, v_bias, out_bias, ln2_gain, ln2_bias, fc2_bias, fc1_bias)
    packed = lax.all_gather(jnp.concatenate(vectors), "fsdp", axis=0)
    own_width = width // groups
    wide = [
        packed[:, i * own_width : (i + 1) * own_width].reshape(width).astype(F32) for i in range(8)
    ]
    gain_one, bias_one, bias_q, bias_v, bias_out, gain_two, bias_two, bias_fc2 = wide
    bias_fc1 = take(
        jnp.moveaxis(packed[:, 8 * own_width :].reshape(groups, 2, half_rows), 1, 0), core
    )
    bias_fc1 = bias_fc1.reshape(groups * half_rows).astype(F32)
    bias_q, bias_v = take(bias_q.reshape(2, half), core), take(bias_v.reshape(2, half), core)

    own_qkv = lax.dynamic_index_in_dim(
        qkv_weight.reshape(own_width, 3, 2, half), core, 2, keepdims=False
    ).reshape(own_width, 3 * half)
    full_qkv = gather_rows(own_qkv)
    full_out = lax.dynamic_slice_in_dim(gather_rows(out_weight), core * half, half, 0)
    own_fc1 = lax.dynamic_index_in_dim(
        fc1_weight.reshape(own_width, groups, 2, half_rows), core, 2, keepdims=False
    ).reshape(own_width, groups * half_rows)
    full_fc1 = gather_rows(own_fc1)
    full_fc2 = gather_rows(lax.dynamic_slice_in_dim(fc2_weight, core * half_rows, half_rows, 0))

    own_inputs = own_clip(inputs)
    own_grads = own_clip(cotangent)
    all_inputs = with_partner(own_inputs)
    all_grads = with_partner(own_grads)
    clip_valid = take(valid, chip).reshape(2 * clips, rows)
    own_valid = jnp.concatenate([take(clip_valid, place), take(clip_valid, place ^ 2)])
    other_valid = jnp.concatenate([take(clip_valid, place ^ 1), take(clip_valid, place ^ 3)])
    key_valid = jnp.concatenate([own_valid, other_valid])
    lane = jnp.arange(PAIR) % HEAD
    key_mask = jnp.where(key_valid > 0, 0.0, MASKED)[:, None]
    key_base = jnp.where(lane == 0, key_mask, jnp.where(lane < 4, 1.0, 0.0)).astype(BF16)

    normal_one = normalize(all_inputs.astype(F32))[0]
    h_one = (normal_one * gain_one + bias_one).astype(BF16)
    product = dot(h_one, full_qkv)
    mixed = jnp.concatenate(
        [
            ((product[:, :half] + bias_q) * scale_factor).astype(BF16),
            product[:, half : 2 * half].astype(BF16),
            (product[:, 2 * half :] + bias_v).astype(BF16),
        ],
        axis=1,
    )
    context, queries = attend(mixed, key_base)
    attn_branch = sum_partner(dot(context, full_out)) + bias_out
    residual_mid = own_inputs.astype(F32) + attn_branch
    normal_two, scale_two = normalize(residual_mid)
    h_two = with_partner((normal_two * gain_two + bias_two).astype(BF16))
    active, slope = gelu_both(dot(h_two, full_fc1) + bias_fc1)
    active, slope = active.astype(BF16), slope.astype(BF16)
    mlp_branch = sum_partner(dot(active, full_fc2)) + bias_fc2
    residual_out = residual_mid + mlp_branch
    output = all_clips(residual_out.astype(BF16))
    counted = own_valid.astype(F32)[:, None]
    squares = jnp.stack(
        [
            jnp.sum(counted * residual_out * residual_out),
            jnp.sum(counted * attn_branch * attn_branch),
            jnp.sum(counted * mlp_branch * mlp_branch),
            jnp.sum(counted),
        ]
    )

    grad_fc2 = scatter_rows(dot(active, all_grads, TN))
    grad_hidden = (dot(all_grads, full_fc2, NT) * slope.astype(F32)).astype(BF16)
    grad_fc1 = scatter_rows(dot(h_two, grad_hidden, TN))
    grad_h_two = sum_partner(dot(grad_hidden, full_fc1, NT))
    grad_residual = own_grads.astype(F32) + normalize_back(
        normal_two, scale_two, grad_h_two, gain_two
    )
    own_grad_attn = grad_residual.astype(BF16)
    grad_attn = with_partner(own_grad_attn)
    grad_out = dot(context, grad_attn, TN).astype(BF16)
    kept = lax.dynamic_slice_in_dim(grad_out, core * half, half, 1)
    received = swap_core(lax.dynamic_slice_in_dim(grad_out, (1 - core) * half, half, 1))
    grad_out = scatter_rows(jnp.concatenate(in_core_order(kept, received, core, 0), axis=0))
    grad_context = dot(grad_attn, full_out, NT).astype(BF16)
    grad_q, grad_k, grad_v = attend_back(queries, mixed, grad_context, context, key_base)
    grad_mixed = jnp.concatenate([grad_q, grad_k, grad_v], axis=1)
    grad_qkv = scatter_rows(dot(h_one, grad_mixed, TN))
    grad_h_one = sum_partner(dot(grad_mixed, full_qkv, NT))
    own_normal, own_scale = normalize(own_inputs.astype(F32))
    input_grad = all_clips(
        (grad_residual + normalize_back(own_normal, own_scale, grad_h_one, gain_one)).astype(BF16)
    )

    def by_core(values):
        full = jnp.zeros((2, values.shape[0]), F32)
        return lax.dynamic_update_index_in_dim(full, values, core, 0).reshape(-1)

    mixed_sums = column_sum(grad_mixed)
    vector_grads = [
        column_sum(grad_h_one * own_normal),
        column_sum(grad_h_one),
        by_core(mixed_sums[:half]),
        by_core(mixed_sums[2 * half :]),
        column_sum(own_grad_attn),
        column_sum(grad_h_two * normal_two),
        column_sum(grad_h_two),
        column_sum(own_grads),
    ]
    hidden_sums = jnp.zeros((groups, 2, half_rows), F32)
    hidden_sums = lax.dynamic_update_index_in_dim(
        hidden_sums, column_sum(grad_hidden).reshape(groups, half_rows), core, 1
    )
    flat = jnp.concatenate(vector_grads + [hidden_sums.reshape(-1), squares])
    flat = lax.psum(flat, ("seq", "fsdp"))
    totals = flat[-4:]
    branch_rms = jnp.sqrt(totals[:3] / (totals[3] * width))
    own_vectors = [
        lax.dynamic_slice_in_dim(flat, i * width + group * own_width, own_width) for i in range(8)
    ]
    own_hidden = lax.dynamic_slice_in_dim(flat, 8 * width + group * hidden_rows, hidden_rows)

    def finish(values):
        values = (values.astype(F32) + swap_chip(values).astype(F32)).astype(BF16)
        return in_core_order(values, swap_core(values), core, 0)

    qkv_parts = [part.reshape(own_width, 3, 1, half) for part in finish(grad_qkv)]
    qkv_grad = jnp.concatenate(qkv_parts, axis=2).reshape(own_width, 3 * width).astype(F32)
    out_grad = jnp.concatenate(finish(grad_out), axis=1).astype(F32)
    fc1_parts = [part.reshape(own_width, groups, 1, half_rows) for part in finish(grad_fc1)]
    fc1_grad = jnp.concatenate(fc1_parts, axis=2).reshape(own_width, -1).astype(F32)
    fc2_grad = jnp.concatenate(finish(grad_fc2), axis=0).astype(F32)
    return (
        output,
        input_grad,
        own_vectors[0],
        own_vectors[1],
        qkv_grad,
        own_vectors[2],
        own_vectors[3],
        out_grad,
        own_vectors[4],
        own_vectors[5],
        own_vectors[6],
        fc1_grad,
        own_hidden,
        fc2_grad,
        own_vectors[7],
        branch_rms,
    )


def solution(mesh):
    tokens, rows, vector = P("fsdp", "seq", None), P("fsdp", None), P("fsdp")
    return jax.shard_map(
        body,
        mesh=mesh,
        in_specs=(
            tokens,
            tokens,
            rows,
            vector,
            vector,
            rows,
            vector,
            vector,
            rows,
            vector,
            vector,
            vector,
            rows,
            vector,
            rows,
            vector,
        ),
        out_specs=(
            tokens,
            tokens,
            vector,
            vector,
            rows,
            vector,
            vector,
            rows,
            vector,
            vector,
            vector,
            rows,
            vector,
            rows,
            vector,
            P(),
        ),
        check_vma=False,
    )
```

time: 1750 us -> 670 us (0.38)
  waiting for transfers between devices: 820 us -> 253 us
  matrix products: 365 us -> 109 us
  blocking collectives: 255 us -> 78.5 us
  Pallas kernels: 0 us -> 104 us
  local copies, waits for them, and re-layouts: 121 us -> 37 us
  other arithmetic: 130 us -> 48.5 us
    reduce_scatter x4, waiting for transfers between devices: 677 us -> 57.6 us  [scatter_rows(): lax.psum_scatter(values.astype(BF16), 'fsdp', scatter_dimension=0, tiled=...]
    dot_general x40 -> x12, matrix products: 365 us -> 109 us  [dot(): return lax.dot_general(left, right, dims, preferred_element_type=F32)]
    all_gather x9 -> x1, blocking collectives: 170 us -> 31.5 us  [body(): packed = lax.all_gather(jnp.concatenate(vectors), 'fsdp', axis=0)]
    all_to_all x8 -> x0, waiting for transfers between devices: 107 us -> none  [the longest x1 19.5 us: body(): lax.all_to_all(queries.reshape(shaped), 'seq', split_axis=2, concat_axis=...]
    pallas_call x0 -> x2, Pallas kernels: none -> 104 us  [the longest x1 64.2 us: attend_back(): pl.pallas_call(attend_back_kernel, grid=(pairs,), in_specs=[pl.BlockSpec(...]
    ppermute x0 -> x21, waiting for transfers between devices: none -> 94.6 us  [the longest x8 83 us: swap_chip(): return lax.ppermute(values, 'seq', [(0, 2), (2, 0), (1, 3), (3, 1)])]
    convert_element_type x34 -> x14, other arithmetic: 88.6 us -> 9.78 us  [the longest x1 1.96 us: body(): (grad_residual + normalize_back(own_normal, own_scale, grad_h_one, gain_o...]
    all_gather x4, waiting for transfers between devices: 25.8 us -> 100 us  [gather_rows(): return lax.all_gather(values, 'fsdp', axis=0, tiled=True)]
  transfers between devices with their start and end apart: 17 -> 29, of which waited for: 12 -> 16; matrix products, arithmetic and copies ran while one was open for 30% -> 23% of each run, Pallas kernels for 0% -> 16%
where the time goes in v1:
time: 670 us; the launch traced here: 661 us
  waiting for transfers between devices  253 us (38%)
  matrix products  109 us (16%)
  Pallas kernels  104 us (16%)
  blocking collectives  78.5 us (12%)
  other arithmetic  48.5 us (7%)
  local copies, waits for them, and re-layouts  37 us (6%)
  between operations  16.1 us (2%)
  starting transfers between devices  14.7 us (2%)
    dot_general x12, matrix products, dot(): return lax.dot_general(left, right, dims, preferred_element_type=F32)  109 us
    all_gather x4, waiting for transfers between devices, gather_rows(): return lax.all_gather(values, 'fsdp', axis=0, tiled=True)  100 us
    ppermute x8, waiting for transfers between devices, swap_chip(): return lax.ppermute(values, 'seq', [(0, 2), (2, 0), (1, 3), (3, 1)])  83 us
    pallas_call x1, Pallas kernels, attend_back(): pl.pallas_call(attend_back_kernel, grid=(pairs,), in_specs=[pl.BlockSpec(...  64.2 us
    reduce_scatter x4, waiting for transfers between devices, scatter_rows(): lax.psum_scatter(values.astype(BF16), 'fsdp', scatter_dimension=0, tiled=...  57.6 us
    psum x1, blocking collectives, body(): flat = lax.psum(flat, ('seq', 'fsdp'))  47 us
    pallas_call x1, Pallas kernels, attend(): pl.pallas_call(attend_kernel, grid=(pairs,), in_specs=[tile(lambda i: (0,...  40.1 us
    all_gather x1, blocking collectives, body(): packed = lax.all_gather(jnp.concatenate(vectors), 'fsdp', axis=0)  31.5 us
  transfers between devices with their start and end apart: 29, of which 16 were waited for; matrix products, arithmetic and copies ran while one was open for 23% of the time, Pallas kernels for 16%

profile of v1, /device:TPU:0, one launch (start us, length us, event | category | flops | bytes accessed | tf_op | source)
XLA Modules:
  0.0 661.4 jit_solution(3655402561101353292)
XLA Ops:
  16.8 17.9 %collective-permute-done = bf16[392,1024]{1,0:T(8,128)(2,1)S(1)} collective-permute-done((bf16[392,1024]{1,0:T(8,128)(2,1)S(1)}, bf16[392,1024]{1,0:T(8,128)(2,1)S(1)}, u32[]{:S(2)}, u32[]{:S(2)}) %collective-permute-start) | collective-permute-done | bytes 802848 | tf_op jit(solution)/shard_map/ppermute | solution.py:206
  38.8 31.5 %all-gather.1 = bf16[8,1,1536]{2,1,0:T(2,128)(2,1)S(1)} all-gather(bf16[1,1,1536]{2,1,0:T(2,128)(2,1)S(1)} %reshape.299), channel_id=2, replica_groups=mesh['seq'=4,'fsdp'=8] {'fsdp'}, dimensions={0}, use_global_device_ids=true | all-gather | bytes 27648 | tf_op jit(solution)/shard_map/all_gather | solution.py:276
  77.2 7.8 %fusion.58 = f32[1568,1536]{1,0:T(8,128)S(1)} fusion(bf16[1024,1536]{0,1:T(8,128)(2,1)} %all-gather.7.cloned.1.call-done, f32[1024]{0:T(1024)S(1)} %get-tuple-element.115, f32[1024]{0:T(1024)S(1)} %get-tuple-element.116, f32[1568]{0:T(1024)S(1)} %add_rsqrt_fusion, f32[1568]{0:T(1024)S(1)} %broadcast_multiply_fusion, ...), kind=kOutput, calls=%fused_computation.176 | convolution fusion | flops 4950163456 | bytes 16011520 | tf_op jit(solution)/shard_map/dot_general | solution.py:24
  88.6 40.1 %attend.1 = (bf16[1568,512]{1,0:T(8,128)(2,1)}, bf16[8,1568,128]{2,1,0:T(8,128)(2,1)}) custom-call(bf16[1568,1536]{1,0:T(8,128)(2,1)} %pad_maximum_fusion.q_ref.k_ref.v_ref, bf16[1568,1536]{1,0:T(8,128)(2,1)} %pad_maximum_fusion.q_ref.k_ref.v_ref, bf16[1568,1536]{1,0:T(8,128)(2,1)} %pad_maximum_fusion.q_ref.k_ref.v_ref, ...), custom_call_target="tpu_custom_call" | custom-call | flops 20141047808 | bytes 8388608 | tf_op jit(solution)/shard_map/attend/pallas_call | solution.py:82
  128.8 3.6 fusion.36
  133.1 3.1 collective-permute-done.2
  136.2 3.9 fusion.60
  144.2 18.6 %collective-permute-done.6 = bf16[392,1024]{1,0:T(8,128)(2,1)S(1)} collective-permute-done((bf16[392,1024]{1,0:T(8,128)(2,1)S(1)}, bf16[392,1024]{1,0:T(8,128)(2,1)S(1)}, u32[]{:S(2)}, u32[]{:S(2)}) %collective-permute-start.6) | collective-permute-done | bytes 802848 | tf_op jit(solution)/shard_map/ppermute | solution.py:206
  164.3 38.8 %all-gather.11.cloned.1.call-done = bf16[1024,2048]{0,1:T(8,128)(2,1)} async-done(((bf16[128,2048]{0,1:T(8,128)(2,1)}), bf16[1024,2048]{0,1:T(8,128)(2,1)}) %all-gather.11.cloned.1.call-update) | async-done | bytes 4194320 | tf_op jit(solution)/shard_map/all_gather | solution.py:220
  203.1 13.9 %multiply_convert_fusion.1 = (bf16[1568,2048]{1,0:T(8,128)(2,1)}, f32[1568,2048]{1,0:T(8,128)}) fusion(f32[2048]{0:T(1024)S(1)} %bitcast.136, bf16[1024,2048]{0,1:T(8,128)(2,1)} %all-gather.11.cloned.1.call-done, bf16[784,1024]{1,0:T(8,128)(2,1)} %collective-permute-done.3, bf16[784,1024]{1,0:T(8,128)(2,1)} %add_convert_fusion), kind=kOutput, calls=%fused_computation.8 | convolution fusion | flops 6602358784 | bytes 26681344 | tf_op jit(solution)/shard_map/dot_general | solution.py:24
  217.1 60.2 %all-gather.13.cloned.1.call-done = bf16[2048,1024]{1,0:T(8,128)(2,1)} async-done(((bf16[256,1024]{1,0:T(8,128)(2,1)}), bf16[2048,1024]{1,0:T(8,128)(2,1)}) %all-gather.13.cloned.1.call-update) | async-done | bytes 4194320 | tf_op jit(solution)/shard_map/all_gather | solution.py:220
  277.3 15.4 %convert_reduce_fusion = (f32[2048]{0:T(1024)S(1)}, bf16[1568,2048]{1,0:T(8,128)(2,1)S(1)}) fusion(f32[1568,2048]{1,0:T(8,128)} %get-tuple-element.124, f32[2048]{0:T(1024)S(1)} %bitcast.137, bf16[2048,1024]{1,0:T(8,128)(2,1)} %all-gather.13.cloned.1.call-done, bf16[784,1024]{1,0:T(8,128)(2,1)} %collective-permute-done.7, bf16[392,1024]{1,0:T(8,128)(2,1)} %copy-done.18, ...), kind=kOutput, calls=%fused_computation.6 | convolution fusion | flops 6634469376 | bytes 26689536 | tf_op jit(solution)/shard_map/dot_general | solution.py:24
  292.7 8.8 %fusion.64 = f32[1568,1024]{1,0:T(8,128)} fusion(bf16[1568,2048]{1,0:T(8,128)(2,1)S(1)} %get-tuple-element.126, bf16[1024,2048]{0,1:T(8,128)(2,1)S(1)} %copy-done.50), kind=kOutput, calls=%fused_computation.181 | convolution fusion | flops 6576668672 | bytes 17039360 | tf_op jit(solution)/shard_map/dot_general | solution.py:24
  301.6 3.3 slice.229
  304.9 10.7 %convolution_convert_fusion.1 = bf16[1024,2048]{1,0:T(8,128)(2,1)} fusion(bf16[1568,2048]{1,0:T(8,128)(2,1)S(1)} %get-tuple-element.126, bf16[784,1024]{1,0:T(8,128)(2,1)} %collective-permute-done.3, bf16[784,1024]{1,0:T(8,128)(2,1)} %add_convert_fusion), kind=kOutput, calls=%fused_computation.34 | convolution fusion | flops 6585188352 | bytes 13828096 | tf_op jit(solution)/shard_map/dot_general | solution.py:24
  315.7 10.2 %fusion.63 = f32[1568,1024]{1,0:T(8,128)S(1)} fusion(bf16[1568,2048]{1,0:T(8,128)(2,1)} %get-tuple-element.123, bf16[2048,1024]{1,0:T(8,128)(2,1)} %all-gather.13.cloned.1.call-done), kind=kOutput, calls=%fused_computation.180 | convolution fusion | flops 6576668672 | bytes 17039360 | tf_op jit(solution)/shard_map/dot_general | solution.py:24
  326.8 3.0 collective-permute-done.4
  329.8 7.5 %fusion.25 = (f32[]{:T(128)}, f32[]{:T(128)}, f32[1024]{0:T(1024)S(1)}, f32[784]{0:T(1024)S(1)}, f32[784]{0:T(1024)S(1)}, /*index=5*/f32[1024]{0:T(1024)S(1)}, f32[]{:T(128)}, bf16[784,1024]{1,0:T(8,128)(2,1)}) fusion(bf16[784,1024]{1,0:T(8,128)(2,1)S(1)} %collective-permute-done.4, f32[1568,1024]{1,0:T(8,128)S(1)} %fusion.63, ...), kind=kLoop, calls=%fused_computation.45 | loop fusion | flops 22475228 | bytes 19303756 | tf_op jit(solution)/shard_map/reduce_sum | solution.py:337
  337.3 5.4 convert_reduce_fusion.5
  343.1 3.3 collective-permute-done.9
  347.5 4.0 fusion.34
  356.1 12.7 %convolution_convert_fusion = bf16[2048,1024]{1,0:T(8,128)(2,1)} fusion(bf16[1568,2048]{1,0:T(8,128)(2,1)} %get-tuple-element.123, bf16[784,1024]{1,0:T(8,128)(2,1)} %collective-permute-done.7, bf16[392,1024]{1,0:T(8,128)(2,1)S(1)} %copy-done.20, bf16[392,1024]{1,0:T(8,128)(2,1)S(1)} %copy-done.13), kind=kOutput, calls=%fused_computation.33 | convolution fusion | flops 6588399616 | bytes 13828096 | tf_op jit(solution)/shard_map/dot_general | solution.py:24
  370.4 5.0 convolution_convert_fusion.3.grad_ref
  375.4 64.2 %attend_back.1 = (bf16[1568,512]{1,0:T(8,128)(2,1)}, bf16[1568,512]{1,0:T(8,128)(2,1)}, bf16[1568,512]{1,0:T(8,128)(2,1)}) custom-call(bf16[8,1568,128]{2,1,0:T(8,128)(2,1)} %get-tuple-element.22.query_ref, bf16[1568,1536]{1,0:T(8,128)(2,1)} %pad_maximum_fusion.q_ref.k_ref.v_ref, bf16[1568,1536]{1,0:T(8,128)(2,1)} %pad_maximum_fusion.q_ref.k_ref.v_ref, ...), custom_call_target="tpu_custom_call" | custom-call | flops 50352619520 | bytes 12582912 | tf_op jit(solution)/shard_map/attend_back/pallas_call | solution.py:156
  444.4 8.9 %convolution_convert_fusion.2 = bf16[1024,1536]{1,0:T(8,128)(2,1)} fusion(bf16[1568,1536]{1,0:T(8,128)(2,1)S(1)} %constant_dynamic-update-slice_fusion.1, f32[1024]{0:T(1024)S(1)} %copy-done.39, f32[1024]{0:T(1024)S(1)} %copy-done.32, f32[1568]{0:T(1024)S(1)} %copy-done.37, f32[1568]{0:T(1024)S(1)} %copy-done.34, ...), kind=kOutput, calls=%fused_computation.35 | convolution fusion | flops 4951736320 | bytes 11194624 | tf_op jit(solution)/shard_map/dot_general | solution.py:24
  453.3 7.9 %fusion.65 = f32[1568,1024]{1,0:T(8,128)S(1)} fusion(bf16[1568,1536]{1,0:T(8,128)(2,1)} %copy-done.10, bf16[1024,1536]{0,1:T(8,128)(2,1)} %all-gather.7.cloned.1.call-done), kind=kOutput, calls=%fused_computation.182 | convolution fusion | flops 4932501504 | bytes 14385152 | tf_op jit(solution)/shard_map/dot_general | solution.py:24
  469.2 18.2 %collective-permute-done.5 = bf16[392,1024]{1,0:T(8,128)(2,1)} collective-permute-done((bf16[392,1024]{1,0:T(8,128)(2,1)}, bf16[392,1024]{1,0:T(8,128)(2,1)}, u32[]{:S(2)}, u32[]{:S(2)}) %collective-permute-start.5) | collective-permute-done | bytes 802848 | tf_op jit(solution)/shard_map/ppermute | solution.py:206
  499.3 47.0 %psum.7 = f32[12292]{0:T(1024)S(1)} all-reduce(f32[12292]{0:T(1024)S(1)} %concatenate.98), channel_id=1, replica_groups=mesh['seq'=4,'fsdp'=8] {'seq','fsdp'}, use_global_device_ids=true, to_apply=%region_22.23 | all-reduce | flops 12292 | bytes 98336 | tf_op jit(solution)/shard_map/psum | solution.py:385
  554.3 11.7 %collective-permute-done.15 = bf16[128,512]{1,0:T(8,128)(2,1)S(1)} collective-permute-done((bf16[128,512]{1,0:T(8,128)(2,1)}, bf16[128,512]{1,0:T(8,128)(2,1)S(1)}, u32[]{:S(2)}, u32[]{:S(2)}) %collective-permute-start.15) | collective-permute-done | bytes 131104 | tf_op jit(solution)/shard_map/ppermute | solution.py:206
  568.4 12.4 %collective-permute-done.19 = bf16[256,1024]{1,0:T(8,128)(2,1)S(1)} collective-permute-done((bf16[256,1024]{1,0:T(8,128)(2,1)}, bf16[256,1024]{1,0:T(8,128)(2,1)S(1)}, u32[]{:S(2)}, u32[]{:S(2)}) %collective-permute-start.19) | collective-permute-done | bytes 524320 | tf_op jit(solution)/shard_map/ppermute | solution.py:206
  581.1 57.6 %reduce-scatter.5.cloned.1.call-done = bf16[128,1536]{1,0:T(8,128)(2,1)} async-done(((bf16[1024,1536]{1,0:T(8,128)(2,1)}), bf16[128,1536]{1,0:T(8,128)(2,1)}) %reduce-scatter.5.cloned.1.call-update) | async-done | bytes 393232 | tf_op jit(solution)/shard_map/reduce_scatter | solution.py:224
  644.9 4.2 collective-permute-done.12
  (274 shorter events, 84.3 us)
Async XLA Ops:
  7.2 70.0 %all-gather.7.cloned.1.call-start = ((), (), s32[]{:S(2)}) async-start(), calls=%async_computation.4 | async-start | bytes 3538944 | tf_op jit(solution)/shard_map/all_gather | solution.py:220
  9.7 119.0 %all-gather.9.cloned.1.call-start = ((), (), s32[]{:S(2)}) async-start(), calls=%async_computation.5 | async-start | bytes 2359296 | tf_op jit(solution)/shard_map/all_gather | solution.py:220
  10.5 192.6 %all-gather.11.cloned.1.call-start = ((), (), s32[]{:S(2)}) async-start(), calls=%async_computation.6 | async-start | bytes 4718592 | tf_op jit(solution)/shard_map/all_gather | solution.py:220
  12.1 265.2 %all-gather.13.cloned.1.call-start = ((), (), s32[]{:S(2)}) async-start(), calls=%async_computation.7 | async-start | bytes 4718592 | tf_op jit(solution)/shard_map/all_gather | solution.py:220
  13.7 119.1 %copy-start.2 = (bf16[392,1024]{1,0:T(8,128)(2,1)}, bf16[392,1024]{1,0:T(8,128)(2,1)S(1)}, u32[]{:S(2)}) copy-start(bf16[392,1024]{1,0:T(8,128)(2,1)S(1)} %get-tuple-element.89) | copy-start | bytes 2408452
  13.8 56.6 %copy-start.40 = (s32[2,1568]{1,0:T(2,128)S(1)}, s32[2,1568]{1,0:T(2,128)}, u32[]{:S(2)}) copy-start(s32[2,1568]{1,0:T(2,128)} %param.18) | copy-start | bytes 37636
  13.8 20.9 %collective-permute-start = (bf16[392,1024]{1,0:T(8,128)(2,1)S(1)}, bf16[392,1024]{1,0:T(8,128)(2,1)S(1)}, u32[]{:S(2)}, u32[]{:S(2)}) collective-permute-start(bf16[392,1024]{1,0:T(8,128)(2,1)S(1)} %get-tuple-element.90), channel_id=1, source_target_pairs={{0,16},{16,0},{8,24},{24,8},{1,17},{17,1},{9,25},{25,9},{2,18},{18... | collective-permute-start | bytes 2408456 | tf_op jit(solution)/shard_map/ppermute | solution.py:206
  34.7 98.1 %copy-start.4 = (bf16[392,1024]{1,0:T(8,128)(2,1)}, bf16[392,1024]{1,0:T(8,128)(2,1)S(1)}, u32[]{:S(2)}) copy-start(bf16[392,1024]{1,0:T(8,128)(2,1)S(1)} %collective-permute-done) | copy-start | bytes 2408452
  36.1 35.6 %collective-permute-start.1 = (bf16[784,1024]{1,0:T(8,128)(2,1)}, bf16[784,1024]{1,0:T(8,128)(2,1)}, u32[]{:S(2)}, u32[]{:S(2)}) collective-permute-start(bf16[784,1024]{1,0:T(8,128)(2,1)} %pad_maximum_fusion.9), channel_id=1, source_target_pairs={{0,8},{8,0},{16,24},{24,16},{1,9},{9,1},{17,25},{25,17},{2,10},{10... | collective-permute-start | bytes 4816904 | tf_op jit(solution)/shard_map/ppermute | solution.py:202
  36.9 512.5 %reduce-scatter.9.cloned.1.call-start = ((), (), s32[]{:S(2)}) async-start(), calls=%async_computation.10 | async-start | bytes 4718592 | tf_op jit(solution)/shard_map/reduce_scatter | solution.py:224
  132.6 3.5 collective-permute-start.2
  142.3 60.8 %collective-permute-start.3 = (bf16[784,1024]{1,0:T(8,128)(2,1)}, bf16[784,1024]{1,0:T(8,128)(2,1)}, u32[]{:S(2)}, u32[]{:S(2)}) collective-permute-start(bf16[784,1024]{1,0:T(8,128)(2,1)} %add_convert_fusion), channel_id=1, source_target_pairs={{0,8},{8,0},{16,24},{24,16},{1,9},{9,1},{17,25},{25,17},{2,10},{10... | collective-permute-start | bytes 4816904 | tf_op jit(solution)/shard_map/ppermute | solution.py:202
  142.6 20.2 %collective-permute-start.6 = (bf16[392,1024]{1,0:T(8,128)(2,1)S(1)}, bf16[392,1024]{1,0:T(8,128)(2,1)S(1)}, u32[]{:S(2)}, u32[]{:S(2)}) collective-permute-start(bf16[392,1024]{1,0:T(8,128)(2,1)S(1)} %get-tuple-element.88), channel_id=1, source_target_pairs={{0,16},{16,0},{8,24},{24,8},{1,17},{17,1},{9,25},{25,9},{2,18},{18... | collective-permute-start | bytes 2408456 | tf_op jit(solution)/shard_map/ppermute | solution.py:206
  164.3 52.8 %collective-permute-start.7 = (bf16[784,1024]{1,0:T(8,128)(2,1)}, bf16[784,1024]{1,0:T(8,128)(2,1)}, u32[]{:S(2)}, u32[]{:S(2)}) collective-permute-start(bf16[784,1024]{1,0:T(8,128)(2,1)} %pad_maximum_fusion.11), channel_id=1, source_target_pairs={{0,8},{8,0},{16,24},{24,16},{1,9},{9,1},{17,25},{25,17},{2,10},{10... | collective-permute-start | bytes 4816904 | tf_op jit(solution)/shard_map/ppermute | solution.py:202
  304.9 21.9 %collective-permute-start.8 = (bf16[784,1024]{1,0:T(8,128)(2,1)}, bf16[784,1024]{1,0:T(8,128)(2,1)}, u32[]{:S(2)}, u32[]{:S(2)}) collective-permute-start(bf16[784,1024]{1,0:T(8,128)(2,1)} %slice.229), channel_id=1, source_target_pairs={{0,8},{8,0},{16,24},{24,16},{1,9},{9,1},{17,25},{25,17},{2,10},{10... | collective-permute-start | bytes 4816904 | tf_op jit(solution)/shard_map/ppermute | solution.py:202
  315.7 237.2 %reduce-scatter.7.cloned.1.call-start = ((), (), s32[]{:S(2)}) async-start(), calls=%async_computation.9 | async-start | bytes 1179648 | tf_op jit(solution)/shard_map/reduce_scatter | solution.py:224
  326.1 3.7 collective-permute-start.4
  342.7 3.7 collective-permute-start.9
  351.6 2.1 collective-permute-start.14
  356.0 210.2 %reduce-scatter.11.cloned.1.call-start = ((), (), s32[]{:S(2)}) async-start(), calls=%async_computation.11 | async-start | bytes 4718592 | tf_op jit(solution)/shard_map/reduce_scatter | solution.py:224
  368.9 269.7 %reduce-scatter.5.cloned.1.call-start = ((), (), s32[]{:S(2)}) async-start(), calls=%async_computation.8 | async-start | bytes 3538944 | tf_op jit(solution)/shard_map/reduce_scatter | solution.py:224
  465.4 24.8 %collective-permute-start.10 = (bf16[784,1024]{1,0:T(8,128)(2,1)}, bf16[784,1024]{1,0:T(8,128)(2,1)S(1)}, u32[]{:S(2)}, u32[]{:S(2)}) collective-permute-start(bf16[784,1024]{1,0:T(8,128)(2,1)} %slice.228), channel_id=1, source_target_pairs={{0,8},{8,0},{16,24},{24,16},{1,9},{9,1},{17,25},{25,17},{2,10},{10... | collective-permute-start | bytes 4816904 | tf_op jit(solution)/shard_map/ppermute | solution.py:202
  466.9 20.5 %collective-permute-start.5 = (bf16[392,1024]{1,0:T(8,128)(2,1)}, bf16[392,1024]{1,0:T(8,128)(2,1)}, u32[]{:S(2)}, u32[]{:S(2)}) collective-permute-start(bf16[392,1024]{1,0:T(8,128)(2,1)} %slice.137), channel_id=1, source_target_pairs={{0,16},{16,0},{8,24},{24,8},{1,17},{17,1},{9,25},{25,9},{2,18},{18... | collective-permute-start | bytes 2408456 | tf_op jit(solution)/shard_map/ppermute | solution.py:206
  494.2 57.4 %collective-permute-start.11 = (bf16[392,1024]{1,0:T(8,128)(2,1)S(1)}, bf16[392,1024]{1,0:T(8,128)(2,1)S(1)}, u32[]{:S(2)}, u32[]{:S(2)}) collective-permute-start(bf16[392,1024]{1,0:T(8,128)(2,1)S(1)} %slice.143), channel_id=1, source_target_pairs={{0,16},{16,0},{8,24},{24,8},{1,17},{17,1},{9,25},{25,9},{2,18},{18... | collective-permute-start | bytes 2408456 | tf_op jit(solution)/shard_map/ppermute | solution.py:206
  549.4 17.4 %collective-permute-start.17 = (bf16[128,2048]{1,0:T(8,128)(2,1)}, bf16[128,2048]{1,0:T(8,128)(2,1)S(1)}, u32[]{:S(2)}, u32[]{:S(2)}) collective-permute-start(bf16[128,2048]{1,0:T(8,128)(2,1)} %reduce-scatter.9.cloned.1.call-done), channel_id=1, source_target_pairs={{0,16},{16,0},{8,24},{24,8},{1,17},{17,1},{9,25},{25,9},{2,18},{18... | collective-permute-start | bytes 1572872 | tf_op jit(solution)/shard_map/ppermute | solution.py:206
  552.9 13.2 %collective-permute-start.15 = (bf16[128,512]{1,0:T(8,128)(2,1)}, bf16[128,512]{1,0:T(8,128)(2,1)S(1)}, u32[]{:S(2)}, u32[]{:S(2)}) collective-permute-start(bf16[128,512]{1,0:T(8,128)(2,1)} %reduce-scatter.7.cloned.1.call-done), channel_id=1, source_target_pairs={{0,16},{16,0},{8,24},{24,8},{1,17},{17,1},{9,25},{25,9},{2,18},{18... | collective-permute-start | bytes 393224 | tf_op jit(solution)/shard_map/ppermute | solution.py:206
  566.1 1.4 collective-permute-start.16
  566.2 14.5 %collective-permute-start.19 = (bf16[256,1024]{1,0:T(8,128)(2,1)}, bf16[256,1024]{1,0:T(8,128)(2,1)S(1)}, u32[]{:S(2)}, u32[]{:S(2)}) collective-permute-start(bf16[256,1024]{1,0:T(8,128)(2,1)} %reduce-scatter.11.cloned.1.call-done), channel_id=1, source_target_pairs={{0,16},{16,0},{8,24},{24,8},{1,17},{17,1},{9,25},{25,9},{2,18},{18... | collective-permute-start | bytes 1572872 | tf_op jit(solution)/shard_map/ppermute | solution.py:206
  566.9 73.2 %collective-permute-start.18 = (bf16[128,2048]{1,0:T(8,128)(2,1)S(1)}, bf16[128,2048]{1,0:T(8,128)(2,1)S(1)}, u32[]{:S(2)}, u32[]{:S(2)}) collective-permute-start(bf16[128,2048]{1,0:T(8,128)(2,1)S(1)} %add_convert_fusion.2), channel_id=1, source_target_pairs={{0,8},{8,0},{16,24},{24,16},{1,9},{9,1},{17,25},{25,17},{2,10},{10... | collective-permute-start | bytes 1572872 | tf_op jit(solution)/shard_map/ppermute | solution.py:202
  581.0 69.3 %collective-permute-start.20 = (bf16[256,1024]{1,0:T(8,128)(2,1)S(1)}, bf16[256,1024]{1,0:T(8,128)(2,1)S(1)}, u32[]{:S(2)}, u32[]{:S(2)}) collective-permute-start(bf16[256,1024]{1,0:T(8,128)(2,1)S(1)} %add_convert_fusion.1), channel_id=1, source_target_pairs={{0,8},{8,0},{16,24},{24,16},{1,9},{9,1},{17,25},{25,17},{2,10},{10... | collective-permute-start | bytes 1572872 | tf_op jit(solution)/shard_map/ppermute | solution.py:202
  638.6 10.5 %collective-permute-start.12 = (bf16[128,1536]{1,0:T(8,128)(2,1)}, bf16[128,1536]{1,0:T(8,128)(2,1)}, u32[]{:S(2)}, u32[]{:S(2)}) collective-permute-start(bf16[128,1536]{1,0:T(8,128)(2,1)} %reduce-scatter.5.cloned.1.call-done), channel_id=1, source_target_pairs={{0,16},{16,0},{8,24},{24,8},{1,17},{17,1},{9,25},{25,9},{2,18},{18... | collective-permute-start | bytes 1179656 | tf_op jit(solution)/shard_map/ppermute | solution.py:206
  650.2 1.8 collective-permute-start.13
  (52 other events, 517.5 us)
Sparse Core Ops, SparseCore 0:
  10.7 66.4 all-gather.6
  79.3 47.5 all-gather.8
  129.6 73.4 all-gather.10
  205.7 71.5 all-gather.12
  315.8 86.2 reduce-scatter.8
  406.3 63.0 reduce-scatter.6
  473.1 87.1 reduce-scatter.10
  564.3 74.2 reduce-scatter.4

commit v2 on v1

v2 whole, which is shorter than its diff:
```python
from functools import partial

import jax
import jax.numpy as jnp
from jax import lax
from jax.experimental import pallas as pl
from jax.experimental.pallas import tpu as pltpu
from jax.sharding import PartitionSpec as P

HEADS = 16
HEAD = 64
PAIR = 2 * HEAD
EPS = 1e-06
MASKED = -1e30
VMEM_BYTES = 56 * 2**20
BF16 = jnp.bfloat16
F32 = jnp.float32
NN = (((1,), (0,)), ((), ()))
NT = (((1,), (1,)), ((), ()))
TN = (((0,), (0,)), ((), ()))
SMALL_COST = pl.CostEstimate(flops=10**7, bytes_accessed=2**20, transcendentals=0)


def dot(left, right, dims=NN):
    return lax.dot_general(left, right, dims, preferred_element_type=F32)


def lanes_of(shape):
    return lax.broadcasted_iota(jnp.int32, shape, len(shape) - 1)


def three_parts(column):
    high = column.astype(BF16).astype(F32)
    rest = column - high
    middle = rest.astype(BF16).astype(F32)
    return high, middle, rest - middle


def block_rows(length):
    for rows in (224, 112, 16):
        if length % rows == 0:
            return rows
    return length


def attend_kernel(q_ref, k_ref, v_ref, key_base_ref, *refs):
    context_ref, query_ref = refs[-2:]
    length = q_ref.shape[0]
    rows = block_rows(length)
    low = lanes_of((length, PAIR)) < HEAD
    keys, values, key_base = k_ref[...], v_ref[...], key_base_ref[...]
    ones = jnp.ones((length, PAIR), BF16)
    keys_of = [jnp.where(low, keys, key_base), jnp.where(low, key_base, keys)]
    values_of = [jnp.where(low, values, ones), jnp.where(low, ones, values)]
    lane = lanes_of((rows, PAIR))
    low_rows = lane < HEAD
    for step in range(length // rows):
        span = slice(step * rows, (step + 1) * rows)
        queries = q_ref[span, :]
        results = []
        for head in range(2):
            base = HEAD * (1 - head)
            own = low_rows if head == 0 else jnp.logical_not(low_rows)
            unit = jnp.where(lane == base, 1.0, 0.0)
            scores = dot(jnp.where(own, queries, unit.astype(BF16)), keys_of[head], NT)
            highest = jnp.max(scores, axis=1, keepdims=True)
            weights = jnp.exp(scores - highest).astype(BF16)
            mixed = dot(weights, values_of[head])
            total = mixed[:, base : base + 1]
            high, middle, rest = three_parts(-(highest + jnp.log(total)))
            extra = jnp.where(lane == base + 3, rest, unit)
            extra = jnp.where(lane == base + 2, middle, extra)
            extra = jnp.where(lane == base + 1, high, extra)
            query_ref[head, span, :] = jnp.where(own, queries, extra.astype(BF16))
            results.append(mixed / total)
        context_ref[span, :] = jnp.where(low_rows, results[0], results[1]).astype(BF16)


def attend(mixed, key_base, pair, context, place, places):
    length = mixed.shape[0]
    tile = lambda column: pl.BlockSpec((length, PAIR), lambda i: (0, column))
    in_specs = [tile(3 * pair), tile(3 * pair + 1), tile(3 * pair + 2), tile(0)]
    operands = (mixed, mixed, mixed, key_base)
    aliases = {}
    if context is not None:
        in_specs.append(pl.BlockSpec(memory_space=pl.ANY))
        operands += (context,)
        aliases = {4: 0}
    return pl.pallas_call(
        attend_kernel,
        grid=(1,),
        in_specs=in_specs,
        out_specs=[tile(place), pl.BlockSpec((2, length, PAIR), lambda i: (0, 0, 0))],
        out_shape=[
            jax.ShapeDtypeStruct((length, places * PAIR), BF16),
            jax.ShapeDtypeStruct((2, length, PAIR), BF16),
        ],
        input_output_aliases=aliases,
        compiler_params=pltpu.CompilerParams(vmem_limit_bytes=VMEM_BYTES),
        cost_estimate=SMALL_COST,
        name="attend",
    )(*operands)


def attend_back_kernel(query_ref, k_ref, v_ref, grad_ref, context_ref, key_base_ref, *refs):
    grad_mixed_ref, sums_ref = refs[-2:]
    length = k_ref.shape[0]
    rows = block_rows(length)
    low = lanes_of((length, PAIR)) < HEAD
    keys, values, key_base = k_ref[...], v_ref[...], key_base_ref[...]
    ones = jnp.ones((length, PAIR), BF16)
    lane = lanes_of((rows, PAIR))
    low_rows = lane < HEAD
    steps = length // rows
    grad_q, grad_k, grad_v = [], [], []
    sum_q = jnp.zeros((1, PAIR), F32)
    for head in range(2):
        base = HEAD * (1 - head)
        own = low if head == 0 else jnp.logical_not(low)
        own_rows = low_rows if head == 0 else jnp.logical_not(low_rows)
        head_keys = jnp.where(own, keys, key_base)
        head_values = jnp.where(own, values, ones)
        sum_k = jnp.zeros((length, PAIR), F32)
        sum_v = jnp.zeros((length, PAIR), F32)
        for step in range(steps):
            span = slice(step * rows, (step + 1) * rows)
            queries = query_ref[head, span, :]
            grads = grad_ref[span, :]
            product = grads.astype(F32) * context_ref[span, :].astype(F32)
            inner = jnp.sum(jnp.where(own_rows, product, 0.0), axis=1, keepdims=True)
            high, middle, rest = three_parts(-inner)
            extra = jnp.where(lane == base + 2, rest, 0.0)
            extra = jnp.where(lane == base + 1, middle, extra)
            extra = jnp.where(lane == base, high, extra)
            head_grads = jnp.where(own_rows, grads, extra.astype(BF16))
            probs = jnp.exp(dot(head_keys, queries, NT))
            grad_scores = (probs * dot(head_values, head_grads, NT)).astype(BF16)
            sum_v = sum_v + dot(probs.astype(BF16), grads)
            sum_k = sum_k + dot(grad_scores, queries)
            part = dot(grad_scores, keys, TN)
            if head == 0:
                grad_q.append(part)
            else:
                both = jnp.where(low_rows, grad_q[step], part).astype(BF16)
                both = both * (HEAD ** (-0.5))
                grad_mixed_ref[span, :PAIR] = both
                sum_q = sum_q + jnp.sum(both.astype(F32), axis=0, keepdims=True)
        grad_k.append(sum_k)
        grad_v.append(sum_v)
    grad_mixed_ref[:, PAIR : 2 * PAIR] = jnp.where(low, grad_k[0], grad_k[1]).astype(BF16)
    both = jnp.where(low, grad_v[0], grad_v[1]).astype(BF16)
    grad_mixed_ref[:, 2 * PAIR :] = both
    sums_ref[0:1, :] = sum_q
    sums_ref[1:2, :] = jnp.sum(both.astype(F32), axis=0, keepdims=True)


def attend_back(queries, mixed, grad_context, context, key_base, pair, place, grad_mixed):
    length = mixed.shape[0]
    tile = lambda column: pl.BlockSpec((length, PAIR), lambda i: (0, column))
    in_specs = [
        pl.BlockSpec((2, length, PAIR), lambda i: (0, 0, 0)),
        tile(3 * pair + 1),
        tile(3 * pair + 2),
        tile(place),
        tile(place),
        tile(0),
    ]
    operands = (queries, mixed, mixed, grad_context, context, key_base)
    aliases = {}
    if grad_mixed is not None:
        in_specs.append(pl.BlockSpec(memory_space=pl.ANY))
        operands += (grad_mixed,)
        aliases = {6: 0}
    return pl.pallas_call(
        attend_back_kernel,
        grid=(1,),
        in_specs=in_specs,
        out_specs=[
            pl.BlockSpec((length, 3 * PAIR), lambda i: (0, pair)),
            pl.BlockSpec((2, PAIR), lambda i: (0, 0)),
        ],
        out_shape=[
            jax.ShapeDtypeStruct((length, 6 * PAIR), BF16),
            jax.ShapeDtypeStruct((2, PAIR), F32),
        ],
        input_output_aliases=aliases,
        compiler_params=pltpu.CompilerParams(vmem_limit_bytes=VMEM_BYTES),
        cost_estimate=SMALL_COST,
        name="attend_back",
    )(*operands)


def normalize(values):
    center = values - jnp.mean(values, axis=-1, keepdims=True)
    spread = jnp.mean(center * center, axis=-1, keepdims=True)
    scale = lax.rsqrt(spread + EPS)
    return center * scale, scale


def normalize_back(normal, scale, grad, gain):
    inner = grad * gain
    first = jnp.mean(inner, axis=-1, keepdims=True)
    second = jnp.mean(inner * normal, axis=-1, keepdims=True)
    return scale * (inner - first - normal * second)


def gelu_both(values):
    half = 0.5 * (1.0 + lax.erf(values * (0.5**0.5)))
    density = jnp.exp(-0.5 * values * values) * (0.5 / jnp.pi) ** 0.5
    return values * half, half + values * density


def column_sum(values):
    return jnp.sum(values, axis=0, dtype=F32)


def swap_core(values):
    return lax.ppermute(values, "seq", [(0, 1), (1, 0), (2, 3), (3, 2)])


def swap_chip(values):
    return lax.ppermute(values, "seq", [(0, 2), (2, 0), (1, 3), (3, 1)])


def with_partner(values):
    return jnp.concatenate([values, swap_core(values)], axis=0)


def sum_partner(partial_sums):
    half = partial_sums.shape[0] // 2
    received = swap_core(partial_sums[half:].astype(BF16))
    return partial_sums[:half] + received.astype(F32)


def swap_group(values, bit):
    return lax.ppermute(values, "fsdp", [(i, i ^ bit) for i in range(8)])


def order_kernel(count, *refs):
    pieces, full_ref, sems = refs[:count], refs[count], refs[-1]
    group = lax.axis_index("fsdp")
    rows = full_ref.shape[0] // count
    copies = []
    for relative, piece in enumerate(pieces):
        start = pl.multiple_of((group ^ relative) * rows, rows)
        copies.append(
            pltpu.make_async_copy(
                piece.at[pl.ds(0, rows)], full_ref.at[pl.ds(start, rows)], sems.at[relative]
            )
        )
    for copy in copies:
        copy.start()
    if len(refs) > count + 2:
        own_width, core = 128, lax.rem(lax.axis_index("seq"), 2)
        wide_ref, bias_ref = refs[count + 1], refs[count + 2]
        for relative, piece in enumerate(pieces):
            place = group ^ relative
            columns = pl.ds(pl.multiple_of(place * own_width, own_width), own_width)
            extra = piece[rows : rows + 8, :].astype(F32)
            lines = [
                extra[k : k + 1, own_width * n : own_width * (n + 1)]
                for k in range(2)
                for n in range(6)
            ]
            for n in range(8):
                wide_ref[n : n + 1, columns] = lines[n]
            for n in range(2):
                start = pl.multiple_of((place * 2 + n) * own_width, own_width)
                bias_ref[:, pl.ds(start, own_width)] = jnp.where(
                    core == 0, lines[8 + n], lines[10 + n]
                )
    for copy in copies:
        copy.wait()


def in_order(pieces, rows, with_vectors=False):
    count, columns = len(pieces), pieces[0].shape[1]
    out_specs = [pl.BlockSpec(memory_space=pl.ANY)]
    out_shape = [jax.ShapeDtypeStruct((count * rows, columns), pieces[0].dtype)]
    if with_vectors:
        out_specs += [pl.BlockSpec(memory_space=pltpu.VMEM)] * 2
        out_shape += [jax.ShapeDtypeStruct((8, 1024), F32), jax.ShapeDtypeStruct((1, 2048), F32)]
    result = pl.pallas_call(
        partial(order_kernel, count),
        in_specs=[pl.BlockSpec(memory_space=pltpu.VMEM)] * count,
        out_specs=out_specs,
        out_shape=out_shape,
        scratch_shapes=[pltpu.SemaphoreType.DMA((count,))],
        compiler_params=pltpu.CompilerParams(vmem_limit_bytes=16 * 2**20),
        cost_estimate=pl.CostEstimate(
            flops=0, bytes_accessed=4 * count * rows * columns, transcendentals=0
        ),
        name="in_order",
    )(*pieces)
    return result if with_vectors else result[0]


def own_kernel(qkv_ref, out_ref, *refs):
    vector_refs, (first_ref, second_ref) = refs[:-2], refs[-2:]
    core = lax.rem(lax.axis_index("seq"), 2)
    rows = qkv_ref.shape[0]
    for n in range(3):
        for pair in range(4):
            block_ref = second_ref if pair >= 2 else first_ref
            start = pl.multiple_of((8 * n + pair + 4 * core) * PAIR, PAIR)
            target = (3 * (pair % 2) + n) * PAIR
            block_ref[:rows, target : target + PAIR] = qkv_ref[:, pl.ds(start, PAIR)]
    out_half = out_ref.shape[1] // 2
    start = pl.multiple_of(core * out_half, out_half)
    second_ref[:, 6 * PAIR :] = out_ref[:, pl.ds(start, out_half)]
    lines = []
    for ref in vector_refs:
        vector = ref[...].astype(F32).reshape(ref.shape[0] // PAIR, PAIR)
        lines += [vector[n : n + 1] for n in range(ref.shape[0] // PAIR)]
    row = lax.broadcasted_iota(jnp.int32, (8, PAIR), 0)
    for n in range(6):
        block = jnp.where(row == 0, lines[n], jnp.where(row == 1, lines[n + 6], 0.0))
        first_ref[rows:, PAIR * n : PAIR * (n + 1)] = block.astype(BF16)


def own_qkv_blocks(qkv_weight, out_weight, vectors):
    rows, columns = qkv_weight.shape[0], qkv_weight.shape[1] // 4
    out_half = out_weight.shape[1] // 2
    return pl.pallas_call(
        own_kernel,
        in_specs=[pl.BlockSpec(memory_space=pltpu.VMEM)] * (2 + len(vectors)),
        out_specs=[pl.BlockSpec(memory_space=pltpu.VMEM)] * 2,
        out_shape=[
            jax.ShapeDtypeStruct((rows + 8, columns), BF16),
            jax.ShapeDtypeStruct((rows, columns + out_half), BF16),
        ],
        cost_estimate=SMALL_COST,
        name="own_qkv",
    )(qkv_weight, out_weight, *vectors)


def after(values, *others):
    return lax.optimization_barrier((values,) + others)[0] if others else values


class Gather:
    SOURCE = {4: 0, 2: 0, 1: 0, 6: 4, 3: 2, 5: 4, 7: 6}
    STEP = {4: 4, 2: 2, 1: 1, 6: 2, 3: 1, 5: 1, 7: 1}

    def __init__(self, own):
        self.pieces = [own] + [None] * 7
        self.grouped = lax.axis_size("fsdp") == 8

    def send(self, *parts, ready=()):
        if not self.grouped:
            return
        sources = [self.pieces[self.SOURCE[part]] for part in parts]
        if ready:
            sources = lax.optimization_barrier(tuple(sources) + tuple(ready))
        for part, source in zip(parts, sources):
            self.pieces[part] = swap_group(source, self.STEP[part])

    def got(self, *parts):
        return tuple(self.pieces[part] for part in parts) if self.grouped else ()

    def result(self):
        if not self.grouped:
            return lax.all_gather(self.pieces[0], "fsdp", axis=0, tiled=True)
        return in_order(self.pieces, self.pieces[0].shape[0])


def add_low(left, right):
    return (left.astype(F32) + right.astype(F32)).astype(BF16)


def split_kernel(full_ref, *refs):
    sems = refs[2]
    group = lax.axis_index("fsdp")
    rows = full_ref.shape[0] // 8
    copies = []
    for n in range(8):
        far, near, side = n % 2, (n // 2) % 2, n // 4
        start = pl.multiple_of((group ^ (4 * far + 2 * near + side)) * rows, rows)
        target = refs[side].at[pl.ds((n % 4) * rows, rows)]
        copies.append(
            pltpu.make_async_copy(full_ref.at[pl.ds(start, rows)], target, sems.at[n])
        )
    for copy in copies:
        copy.start()
    for copy in copies:
        copy.wait()


def split_blocks(values):
    rows, columns = values.shape
    return pl.pallas_call(
        split_kernel,
        in_specs=[pl.BlockSpec(memory_space=pltpu.VMEM)],
        out_specs=[pl.BlockSpec(memory_space=pl.ANY)] * 2,
        out_shape=[jax.ShapeDtypeStruct((rows // 2, columns), values.dtype)] * 2,
        scratch_shapes=[pltpu.SemaphoreType.DMA((8,))],
        compiler_params=pltpu.CompilerParams(vmem_limit_bytes=16 * 2**20),
        cost_estimate=SMALL_COST,
        name="split_blocks",
    )(values)


class Scatter:
    def __init__(self, values, *ready, halves=None):
        self.grouped = lax.axis_size("fsdp") == 8
        self.halved = halves is not None
        values = values.astype(BF16)
        if self.halved:
            self.kept, self.sent = halves
            self.crossed = swap_chip(self.sent)
        elif self.grouped:
            self.keep, self.side_send = split_blocks(values)
            self.side = swap_group(after(self.side_send, *ready), 1)
        else:
            self.sums = lax.psum_scatter(values, "fsdp", scatter_dimension=0, tiled=True)

    def cross(self, *ready):
        values = add_low(self.kept, after(self.crossed, *ready))
        if self.grouped:
            self.keep, self.side_send = split_blocks(values)
            self.side = swap_group(self.side_send, 1)
        else:
            self.sums = lax.psum_scatter(values, "fsdp", scatter_dimension=0, tiled=True)

    def got(self, *names):
        return tuple(getattr(self, name) for name in names if hasattr(self, name))

    def step(self, name, next_name, bit, ready):
        if self.grouped:
            received = after(getattr(self, name), *ready)
            half = self.keep.shape[0] // 2
            send = add_low(self.keep[half:], received[half:])
            self.keep = add_low(self.keep[:half], received[:half])
            setattr(self, next_name, swap_group(send, bit))

    def near(self, *ready):
        self.step("side", "near_sums", 2, ready)

    def far(self, *ready):
        self.step("near_sums", "far_sums", 4, ready)

    def chips(self, *ready):
        if self.grouped:
            self.sums = add_low(self.keep, after(self.far_sums, *ready))
        self.other_chip = swap_chip(self.sums)

    def cores(self, *ready):
        other_chip = after(self.other_chip, *ready)
        if self.halved:
            chip = lax.axis_index("seq") // 2
            first = jnp.where(chip == 0, self.sums, other_chip)
            second = jnp.where(chip == 0, other_chip, self.sums)
            self.total = jnp.concatenate([first, second], axis=1)
        else:
            self.total = add_low(self.sums, other_chip)
        self.other_core = swap_core(self.total)

    def finish(self):
        self.near()
        self.far()
        self.chips()
        self.cores()


def take(values, index):
    return lax.dynamic_index_in_dim(values, index, 0, keepdims=False)


def in_core_order(own, other, core, axis):
    first = jnp.where(core == 0, own, other)
    second = jnp.where(core == 0, other, own)
    return first, second


def body(
    inputs,
    cotangent,
    valid,
    ln1_gain,
    ln1_bias,
    qkv_weight,
    q_bias,
    v_bias,
    out_weight,
    out_bias,
    ln2_gain,
    ln2_bias,
    fc1_weight,
    fc1_bias,
    fc2_weight,
    fc2_bias,
):
    clips, rows, width = inputs.shape
    groups = lax.axis_size("fsdp")
    place = lax.axis_index("seq")
    group = lax.axis_index("fsdp")
    chip, core = place // 2, place % 2
    half = width // 2
    hidden_rows = fc2_weight.shape[0]
    half_rows = hidden_rows // 2
    own_rows = clips * rows
    scale_factor = HEAD ** (-0.5)

    def all_clips(values):
        mine, back = values[:rows], swap_chip(values[rows:])
        first = jnp.where(chip == 0, mine, back)
        second = jnp.where(chip == 0, back, mine)
        return jnp.stack([first, second])

    own_width = width // groups
    vectors = (ln1_gain, ln1_bias, q_bias, v_bias, out_bias, ln2_gain, ln2_bias, fc2_bias, fc1_bias)
    quarter = half // 2
    row_width = 3 * quarter
    used = 8 * own_width + fc1_bias.shape[0]
    if groups == 8:
        own_first, own_second = own_qkv_blocks(qkv_weight, out_weight, vectors)
    else:
        by_head = qkv_weight.reshape(own_width, 3, 2, 2, 2, PAIR)
        by_head = lax.dynamic_index_in_dim(by_head, core, 2, keepdims=False)
        by_head = by_head.transpose(0, 2, 3, 1, 4).reshape(own_width, 2, row_width)
        out_columns = lax.dynamic_slice_in_dim(out_weight, core * half, half, 1)
        own_first = by_head[:, 0]
        own_second = jnp.concatenate([by_head[:, 1], out_columns], axis=1)

    own_fc1 = lax.dynamic_index_in_dim(
        fc1_weight.reshape(own_width, groups, 2, half_rows), core, 2, keepdims=False
    ).reshape(own_width, groups * half_rows)
    own_fc2 = lax.dynamic_slice_in_dim(fc2_weight, core * half_rows, half_rows, 0)

    qkv_a, qkv_b = Gather(own_first), Gather(own_second)
    fc1_gather, fc2_gather = Gather(own_fc1), Gather(own_fc2)
    qkv_a.send(4, 2, 1)
    other_inputs = swap_chip(after(take(inputs, 1 - chip), own_first))
    qkv_a.send(6, 3, 5, ready=qkv_a.got(4, 2, 1) + (own_fc1, own_fc2))
    qkv_b.send(4, ready=qkv_a.got(4, 2, 1))
    qkv_a.send(7, ready=qkv_a.got(6, 3, 5))
    other_inputs = after(other_inputs, *qkv_a.got(6, 3, 5))
    qkv_b.send(2, 1, ready=qkv_a.got(6, 3, 5))
    own_inputs = jnp.concatenate([take(inputs, chip), other_inputs], axis=0)
    all_inputs = with_partner(own_inputs)
    if groups == 8:
        qkv_first, wide, bias_fc1 = in_order(qkv_a.pieces, own_width, True)
    else:
        qkv_first = qkv_a.result()
        packed = lax.all_gather(jnp.concatenate(vectors), "fsdp", axis=0)
        wide = [
            packed[:, i * own_width : (i + 1) * own_width].reshape(width).astype(F32)
            for i in range(8)
        ]
        bias_fc1 = packed[:, 8 * own_width : used].reshape(groups, 2, half_rows)
        bias_fc1 = take(jnp.moveaxis(bias_fc1, 1, 0), core)
        bias_fc1 = bias_fc1.reshape(groups * half_rows).astype(F32)
    gain_one, bias_one, bias_q, bias_v, bias_out, gain_two, bias_two, bias_fc2 = [
        wide[i] for i in range(8)
    ]
    bias_q = take(bias_q.reshape(2, 2, 2, PAIR), core)
    bias_v = take(bias_v.reshape(2, 2, 2, PAIR), core)
    bias_mixed = jnp.stack([bias_q, jnp.zeros_like(bias_q), bias_v], axis=2).reshape(2, row_width)
    scale_mixed = jnp.array([scale_factor, 1.0, 1.0] * 2, F32).repeat(PAIR)
    clip_valid = take(valid, chip).reshape(2 * clips, rows)
    own_valid = jnp.concatenate([take(clip_valid, place), take(clip_valid, place ^ 2)])
    other_valid = jnp.concatenate([take(clip_valid, place ^ 1), take(clip_valid, place ^ 3)])
    key_valid = jnp.concatenate([own_valid, other_valid])
    lane = jnp.arange(PAIR) % HEAD
    key_mask = jnp.where(key_valid > 0, 0.0, MASKED)[:, None]
    key_base = jnp.where(lane == 0, key_mask, jnp.where(lane < 4, 1.0, 0.0)).astype(BF16)


    def project(weight, i):
        return ((dot(h_one, weight) + bias_mixed[i]) * scale_mixed).astype(BF16)

    normal_one = normalize(all_inputs.astype(F32))[0]
    h_one = (normal_one * gain_one + bias_one).astype(BF16)
    mixed = [project(qkv_first, 0)]
    context, queries = [], []

    def attend_pair(pair, *ready):
        before = context[-1] if context else None
        base = after(key_base, *ready)
        results = attend(mixed[pair // 2], base, pair % 2, before, pair, 4)
        context.append(results[0])
        queries.append(results[1])

    ready = (mixed[0],) + qkv_b.got(4, 2, 1)
    qkv_b.send(6, 3, 5, ready=ready)
    fc1_gather.send(4, ready=ready)
    attend_pair(0, *ready)
    ready = (queries[0],) + qkv_b.got(6, 3, 5)
    qkv_b.send(7, ready=ready)
    fc1_gather.send(2, 1, ready=ready)
    attend_pair(1, *ready)
    second_columns = qkv_b.result()
    mixed.append(project(second_columns[:, :row_width], 1))
    ready = (queries[1], mixed[1]) + fc1_gather.got(4, 2, 1)
    fc1_gather.send(6, 3, 5, ready=ready)
    fc2_gather.send(4, ready=ready)
    kept = lax.dynamic_slice(second_columns, (core * half, row_width), (half, half))
    received = lax.dynamic_slice(second_columns, ((1 - core) * half, row_width), (half, half))
    received = swap_core(after(received, mixed[1]))
    attend_pair(2, kept, *ready)
    ready = (queries[2], received) + fc1_gather.got(6, 3, 5)
    fc1_gather.send(7, ready=ready)
    fc2_gather.send(2, ready=ready)
    other_grads = swap_chip(after(take(cotangent, 1 - chip), *ready))
    attend_pair(3, *ready)
    own_grads = jnp.concatenate([take(cotangent, chip), after(other_grads, queries[3])], axis=0)
    full_out = jnp.concatenate(in_core_order(kept, received, core, 1), axis=1)
    full_qkv = (qkv_first, second_columns[:, :row_width])
    ready = (own_grads, queries[3]) + fc2_gather.got(4, 2)
    all_context = after(context[3], *ready)
    fc2_gather.send(1, 3, 6, ready=ready)
    attn_branch = sum_partner(dot(all_context, full_out)) + bias_out
    residual_mid = own_inputs.astype(F32) + attn_branch
    normal_two, scale_two = normalize(residual_mid)
    h_two = with_partner((normal_two * gain_two + bias_two).astype(BF16))
    all_grads = with_partner(after(own_grads, residual_mid))
    full_fc1 = fc1_gather.result()
    h_two = after(h_two, *fc2_gather.got(1, 3, 6))
    fc2_gather.send(5, ready=(h_two,))
    active, slope = gelu_both(dot(h_two, full_fc1) + bias_fc1)
    active, slope = active.astype(BF16), slope.astype(BF16)
    active = after(active, *fc2_gather.got(5))
    fc2_gather.send(7, ready=(active,))
    fc2_product = dot(active, all_grads, TN).astype(BF16)
    fc2_scatter = Scatter(fc2_product)

    full_fc2 = fc2_gather.result()
    late_grads = after(all_grads, *fc2_scatter.got("keep"))
    grad_hidden = (dot(late_grads, full_fc2, NT) * slope.astype(F32)).astype(BF16)
    fc1_product = dot(h_two, grad_hidden, TN).astype(BF16)
    fc1_half = fc1_product.shape[1] // 2
    fc1_halves = [
        lax.dynamic_slice_in_dim(fc1_product, part * fc1_half, fc1_half, 1)
        for part in (chip, 1 - chip)
    ]
    fc1_scatter = Scatter(fc1_product, halves=fc1_halves)
    mlp_branch = sum_partner(dot(after(active, fc1_scatter.sent), full_fc2)) + bias_fc2
    residual_out = residual_mid + mlp_branch
    counted = own_valid.astype(F32)[:, None]
    squares = jnp.stack(
        [
            jnp.sum(counted * residual_out * residual_out),
            jnp.sum(counted * attn_branch * attn_branch),
            jnp.sum(counted * mlp_branch * mlp_branch),
            jnp.sum(counted),
        ]
    )
    low_output = residual_out.astype(BF16)
    grad_h_two = sum_partner(dot(after(grad_hidden, residual_out), full_fc1, NT))
    grad_residual = own_grads.astype(F32) + normalize_back(
        normal_two, scale_two, grad_h_two, gain_two
    )
    own_grad_attn = grad_residual.astype(BF16)
    grad_attn = with_partner(own_grad_attn)
    grad_out = dot(all_context, grad_attn, TN).astype(BF16)
    kept = lax.dynamic_slice_in_dim(grad_out, core * half, half, 1)
    received = swap_core(lax.dynamic_slice_in_dim(grad_out, (1 - core) * half, half, 1))
    grad_context = dot(grad_attn, full_out, NT).astype(BF16)
    halves, sums = [None, None], []

    def back_pair(pair, *ready):
        grad_mixed, parts = attend_back(
            queries[pair],
            mixed[pair // 2],
            grad_context,
            all_context,
            after(key_base, *ready),
            pair % 2,
            pair,
            halves[pair // 2],
        )
        halves[pair // 2] = grad_mixed
        sums.append(parts)

    back_pair(0, grad_context)
    grad_out = jnp.concatenate(
        in_core_order(kept, after(received, grad_context), core, 0), axis=0
    )
    ready = (sums[0], fc1_scatter.crossed) + fc2_scatter.got("side")
    fc2_scatter.near(*ready)
    fc1_scatter.cross(*ready)
    output = all_clips(after(low_output, *ready))
    back_pair(1, grad_out, *ready, *fc2_scatter.got("keep"), *fc1_scatter.got("keep"))
    early = jnp.concatenate([dot(h_one, halves[0], TN).astype(BF16), grad_out], axis=1)
    ready = (sums[1],) + fc2_scatter.got("near_sums") + fc1_scatter.got("side")
    fc2_scatter.far(*ready)
    fc1_scatter.near(*ready)
    early_scatter = Scatter(early, *ready)
    ready += fc2_scatter.got("keep") + fc1_scatter.got("keep") + early_scatter.got("keep")
    back_pair(2, *ready)
    ready = (sums[2], output) + fc2_scatter.got("far_sums") + fc1_scatter.got("near_sums")
    fc2_scatter.chips(*ready)
    fc1_scatter.far(*ready)
    back_pair(3, *ready, fc2_scatter.sums, *fc1_scatter.got("keep"))
    ready = (sums[3], fc2_scatter.other_chip) + fc1_scatter.got("far_sums")
    ready += early_scatter.got("side")
    fc1_scatter.chips(*ready)
    fc2_scatter.cores(*ready)
    early_scatter.near(*ready)
    late_scatter = Scatter(dot(after(h_one, fc1_scatter.sums, *ready), halves[1], TN))
    ready = late_scatter.got("keep")
    grad_h_one = sum_partner(
        dot(after(halves[0], *ready), full_qkv[0], NT) + dot(halves[1], full_qkv[1], NT)
    )
    own_normal, own_scale = normalize(own_inputs.astype(F32))
    input_grad = all_clips(
        (grad_residual + normalize_back(own_normal, own_scale, grad_h_one, gain_one)).astype(BF16)
    )

    def by_core(values):
        full = jnp.zeros((2, values.shape[0]), F32)
        return lax.dynamic_update_index_in_dim(full, values, core, 0).reshape(-1)

    vector_grads = [
        column_sum(grad_h_one * own_normal),
        column_sum(grad_h_one),
        by_core(jnp.concatenate([part[0] for part in sums])),
        by_core(jnp.concatenate([part[1] for part in sums])),
        column_sum(own_grad_attn),
        column_sum(grad_h_two * normal_two),
        column_sum(grad_h_two),
        column_sum(own_grads),
    ]
    hidden_sums = jnp.zeros((groups, 2, half_rows), F32)
    hidden_sums = lax.dynamic_update_index_in_dim(
        hidden_sums, column_sum(grad_hidden).reshape(groups, half_rows), core, 1
    )
    by_group = [part.reshape(groups, own_width) for part in vector_grads]
    by_group.append(hidden_sums.reshape(groups, hidden_rows))
    by_group.append(jnp.broadcast_to(squares, (groups, 4)))
    by_group = jnp.concatenate(by_group, axis=1).astype(BF16)
    by_group = jnp.pad(by_group, ((0, 0), (0, 16 * PAIR - by_group.shape[1])))
    vector_scatter = Scatter(by_group.reshape(groups * 16, PAIR))
    ready = vector_scatter.got("keep")
    late_scatter.near(*ready)
    early_scatter.far(*ready)
    vector_scatter.near()
    fc1_scatter.cores(*ready)
    late_scatter.far()
    vector_scatter.far()
    early_scatter.chips()
    vector_scatter.chips()
    late_scatter.chips()
    early_scatter.cores()
    vector_scatter.cores()
    late_scatter.cores()

    def in_columns(values, other, blocks):
        size = values.shape[1] // blocks
        parts = in_core_order(values, other, core, 0)
        parts = [part.reshape(own_width, blocks, 1, size) for part in parts]
        return jnp.concatenate(parts, axis=2).reshape(own_width, -1).astype(F32)

    fc2_grad = in_core_order(fc2_scatter.total, fc2_scatter.other_core, core, 0)
    fc2_grad = jnp.concatenate(fc2_grad, axis=0).astype(F32)
    fc1_grad = in_columns(fc1_scatter.total, fc1_scatter.other_core, groups)
    early, early_other = early_scatter.total, early_scatter.other_core
    late, late_other = late_scatter.total, late_scatter.other_core
    out_grad = in_columns(early[:, row_width:], early_other[:, row_width:], 1)

    def both_halves(left, right):
        left = left[:, :row_width].reshape(own_width, 1, 2, 3, PAIR)
        right = right.reshape(own_width, 1, 2, 3, PAIR)
        both = jnp.concatenate([left, right], axis=1).transpose(0, 3, 1, 2, 4)
        return both.reshape(own_width, 3 * half)

    qkv_grad = in_columns(both_halves(early, late), both_halves(early_other, late_other), 3)
    flat = vector_scatter.total.astype(F32) + vector_scatter.other_core.astype(F32)
    flat = flat.reshape(-1)
    own_vectors = [flat[i * own_width : (i + 1) * own_width] for i in range(8)]
    own_hidden = flat[8 * own_width : used]
    totals = flat[used : used + 4]
    branch_rms = jnp.sqrt(totals[:3] / (totals[3] * width))
    return (
        output,
        input_grad,
        own_vectors[0],
        own_vectors[1],
        qkv_grad,
        own_vectors[2],
        own_vectors[3],
        out_grad,
        own_vectors[4],
        own_vectors[5],
        own_vectors[6],
        fc1_grad,
        own_hidden,
        fc2_grad,
        own_vectors[7],
        branch_rms,
    )


def solution(mesh):
    tokens, rows, vector = P("fsdp", "seq", None), P("fsdp", None), P("fsdp")
    return jax.shard_map(
        body,
        mesh=mesh,
        in_specs=(
            tokens,
            tokens,
            rows,
            vector,
            vector,
            rows,
            vector,
            vector,
            rows,
            vector,
            vector,
            vector,
            rows,
            vector,
            rows,
            vector,
        ),
        out_specs=(
            tokens,
            tokens,
            vector,
            vector,
            rows,
            vector,
            vector,
            rows,
            vector,
            vector,
            vector,
            rows,
            vector,
            rows,
            vector,
            P(),
        ),
        check_vma=False,
    )
```

time: 670 us -> 560 us (0.84)
  waiting for transfers between devices: 253 us -> 121 us
  blocking collectives: 78.5 us -> 0 us
  starting transfers between devices: 14.7 us -> 72.9 us
  other arithmetic: 48.5 us -> 79.8 us
  Pallas kernels: 104 us -> 135 us
  matrix products: 109 us -> 94.1 us
  between operations: 16.1 us -> 3.13 us
  local copies, waits for them, and re-layouts: 37 us -> 46 us
    all_gather x4 -> x0, waiting for transfers between devices: 100 us -> none  [gather_rows(): return lax.all_gather(values, 'fsdp', axis=0, tiled=True)]
    ppermute x0 -> x43, waiting for transfers between devices: none -> 92.1 us  [swap_group(): return lax.ppermute(values, 'fsdp', [(i, i ^ bit) for i in range(8)])]
    ppermute x8 -> x10, waiting for transfers between devices: 83 us -> 24.9 us  [swap_chip(): return lax.ppermute(values, 'seq', [(0, 2), (2, 0), (1, 3), (3, 1)])]
    ppermute x0 -> x43, starting transfers between devices: none -> 58 us  [swap_group(): return lax.ppermute(values, 'fsdp', [(i, i ^ bit) for i in range(8)])]
    reduce_scatter x4 -> x0, waiting for transfers between devices: 57.6 us -> none  [scatter_rows(): lax.psum_scatter(values.astype(BF16), 'fsdp', scatter_dimension=0, tiled=...]
    psum x1 -> x0, blocking collectives: 47 us -> none  [body(): flat = lax.psum(flat, ('seq', 'fsdp'))]
    all_gather x1 -> x0, blocking collectives: 31.5 us -> none  [body(): packed = lax.all_gather(jnp.concatenate(vectors), 'fsdp', axis=0)]
    pallas_call x2 -> x18, Pallas kernels: 104 us -> 135 us  [the longest x4 73.6 us: attend_back(): pl.pallas_call(attend_back_kernel, grid=(1,), in_specs=in_specs, out_spec...]
  transfers between devices with their start and end apart: 29 -> 68, of which waited for: 16 -> 31; matrix products, arithmetic and copies ran while one was open for 23% -> 22% of each run, Pallas kernels for 16% -> 23%
where the time goes in v2:
time: 560 us; the launch traced here: 552 us
  Pallas kernels  135 us (24%)
  waiting for transfers between devices  121 us (22%)
  matrix products  94.1 us (17%)
  other arithmetic  79.8 us (14%)
  starting transfers between devices  72.9 us (13%)
  local copies, waits for them, and re-layouts  46 us (8%)
    dot_general x15, matrix products, dot(): return lax.dot_general(left, right, dims, preferred_element_type=F32)  94.1 us
    ppermute x43, waiting for transfers between devices, swap_group(): return lax.ppermute(values, 'fsdp', [(i, i ^ bit) for i in range(8)])  92.1 us
    pallas_call x4, Pallas kernels, attend_back(): pl.pallas_call(attend_back_kernel, grid=(1,), in_specs=in_specs, out_spec...  73.6 us
    ppermute x43, starting transfers between devices, swap_group(): return lax.ppermute(values, 'fsdp', [(i, i ^ bit) for i in range(8)])  58 us
    pallas_call x4, Pallas kernels, attend(): pl.pallas_call(attend_kernel, grid=(1,), in_specs=in_specs, out_specs=[ti...  47.7 us
    ppermute x10, waiting for transfers between devices, swap_chip(): return lax.ppermute(values, 'seq', [(0, 2), (2, 0), (1, 3), (3, 1)])  24.9 us
    convert_element_type x20, other arithmetic, add_low(): return (left.astype(F32) + right.astype(F32)).astype(BF16)  19.9 us
    unnamed x190, local copies, waits for them, and re-layouts  19.6 us
  transfers between devices with their start and end apart: 68, of which 31 were waited for; matrix products, arithmetic and copies ran while one was open for 22% of the time, Pallas kernels for 23%

profile of v2, /device:TPU:0, one launch (start us, length us, event | category | flops | bytes accessed | tf_op | source)
XLA Modules:
  0.0 552.0 jit_solution(14667743043267038151)
XLA Ops:
  56.1 4.3 multiply_convert_fusion.3.q_ref.k_ref.v_ref
  63.9 11.7 %attend.4 = (bf16[1568,512]{1,0:T(8,128)(2,1)}, bf16[2,1568,128]{2,1,0:T(8,128)(2,1)}) custom-call(bf16[1568,768]{1,0:T(8,128)(2,1)} %multiply_convert_fusion.3.q_ref.k_ref.v_ref, bf16[1568,768]{1,0:T(8,128)(2,1)} %multiply_convert_fusion.3.q_ref.k_ref.v_ref, bf16[1568,768]{1,0:T(8,128)(2,1)} %multiply_convert_fusion.3.q_ref.k_ref.v_ref, ...), custom_call_target="tpu_custom_call" | custom-call | flops 10000000 | bytes 1048576 | tf_op jit(solution)/shard_map/attend/pallas_call | solution.py:89
  101.4 11.6 %attend.5 = (bf16[1568,512]{1,0:T(8,128)(2,1)}, bf16[2,1568,128]{2,1,0:T(8,128)(2,1)}) custom-call(bf16[1568,768]{1,0:T(8,128)(2,1)} %multiply_convert_fusion.3.q_ref.k_ref.v_ref, bf16[1568,768]{1,0:T(8,128)(2,1)} %multiply_convert_fusion.3.q_ref.k_ref.v_ref, ...), custom_call_target="tpu_custom_call", output_to_operand_aliasing={{0}: (4, {})} | custom-call | flops 10000000 | bytes 1048576 | tf_op jit(solution)/shard_map/attend/pallas_call | solution.py:89
  120.5 12.1 %attend.6 = (bf16[1568,512]{1,0:T(8,128)(2,1)}, bf16[2,1568,128]{2,1,0:T(8,128)(2,1)}) custom-call(bf16[1568,768]{1,0:T(8,128)(2,1)} %multiply_convert_fusion.2.q_ref.k_ref.v_ref, bf16[1568,768]{1,0:T(8,128)(2,1)} %multiply_convert_fusion.2.q_ref.k_ref.v_ref, ...), custom_call_target="tpu_custom_call", output_to_operand_aliasing={{0}: (4, {})} | custom-call | flops 10000000 | bytes 1048576 | tf_op jit(solution)/shard_map/attend/pallas_call | solution.py:89
  132.6 9.3 %collective-permute-done.22.refs_5_ = bf16[128,2048]{1,0:T(8,128)(2,1)} collective-permute-done((bf16[128,2048]{1,0:T(8,128)(2,1)}, bf16[128,2048]{1,0:T(8,128)(2,1)}, u32[]{:S(2)}, u32[]{:S(2)}) %collective-permute-start.22) | collective-permute-done | bytes 524320 | tf_op jit(solution)/shard_map/ppermute | solution.py:236
  147.6 12.2 %attend.7 = (bf16[1568,512]{1,0:T(8,128)(2,1)}, bf16[2,1568,128]{2,1,0:T(8,128)(2,1)}) custom-call(bf16[1568,768]{1,0:T(8,128)(2,1)} %multiply_convert_fusion.2.q_ref.k_ref.v_ref, bf16[1568,768]{1,0:T(8,128)(2,1)} %multiply_convert_fusion.2.q_ref.k_ref.v_ref, ...), custom_call_target="tpu_custom_call", output_to_operand_aliasing={{0}: (4, {})} | custom-call | flops 10000000 | bytes 1048576 | tf_op jit(solution)/shard_map/attend/pallas_call | solution.py:89
  162.9 5.6 %collective-permute-done.24.refs_4_ = bf16[256,1024]{1,0:T(8,128)(2,1)S(1)} collective-permute-done((bf16[256,1024]{1,0:T(8,128)(2,1)S(1)}, bf16[256,1024]{1,0:T(8,128)(2,1)S(1)}, u32[]{:S(2)}, u32[]{:S(2)}) %collective-permute-start.24) | collective-permute-done | bytes 524320 | tf_op jit(solution)/shard_map/ppermute | solution.py:236
  184.9 11.1 %collective-permute-done.31.refs_7_ = bf16[128,2048]{1,0:T(8,128)(2,1)} collective-permute-done((bf16[128,2048]{1,0:T(8,128)(2,1)}, bf16[128,2048]{1,0:T(8,128)(2,1)}, u32[]{:S(2)}, u32[]{:S(2)}) %collective-permute-start.31) | collective-permute-done | bytes 524320 | tf_op jit(solution)/shard_map/ppermute | solution.py:236
  200.6 6.5 %collective-permute-done.28.refs_1_ = bf16[256,1024]{1,0:T(8,128)(2,1)S(1)} collective-permute-done((bf16[256,1024]{1,0:T(8,128)(2,1)S(1)}, bf16[256,1024]{1,0:T(8,128)(2,1)S(1)}, u32[]{:S(2)}, u32[]{:S(2)}) %collective-permute-start.28) | collective-permute-done | bytes 524320 | tf_op jit(solution)/shard_map/ppermute | solution.py:236
  207.1 10.9 %collective-permute-done.29.refs_3_ = bf16[256,1024]{1,0:T(8,128)(2,1)} collective-permute-done((bf16[256,1024]{1,0:T(8,128)(2,1)S(1)}, bf16[256,1024]{1,0:T(8,128)(2,1)}, u32[]{:S(2)}, u32[]{:S(2)}) %collective-permute-start.29) | collective-permute-done | bytes 524320 | tf_op jit(solution)/shard_map/ppermute | solution.py:236
  219.5 10.6 %multiply_convert_fusion.1 = (bf16[1568,2048]{1,0:T(8,128)(2,1)S(1)}, f32[1568,2048]{1,0:T(8,128)}) fusion(f32[2048]{0:T(1024)S(1)} %bitcast.146, bf16[1568,1024]{1,0:T(8,128)(2,1)S(1)} %pad_maximum_fusion.1, bf16[1024,2048]{1,0:T(8,128)(2,1)S(1)} %in_order.6), kind=kOutput, calls=%fused_computation.8 | convolution fusion | flops 6595936256 | bytes 26681344 | tf_op jit(solution)/shard_map/dot_general | solution.py:25
  232.9 8.5 %convolution_convert_fusion.1.full_ref = bf16[2048,1024]{1,0:T(8,128)(2,1)S(1)} fusion(bf16[1568,2048]{1,0:T(8,128)(2,1)S(1)} %get-tuple-element.162, bf16[1568,1024]{1,0:T(8,128)(2,1)S(1)} %constant_dynamic-update-slice_fusion), kind=kOutput, calls=%fused_computation.34 | convolution fusion | flops 6578765824 | bytes 13828096 | tf_op jit(solution)/shard_map/dot_general | solution.py:25
  245.8 13.4 %convert_reduce_fusion = (bf16[2048]{0:T(1024)(128)(2,1)S(1)}, bf16[1568,2048]{1,0:T(8,128)(2,1)S(1)}) fusion(f32[1568,2048]{1,0:T(8,128)} %get-tuple-element.322, f32[2048]{0:T(1024)S(1)} %bitcast.147, bf16[1568,1024]{1,0:T(8,128)(2,1)S(1)} %constant_dynamic-update-slice_fusion, bf16[2048,1024]{1,0:T(8,128)(2,1)S(1)} %in_order.7), kind=kOutput, calls=%fused_computation.6 | convolution fusion | flops 6624835584 | bytes 26685440 | tf_op jit(solution)/shard_map/dot_general | solution.py:25
  259.2 8.4 %convolution_convert_fusion = bf16[1024,2048]{1,0:T(8,128)(2,1)S(1)} fusion(bf16[1568,1024]{1,0:T(8,128)(2,1)S(1)} %pad_maximum_fusion.1, bf16[1568,2048]{1,0:T(8,128)(2,1)S(1)} %get-tuple-element.163), kind=kOutput, calls=%fused_computation.33 | convolution fusion | flops 6578765824 | bytes 13828096 | tf_op jit(solution)/shard_map/dot_general | solution.py:25
  271.1 9.5 %fusion.48 = f32[1568,1024]{1,0:T(8,128)S(1)} fusion(bf16[1568,2048]{1,0:T(8,128)(2,1)} %copy-done.85, bf16[2048,1024]{1,0:T(8,128)(2,1)S(1)} %in_order.7), kind=kOutput, calls=%fused_computation.220 | convolution fusion | flops 6576668672 | bytes 17039360 | tf_op jit(solution)/shard_map/dot_general | solution.py:25
  288.5 7.0 %fusion.49 = f32[1568,1024]{1,0:T(8,128)S(1)} fusion(bf16[1568,2048]{1,0:T(8,128)(2,1)S(1)} %get-tuple-element.163, bf16[1024,2048]{1,0:T(8,128)(2,1)S(1)} %in_order.6), kind=kOutput, calls=%fused_computation.221 | convolution fusion | flops 6576668672 | bytes 17039360 | tf_op jit(solution)/shard_map/dot_general | solution.py:25
  301.5 4.6 fusion.44
  310.9 5.0 convolution_convert_fusion.2.grad_ref
  316.0 18.3 %attend_back.4 = (bf16[1568,768]{1,0:T(8,128)(2,1)}, f32[2,128]{1,0:T(2,128)}) custom-call(bf16[2,1568,128]{2,1,0:T(8,128)(2,1)} %get-tuple-element.126.query_ref, bf16[1568,768]{1,0:T(8,128)(2,1)} %multiply_convert_fusion.3.q_ref.k_ref.v_ref, bf16[1568,768]{1,0:T(8,128)(2,1)} %multiply_convert_fusion.3.q_ref.k_ref.v_ref, ...), custom_call_target="tpu_custom_call" | custom-call | flops 10000000 | bytes 1048576 | tf_op jit(solution)/shard_map/attend_back/pallas_call | solution.py:174
  334.3 9.9 %collective-permute-done.39 = bf16[1024,1024]{1,0:T(8,128)(2,1)} collective-permute-done((bf16[1024,1024]{1,0:T(8,128)(2,1)}, bf16[1024,1024]{1,0:T(8,128)(2,1)}, u32[]{:S(2)}, u32[]{:S(2)}) %collective-permute-start.39) | collective-permute-done | bytes 2097184 | tf_op jit(solution)/shard_map/ppermute | solution.py:236
  357.6 18.5 %attend_back.5 = (bf16[1568,768]{1,0:T(8,128)(2,1)}, f32[2,128]{1,0:T(2,128)}) custom-call(bf16[2,1568,128]{2,1,0:T(8,128)(2,1)} %get-tuple-element.130.query_ref, bf16[1568,768]{1,0:T(8,128)(2,1)} %multiply_convert_fusion.3.q_ref.k_ref.v_ref, bf16[1568,768]{1,0:T(8,128)(2,1)} %multiply_convert_fusion.3.q_ref.k_ref.v_ref, ...), custom_call_target="tpu_custom_call", output_to_operand_aliasing={{0}: (6, {})} | custom-call | flops 10000000 | bytes 1048576 | tf_op jit(solution)/shard_map/attend_back/pallas_call | solution.py:174
  376.1 4.9 convolution_convert_fusion.4
  390.2 10.7 %collective-permute-done.40 = bf16[392,1024]{1,0:T(8,128)(2,1)S(1)} collective-permute-done((bf16[392,1024]{1,0:T(8,128)(2,1)S(1)}, bf16[392,1024]{1,0:T(8,128)(2,1)S(1)}, u32[]{:S(2)}, u32[]{:S(2)}) %collective-permute-start.40) | collective-permute-done | bytes 802848 | tf_op jit(solution)/shard_map/ppermute | solution.py:222
  403.9 18.2 %attend_back.6 = (bf16[1568,768]{1,0:T(8,128)(2,1)}, f32[2,128]{1,0:T(2,128)}) custom-call(bf16[2,1568,128]{2,1,0:T(8,128)(2,1)} %get-tuple-element.136.query_ref, bf16[1568,768]{1,0:T(8,128)(2,1)} %multiply_convert_fusion.2.q_ref.k_ref.v_ref, bf16[1568,768]{1,0:T(8,128)(2,1)} %multiply_convert_fusion.2.q_ref.k_ref.v_ref, ...), custom_call_target="tpu_custom_call" | custom-call | flops 10000000 | bytes 1048576 | tf_op jit(solution)/shard_map/attend_back/pallas_call | solution.py:174
  426.2 18.6 %attend_back.7 = (bf16[1568,768]{1,0:T(8,128)(2,1)}, f32[2,128]{1,0:T(2,128)}) custom-call(bf16[2,1568,128]{2,1,0:T(8,128)(2,1)} %get-tuple-element.145.query_ref, bf16[1568,768]{1,0:T(8,128)(2,1)} %multiply_convert_fusion.2.q_ref.k_ref.v_ref, bf16[1568,768]{1,0:T(8,128)(2,1)} %multiply_convert_fusion.2.q_ref.k_ref.v_ref, ...), custom_call_target="tpu_custom_call", output_to_operand_aliasing={{0}: (6, {})} | custom-call | flops 10000000 | bytes 1048576 | tf_op jit(solution)/shard_map/attend_back/pallas_call | solution.py:174
  444.8 4.6 fusion.31
  455.9 4.8 convolution_add_fusion
  472.4 4.3 fusion.21
  479.9 7.2 %collective-permute-done.56 = bf16[256,1280]{1,0:T(8,128)(2,1)} collective-permute-done((bf16[256,1280]{1,0:T(8,128)(2,1)}, bf16[256,1280]{1,0:T(8,128)(2,1)}, u32[]{:S(2)}, u32[]{:S(2)}) %collective-permute-start.56) | collective-permute-done | bytes 655392 | tf_op jit(solution)/shard_map/ppermute | solution.py:236
  493.4 4.6 collective-permute-done.52
  500.2 5.1 collective-permute-done.53
  534.8 6.8 %collective-permute-done.58 = bf16[128,1280]{1,0:T(8,128)(2,1)} collective-permute-done((bf16[128,1280]{1,0:T(8,128)(2,1)S(1)}, bf16[128,1280]{1,0:T(8,128)(2,1)}, u32[]{:S(2)}, u32[]{:S(2)}) %collective-permute-start.58) | collective-permute-done | bytes 327712 | tf_op jit(solution)/shard_map/ppermute | solution.py:222
  (462 shorter events, 250.1 us)
Async XLA Ops:
  5.6 27.2 %collective-permute-start = (bf16[392,1024]{1,0:T(8,128)(2,1)}, bf16[392,1024]{1,0:T(8,128)(2,1)}, u32[]{:S(2)}, u32[]{:S(2)}) collective-permute-start(bf16[392,1024]{1,0:T(8,128)(2,1)} %get-tuple-element.110), channel_id=1, source_target_pairs={{0,16},{16,0},{8,24},{24,8},{1,17},{17,1},{9,25},{25,9},{2,18},{18... | collective-permute-start | bytes 2408456 | tf_op jit(solution)/shard_map/ppermute | solution.py:222
  37.5 22.9 %collective-permute-start.11 = (bf16[128,1280]{1,0:T(8,128)(2,1)S(1)}, bf16[128,1280]{1,0:T(8,128)(2,1)S(1)}, u32[]{:S(2)}, u32[]{:S(2)}) collective-permute-start(bf16[128,1280]{1,0:T(8,128)(2,1)S(1)} %copy-done.13), channel_id=1, source_target_pairs={{0,4},{1,5},{2,6},{3,7},{4,0},{5,1},{6,2},{7,3},{8,12},{9,13},{10,... | collective-permute-start | bytes 983048 | tf_op jit(solution)/shard_map/ppermute | solution.py:236
  40.8 19.6 %collective-permute-start.10 = (bf16[128,1280]{1,0:T(8,128)(2,1)S(1)}, bf16[128,1280]{1,0:T(8,128)(2,1)S(1)}, u32[]{:S(2)}, u32[]{:S(2)}) collective-permute-start(bf16[128,1280]{1,0:T(8,128)(2,1)S(1)} %copy-done.13), channel_id=1, source_target_pairs={{0,2},{1,3},{2,0},{3,1},{4,6},{5,7},{6,4},{7,5},{8,10},{9,11},{10,... | collective-permute-start | bytes 983048 | tf_op jit(solution)/shard_map/ppermute | solution.py:236
  41.1 19.3 %collective-permute-start.9 = (bf16[128,1280]{1,0:T(8,128)(2,1)S(1)}, bf16[128,1280]{1,0:T(8,128)(2,1)S(1)}, u32[]{:S(2)}, u32[]{:S(2)}) collective-permute-start(bf16[128,1280]{1,0:T(8,128)(2,1)S(1)} %copy-done.13), channel_id=1, source_target_pairs={{0,1},{1,0},{2,3},{3,2},{4,5},{5,4},{6,7},{7,6},{8,9},{9,8},{10,11... | collective-permute-start | bytes 983048 | tf_op jit(solution)/shard_map/ppermute | solution.py:236
  79.9 33.1 %collective-permute-start.16 = (bf16[128,2048]{1,0:T(8,128)(2,1)S(1)}, bf16[128,2048]{1,0:T(8,128)(2,1)}, u32[]{:S(2)}, u32[]{:S(2)}) collective-permute-start(bf16[128,2048]{1,0:T(8,128)(2,1)S(1)} %bitcast.142), channel_id=1, source_target_pairs={{0,4},{1,5},{2,6},{3,7},{4,0},{5,1},{6,2},{7,3},{8,12},{9,13},{10,... | collective-permute-start | bytes 1572872 | tf_op jit(solution)/shard_map/ppermute | solution.py:236
  83.2 29.8 %collective-permute-start.17 = (bf16[128,2048]{1,0:T(8,128)(2,1)S(1)}, bf16[128,2048]{1,0:T(8,128)(2,1)}, u32[]{:S(2)}, u32[]{:S(2)}) collective-permute-start(bf16[128,2048]{1,0:T(8,128)(2,1)S(1)} %bitcast.143), channel_id=1, source_target_pairs={{0,2},{1,3},{2,0},{3,1},{4,6},{5,7},{6,4},{7,5},{8,10},{9,11},{10,... | collective-permute-start | bytes 1572872 | tf_op jit(solution)/shard_map/ppermute | solution.py:236
  84.7 28.3 %collective-permute-start.18 = (bf16[128,2048]{1,0:T(8,128)(2,1)S(1)}, bf16[128,2048]{1,0:T(8,128)(2,1)S(1)}, u32[]{:S(2)}, u32[]{:S(2)}) collective-permute-start(bf16[128,2048]{1,0:T(8,128)(2,1)S(1)} %bitcast.144), channel_id=1, source_target_pairs={{0,1},{1,0},{2,3},{3,2},{4,5},{5,4},{6,7},{7,6},{8,9},{9,8},{10,11... | collective-permute-start | bytes 1572872 | tf_op jit(solution)/shard_map/ppermute | solution.py:236
  118.1 23.9 %collective-permute-start.22 = (bf16[128,2048]{1,0:T(8,128)(2,1)}, bf16[128,2048]{1,0:T(8,128)(2,1)}, u32[]{:S(2)}, u32[]{:S(2)}) collective-permute-start(bf16[128,2048]{1,0:T(8,128)(2,1)} %collective-permute-done.16.refs_4_), channel_id=1, source_target_pairs={{0,1},{1,0},{2,3},{3,2},{4,5},{5,4},{6,7},{7,6},{8,9},{9,8},{10,11... | collective-permute-start | bytes 1572872 | tf_op jit(solution)/shard_map/ppermute | solution.py:236
  141.9 19.5 %collective-permute-start.23 = (bf16[392,1024]{1,0:T(8,128)(2,1)S(1)}, bf16[392,1024]{1,0:T(8,128)(2,1)S(1)}, u32[]{:S(2)}, u32[]{:S(2)}) collective-permute-start(bf16[392,1024]{1,0:T(8,128)(2,1)S(1)} %get-tuple-element.144), channel_id=1, source_target_pairs={{0,16},{16,0},{8,24},{24,8},{1,17},{17,1},{9,25},{25,9},{2,18},{18... | collective-permute-start | bytes 2408456 | tf_op jit(solution)/shard_map/ppermute | solution.py:222
  142.5 26.0 %collective-permute-start.24 = (bf16[256,1024]{1,0:T(8,128)(2,1)S(1)}, bf16[256,1024]{1,0:T(8,128)(2,1)S(1)}, u32[]{:S(2)}, u32[]{:S(2)}) collective-permute-start(bf16[256,1024]{1,0:T(8,128)(2,1)S(1)} %copy-done.4), channel_id=1, source_target_pairs={{0,4},{1,5},{2,6},{3,7},{4,0},{5,1},{6,2},{7,3},{8,12},{9,13},{10,... | collective-permute-start | bytes 1572872 | tf_op jit(solution)/shard_map/ppermute | solution.py:236
  146.0 23.8 %collective-permute-start.25 = (bf16[256,1024]{1,0:T(8,128)(2,1)S(1)}, bf16[256,1024]{1,0:T(8,128)(2,1)S(1)}, u32[]{:S(2)}, u32[]{:S(2)}) collective-permute-start(bf16[256,1024]{1,0:T(8,128)(2,1)S(1)} %copy-done.4), channel_id=1, source_target_pairs={{0,2},{1,3},{2,0},{3,1},{4,6},{5,7},{6,4},{7,5},{8,10},{9,11},{10,... | collective-permute-start | bytes 1572872 | tf_op jit(solution)/shard_map/ppermute | solution.py:236
  182.4 24.7 %collective-permute-start.28 = (bf16[256,1024]{1,0:T(8,128)(2,1)S(1)}, bf16[256,1024]{1,0:T(8,128)(2,1)S(1)}, u32[]{:S(2)}, u32[]{:S(2)}) collective-permute-start(bf16[256,1024]{1,0:T(8,128)(2,1)S(1)} %copy-done.4), channel_id=1, source_target_pairs={{0,1},{1,0},{2,3},{3,2},{4,5},{5,4},{6,7},{7,6},{8,9},{9,8},{10,11... | collective-permute-start | bytes 1572872 | tf_op jit(solution)/shard_map/ppermute | solution.py:236
  182.9 35.0 %collective-permute-start.29 = (bf16[256,1024]{1,0:T(8,128)(2,1)S(1)}, bf16[256,1024]{1,0:T(8,128)(2,1)}, u32[]{:S(2)}, u32[]{:S(2)}) collective-permute-start(bf16[256,1024]{1,0:T(8,128)(2,1)S(1)} %collective-permute-done.25.refs_2_), channel_id=1, source_target_pairs={{0,1},{1,0},{2,3},{3,2},{4,5},{5,4},{6,7},{7,6},{8,9},{9,8},{10,11... | collective-permute-start | bytes 1572872 | tf_op jit(solution)/shard_map/ppermute | solution.py:236
  184.4 33.5 %collective-permute-start.30 = (bf16[256,1024]{1,0:T(8,128)(2,1)S(1)}, bf16[256,1024]{1,0:T(8,128)(2,1)}, u32[]{:S(2)}, u32[]{:S(2)}) collective-permute-start(bf16[256,1024]{1,0:T(8,128)(2,1)S(1)} %collective-permute-done.24.refs_4_), channel_id=1, source_target_pairs={{0,2},{1,3},{2,0},{3,1},{4,6},{5,7},{6,4},{7,5},{8,10},{9,11},{10,... | collective-permute-start | bytes 1572872 | tf_op jit(solution)/shard_map/ppermute | solution.py:236
  198.2 31.9 %collective-permute-start.33 = (bf16[784,1024]{1,0:T(8,128)(2,1)S(1)}, bf16[784,1024]{1,0:T(8,128)(2,1)S(1)}, u32[]{:S(2)}, u32[]{:S(2)}) collective-permute-start(bf16[784,1024]{1,0:T(8,128)(2,1)S(1)} %copy-done.50), channel_id=1, source_target_pairs={{0,8},{8,0},{16,24},{24,16},{1,9},{9,1},{17,25},{25,17},{2,10},{10... | collective-permute-start | bytes 4816904 | tf_op jit(solution)/shard_map/ppermute | solution.py:218
  296.0 48.2 %collective-permute-start.39 = (bf16[1024,1024]{1,0:T(8,128)(2,1)}, bf16[1024,1024]{1,0:T(8,128)(2,1)}, u32[]{:S(2)}, u32[]{:S(2)}) collective-permute-start(bf16[1024,1024]{1,0:T(8,128)(2,1)} %get-tuple-element.166), channel_id=1, source_target_pairs={{0,1},{1,0},{2,3},{3,2},{4,5},{5,4},{6,7},{7,6},{8,9},{9,8},{10,11... | collective-permute-start | bytes 6291464 | tf_op jit(solution)/shard_map/ppermute | solution.py:236
  297.5 47.9 %collective-permute-start.38 = (bf16[1024,1024]{1,0:T(8,128)(2,1)}, bf16[1024,1024]{1,0:T(8,128)(2,1)}, u32[]{:S(2)}, u32[]{:S(2)}) collective-permute-start(bf16[1024,1024]{1,0:T(8,128)(2,1)} %constant_dynamic-slice_fusion.1), channel_id=1, source_target_pairs={{0,16},{16,0},{8,24},{24,8},{1,17},{17,1},{9,25},{25,9},{2,18},{18... | collective-permute-start | bytes 6291464 | tf_op jit(solution)/shard_map/ppermute | solution.py:222
  356.7 26.0 %collective-permute-start.41 = (bf16[512,512]{1,0:T(8,128)(2,1)}, bf16[512,512]{1,0:T(8,128)(2,1)}, u32[]{:S(2)}, u32[]{:S(2)}) collective-permute-start(bf16[512,512]{1,0:T(8,128)(2,1)} %constant_dynamic-slice_fusion), channel_id=1, source_target_pairs={{0,8},{8,0},{16,24},{24,16},{1,9},{9,1},{17,25},{25,17},{2,10},{10... | collective-permute-start | bytes 1572872 | tf_op jit(solution)/shard_map/ppermute | solution.py:218
  356.7 28.6 %collective-permute-start.42 = (bf16[512,1024]{1,0:T(8,128)(2,1)S(1)}, bf16[512,1024]{1,0:T(8,128)(2,1)}, u32[]{:S(2)}, u32[]{:S(2)}) collective-permute-start(bf16[512,1024]{1,0:T(8,128)(2,1)S(1)} %get-tuple-element.175), channel_id=1, source_target_pairs={{0,1},{1,0},{2,3},{3,2},{4,5},{5,4},{6,7},{7,6},{8,9},{9,8},{10,11... | collective-permute-start | bytes 3145736 | tf_op jit(solution)/shard_map/ppermute | solution.py:236
  357.2 28.1 %collective-permute-start.43 = (bf16[512,1024]{1,0:T(8,128)(2,1)}, bf16[512,1024]{1,0:T(8,128)(2,1)}, u32[]{:S(2)}, u32[]{:S(2)}) collective-permute-start(bf16[512,1024]{1,0:T(8,128)(2,1)} %get-tuple-element.253), channel_id=1, source_target_pairs={{0,2},{1,3},{2,0},{3,1},{4,6},{5,7},{6,4},{7,5},{8,10},{9,11},{10,... | collective-permute-start | bytes 3145736 | tf_op jit(solution)/shard_map/ppermute | solution.py:236
  381.1 19.8 %collective-permute-start.40 = (bf16[392,1024]{1,0:T(8,128)(2,1)S(1)}, bf16[392,1024]{1,0:T(8,128)(2,1)S(1)}, u32[]{:S(2)}, u32[]{:S(2)}) collective-permute-start(bf16[392,1024]{1,0:T(8,128)(2,1)S(1)} %slice.313), channel_id=1, source_target_pairs={{0,16},{16,0},{8,24},{24,8},{1,17},{17,1},{9,25},{25,9},{2,18},{18... | collective-permute-start | bytes 2408456 | tf_op jit(solution)/shard_map/ppermute | solution.py:222
  386.9 35.9 %collective-permute-start.44 = (bf16[256,1024]{1,0:T(8,128)(2,1)S(1)}, bf16[256,1024]{1,0:T(8,128)(2,1)S(1)}, u32[]{:S(2)}, u32[]{:S(2)}) collective-permute-start(bf16[256,1024]{1,0:T(8,128)(2,1)S(1)} %get-tuple-element.261), channel_id=1, source_target_pairs={{0,2},{1,3},{2,0},{3,1},{4,6},{5,7},{6,4},{7,5},{8,10},{9,11},{10,... | collective-permute-start | bytes 1572872 | tf_op jit(solution)/shard_map/ppermute | solution.py:236
  390.2 32.7 %collective-permute-start.45 = (bf16[256,1024]{1,0:T(8,128)(2,1)S(1)}, bf16[256,1024]{1,0:T(8,128)(2,1)S(1)}, u32[]{:S(2)}, u32[]{:S(2)}) collective-permute-start(bf16[256,1024]{1,0:T(8,128)(2,1)S(1)} %get-tuple-element.263), channel_id=1, source_target_pairs={{0,4},{1,5},{2,6},{3,7},{4,0},{5,1},{6,2},{7,3},{8,12},{9,13},{10,... | collective-permute-start | bytes 1572872 | tf_op jit(solution)/shard_map/ppermute | solution.py:236
  402.3 47.1 %collective-permute-start.48 = (bf16[512,1280]{1,0:T(8,128)(2,1)S(1)}, bf16[512,1280]{1,0:T(8,128)(2,1)}, u32[]{:S(2)}, u32[]{:S(2)}) collective-permute-start(bf16[512,1280]{1,0:T(8,128)(2,1)S(1)} %get-tuple-element.188), channel_id=1, source_target_pairs={{0,1},{1,0},{2,3},{3,2},{4,5},{5,4},{6,7},{7,6},{8,9},{9,8},{10,11... | collective-permute-start | bytes 3932168 | tf_op jit(solution)/shard_map/ppermute | solution.py:236
  423.0 26.4 %collective-permute-start.47 = (bf16[256,1024]{1,0:T(8,128)(2,1)S(1)}, bf16[256,1024]{1,0:T(8,128)(2,1)S(1)}, u32[]{:S(2)}, u32[]{:S(2)}) collective-permute-start(bf16[256,1024]{1,0:T(8,128)(2,1)S(1)} %add_convert_fusion.7), channel_id=1, source_target_pairs={{0,16},{16,0},{8,24},{24,8},{1,17},{17,1},{9,25},{25,9},{2,18},{18... | collective-permute-start | bytes 1572872 | tf_op jit(solution)/shard_map/ppermute | solution.py:222
  424.8 24.6 %collective-permute-start.46 = (bf16[128,1024]{1,0:T(8,128)(2,1)S(1)}, bf16[128,1024]{1,0:T(8,128)(2,1)S(1)}, u32[]{:S(2)}, u32[]{:S(2)}) collective-permute-start(bf16[128,1024]{1,0:T(8,128)(2,1)S(1)} %get-tuple-element.279), channel_id=1, source_target_pairs={{0,4},{1,5},{2,6},{3,7},{4,0},{5,1},{6,2},{7,3},{8,12},{9,13},{10,... | collective-permute-start | bytes 786440 | tf_op jit(solution)/shard_map/ppermute | solution.py:236
  470.1 19.8 %collective-permute-start.59 = (bf16[512,768]{1,0:T(8,128)(2,1)S(1)}, bf16[512,768]{1,0:T(8,128)(2,1)}, u32[]{:S(2)}, u32[]{:S(2)}) collective-permute-start(bf16[512,768]{1,0:T(8,128)(2,1)S(1)} %get-tuple-element.198), channel_id=1, source_target_pairs={{0,1},{1,0},{2,3},{3,2},{4,5},{5,4},{6,7},{7,6},{8,9},{9,8},{10,11... | collective-permute-start | bytes 2359304 | tf_op jit(solution)/shard_map/ppermute | solution.py:236
  479.8 43.1 %collective-permute-start.66 = (bf16[128,2048]{1,0:T(8,128)(2,1)S(1)}, bf16[128,2048]{1,0:T(8,128)(2,1)S(1)}, u32[]{:S(2)}, u32[]{:S(2)}) collective-permute-start(bf16[128,2048]{1,0:T(8,128)(2,1)S(1)} %pad_maximum_fusion.14), channel_id=1, source_target_pairs={{0,8},{8,0},{16,24},{24,16},{1,9},{9,1},{17,25},{25,17},{2,10},{10... | collective-permute-start | bytes 1572872 | tf_op jit(solution)/shard_map/ppermute | solution.py:218
  488.1 29.9 %collective-permute-start.57 = (bf16[128,1280]{1,0:T(8,128)(2,1)S(1)}, bf16[128,1280]{1,0:T(8,128)(2,1)S(1)}, u32[]{:S(2)}, u32[]{:S(2)}) collective-permute-start(bf16[128,1280]{1,0:T(8,128)(2,1)S(1)} %add_convert_fusion.16), channel_id=1, source_target_pairs={{0,4},{1,5},{2,6},{3,7},{4,0},{5,1},{6,2},{7,3},{8,12},{9,13},{10,... | collective-permute-start | bytes 983048 | tf_op jit(solution)/shard_map/ppermute | solution.py:236
  493.0 26.7 %collective-permute-start.60 = (bf16[256,768]{1,0:T(8,128)(2,1)S(1)}, bf16[256,768]{1,0:T(8,128)(2,1)S(1)}, u32[]{:S(2)}, u32[]{:S(2)}) collective-permute-start(bf16[256,768]{1,0:T(8,128)(2,1)S(1)} %get-tuple-element.272), channel_id=1, source_target_pairs={{0,2},{1,3},{2,0},{3,1},{4,6},{5,7},{6,4},{7,5},{8,10},{9,11},{10,... | collective-permute-start | bytes 1179656 | tf_op jit(solution)/shard_map/ppermute | solution.py:236
  513.6 32.0 %collective-permute-start.50 = (bf16[392,1024]{1,0:T(8,128)(2,1)}, bf16[392,1024]{1,0:T(8,128)(2,1)}, u32[]{:S(2)}, u32[]{:S(2)}) collective-permute-start(bf16[392,1024]{1,0:T(8,128)(2,1)} %slice.406), channel_id=1, source_target_pairs={{0,16},{16,0},{8,24},{24,8},{1,17},{17,1},{9,25},{25,9},{2,18},{18... | collective-permute-start | bytes 2408456 | tf_op jit(solution)/shard_map/ppermute | solution.py:222
  519.1 22.5 %collective-permute-start.58 = (bf16[128,1280]{1,0:T(8,128)(2,1)S(1)}, bf16[128,1280]{1,0:T(8,128)(2,1)}, u32[]{:S(2)}, u32[]{:S(2)}) collective-permute-start(bf16[128,1280]{1,0:T(8,128)(2,1)S(1)} %add_convert_fusion.15), channel_id=1, source_target_pairs={{0,16},{16,0},{8,24},{24,8},{1,17},{17,1},{9,25},{25,9},{2,18},{18... | collective-permute-start | bytes 983048 | tf_op jit(solution)/shard_map/ppermute | solution.py:222
  (124 other events, 1226.8 us)

commit v3 on v2

--- a/solution.py
+++ b/solution.py
@@ -36,8 +36,8 @@
     return high, middle, rest - middle
 
 
-def block_rows(length):
-    for rows in (224, 112, 16):
+def block_rows(length, *sizes):
+    for rows in sizes + (224, 112, 16):
         if length % rows == 0:
             return rows
     return length
@@ -46,7 +46,7 @@
 def attend_kernel(q_ref, k_ref, v_ref, key_base_ref, *refs):
     context_ref, query_ref = refs[-2:]
     length = q_ref.shape[0]
-    rows = block_rows(length)
+    rows = block_rows(length, 392)
     low = lanes_of((length, PAIR)) < HEAD
     keys, values, key_base = k_ref[...], v_ref[...], key_base_ref[...]
     ones = jnp.ones((length, PAIR), BF16)
@@ -226,10 +226,13 @@
     return jnp.concatenate([values, swap_core(values)], axis=0)
 
 
-def sum_partner(partial_sums):
-    half = partial_sums.shape[0] // 2
-    received = swap_core(partial_sums[half:].astype(BF16))
-    return partial_sums[:half] + received.astype(F32)
+def sum_partner(pairs, dims):
+    half = pairs[0][0].shape[0] // 2
+    other = sum(dot(left[half:], right, dims) for left, right in pairs).astype(BF16)
+    received = swap_core(other)
+    own = [after(left[:half], other) for left, _ in pairs]
+    total = sum(dot(left, right, dims) for left, (_, right) in zip(own, pairs))
+    return total + received.astype(F32)
 
 
 def swap_group(values, bit):
@@ -237,26 +240,31 @@
 
 
 def order_kernel(count, *refs):
-    pieces, full_ref, sems = refs[:count], refs[count], refs[-1]
+    pieces, full_ref, held, arrived, sent = refs[:count], refs[count], *refs[-3:]
     group = lax.axis_index("fsdp")
     rows = full_ref.shape[0] // count
-    copies = []
-    for relative, piece in enumerate(pieces):
+    loads = [
+        pltpu.make_async_copy(piece, held.at[relative], arrived.at[relative])
+        for relative, piece in enumerate(pieces)
+    ]
+    for load in loads:
+        load.start()
+    stores = []
+    for relative in range(count):
         start = pl.multiple_of((group ^ relative) * rows, rows)
-        copies.append(
-            pltpu.make_async_copy(
-                piece.at[pl.ds(0, rows)], full_ref.at[pl.ds(start, rows)], sems.at[relative]
-            )
+        store = pltpu.make_async_copy(
+            held.at[relative, pl.ds(0, rows)], full_ref.at[pl.ds(start, rows)], sent.at[relative]
         )
-    for copy in copies:
-        copy.start()
-    if len(refs) > count + 2:
+        loads[relative].wait()
+        store.start()
+        stores.append(store)
+    if len(refs) > count + 4:
         own_width, core = 128, lax.rem(lax.axis_index("seq"), 2)
         wide_ref, bias_ref = refs[count + 1], refs[count + 2]
-        for relative, piece in enumerate(pieces):
+        for relative in range(count):
             place = group ^ relative
             columns = pl.ds(pl.multiple_of(place * own_width, own_width), own_width)
-            extra = piece[rows : rows + 8, :].astype(F32)
+            extra = held[relative, rows : rows + 8, :].astype(F32)
             lines = [
                 extra[k : k + 1, own_width * n : own_width * (n + 1)]
                 for k in range(2)
@@ -269,8 +277,8 @@
                 bias_ref[:, pl.ds(start, own_width)] = jnp.where(
                     core == 0, lines[8 + n], lines[10 + n]
                 )
-    for copy in copies:
-        copy.wait()
+    for store in stores:
+        store.wait()
 
 
 def in_order(pieces, rows, with_vectors=False):
@@ -282,14 +290,16 @@
         out_shape += [jax.ShapeDtypeStruct((8, 1024), F32), jax.ShapeDtypeStruct((1, 2048), F32)]
     result = pl.pallas_call(
         partial(order_kernel, count),
-        in_specs=[pl.BlockSpec(memory_space=pltpu.VMEM)] * count,
+        in_specs=[pl.BlockSpec(memory_space=pl.ANY)] * count,
         out_specs=out_specs,
         out_shape=out_shape,
-        scratch_shapes=[pltpu.SemaphoreType.DMA((count,))],
+        scratch_shapes=[
+            pltpu.VMEM((count,) + pieces[0].shape, pieces[0].dtype),
+            pltpu.SemaphoreType.DMA((count,)),
+            pltpu.SemaphoreType.DMA((count,)),
+        ],
         compiler_params=pltpu.CompilerParams(vmem_limit_bytes=16 * 2**20),
-        cost_estimate=pl.CostEstimate(
-            flops=0, bytes_accessed=4 * count * rows * columns, transcendentals=0
-        ),
+        cost_estimate=SMALL_COST,
         name="in_order",
     )(*pieces)
     return result if with_vectors else result[0]
@@ -501,8 +511,9 @@
     own_rows = clips * rows
     scale_factor = HEAD ** (-0.5)
 
-    def all_clips(values):
+    def all_clips(values, *ready):
         mine, back = values[:rows], swap_chip(values[rows:])
+        back = after(back, *ready)
         first = jnp.where(chip == 0, mine, back)
         second = jnp.where(chip == 0, back, mine)
         return jnp.stack([first, second])
@@ -606,10 +617,10 @@
     own_grads = jnp.concatenate([take(cotangent, chip), after(other_grads, queries[3])], axis=0)
     full_out = jnp.concatenate(in_core_order(kept, received, core, 1), axis=1)
     full_qkv = (qkv_first, second_columns[:, :row_width])
-    ready = (own_grads, queries[3]) + fc2_gather.got(4, 2)
+    ready = (own_grads, queries[3]) + fc2_gather.got(4, 2) + fc1_gather.got(7)
     all_context = after(context[3], *ready)
     fc2_gather.send(1, 3, 6, ready=ready)
-    attn_branch = sum_partner(dot(all_context, full_out)) + bias_out
+    attn_branch = sum_partner([(all_context, full_out)], NN) + bias_out
     residual_mid = own_inputs.astype(F32) + attn_branch
     normal_two, scale_two = normalize(residual_mid)
     h_two = with_partner((normal_two * gain_two + bias_two).astype(BF16))
@@ -634,7 +645,7 @@
         for part in (chip, 1 - chip)
     ]
     fc1_scatter = Scatter(fc1_product, halves=fc1_halves)
-    mlp_branch = sum_partner(dot(after(active, fc1_scatter.sent), full_fc2)) + bias_fc2
+    mlp_branch = sum_partner([(after(active, fc1_scatter.sent), full_fc2)], NN) + bias_fc2
     residual_out = residual_mid + mlp_branch
     counted = own_valid.astype(F32)[:, None]
     squares = jnp.stack(
@@ -646,7 +657,7 @@
         ]
     )
     low_output = residual_out.astype(BF16)
-    grad_h_two = sum_partner(dot(after(grad_hidden, residual_out), full_fc1, NT))
+    grad_h_two = sum_partner([(after(grad_hidden, residual_out), full_fc1)], NT)
     grad_residual = own_grads.astype(F32) + normalize_back(
         normal_two, scale_two, grad_h_two, gain_two
     )
@@ -679,7 +690,7 @@
     ready = (sums[0], fc1_scatter.crossed) + fc2_scatter.got("side")
     fc2_scatter.near(*ready)
     fc1_scatter.cross(*ready)
-    output = all_clips(after(low_output, *ready))
+    low_output = after(low_output, *ready)
     back_pair(1, grad_out, *ready, *fc2_scatter.got("keep"), *fc1_scatter.got("keep"))
     early = jnp.concatenate([dot(h_one, halves[0], TN).astype(BF16), grad_out], axis=1)
     ready = (sums[1],) + fc2_scatter.got("near_sums") + fc1_scatter.got("side")
@@ -688,7 +699,8 @@
     early_scatter = Scatter(early, *ready)
     ready += fc2_scatter.got("keep") + fc1_scatter.got("keep") + early_scatter.got("keep")
     back_pair(2, *ready)
-    ready = (sums[2], output) + fc2_scatter.got("far_sums") + fc1_scatter.got("near_sums")
+    output = all_clips(low_output, sums[2])
+    ready = (sums[2],) + fc2_scatter.got("far_sums") + fc1_scatter.got("near_sums")
     fc2_scatter.chips(*ready)
     fc1_scatter.far(*ready)
     back_pair(3, *ready, fc2_scatter.sums, *fc1_scatter.got("keep"))
@@ -700,12 +712,15 @@
     late_scatter = Scatter(dot(after(h_one, fc1_scatter.sums, *ready), halves[1], TN))
     ready = late_scatter.got("keep")
     grad_h_one = sum_partner(
-        dot(after(halves[0], *ready), full_qkv[0], NT) + dot(halves[1], full_qkv[1], NT)
+        [(after(halves[0], *ready), full_qkv[0]), (halves[1], full_qkv[1])], NT
     )
+    late_scatter.near()
+    grad_h_one = after(grad_h_one, *late_scatter.got("keep"))
     own_normal, own_scale = normalize(own_inputs.astype(F32))
-    input_grad = all_clips(
-        (grad_residual + normalize_back(own_normal, own_scale, grad_h_one, gain_one)).astype(BF16)
-    )
+    low_input_grad = (
+        grad_residual + normalize_back(own_normal, own_scale, grad_h_one, gain_one)
+    ).astype(BF16)
+    input_grad = all_clips(low_input_grad)
 
     def by_core(values):
         full = jnp.zeros((2, values.shape[0]), F32)
@@ -730,17 +745,17 @@
     by_group.append(jnp.broadcast_to(squares, (groups, 4)))
     by_group = jnp.concatenate(by_group, axis=1).astype(BF16)
     by_group = jnp.pad(by_group, ((0, 0), (0, 16 * PAIR - by_group.shape[1])))
+    by_group = after(by_group, *late_scatter.got("near_sums"))
     vector_scatter = Scatter(by_group.reshape(groups * 16, PAIR))
     ready = vector_scatter.got("keep")
-    late_scatter.near(*ready)
     early_scatter.far(*ready)
+    late_scatter.far(*ready)
     vector_scatter.near()
     fc1_scatter.cores(*ready)
-    late_scatter.far()
     vector_scatter.far()
     early_scatter.chips()
     vector_scatter.chips()
-    late_scatter.chips()
+    late_scatter.chips(input_grad)
     early_scatter.cores()
     vector_scatter.cores()
     late_scatter.cores()

time: 560 us -> 556 us (level)
  waiting for transfers between devices: 121 us -> 134 us
  other arithmetic: 79.8 us -> 67.3 us
  matrix products: 94.1 us -> 101 us
  starting transfers between devices: 72.9 us -> 66.5 us
    ppermute x43, waiting for transfers between devices: 92.1 us -> 109 us  [swap_group(): return lax.ppermute(values, 'fsdp', [(i, i ^ bit) for i in range(8)])]
    dot_general x15 -> x20, matrix products: 94.1 us -> 101 us  [dot(): return lax.dot_general(left, right, dims, preferred_element_type=F32)]
    pallas_call x4, Pallas kernels: 47.7 us -> 41.4 us  [attend(): pl.pallas_call(attend_kernel, grid=(1,), in_specs=in_specs, out_specs=[ti...]
    ppermute x43, starting transfers between devices: 58 us -> 52 us  [swap_group(): return lax.ppermute(values, 'fsdp', [(i, i ^ bit) for i in range(8)])]
    unnamed x190 -> x182, local copies, waits for them, and re-layouts: 19.6 us -> 16.6 us
    reduce_sum x5 -> x4, other arithmetic: 14.1 us -> 11.3 us  [column_sum(): return jnp.sum(values, axis=0, dtype=F32)]
  transfers between devices with their start and end apart: 68 -> 68, of which waited for: 31 -> 32; matrix products, arithmetic and copies ran while one was open for 22% -> 24% of each run, Pallas kernels for 23% -> 24%
where the time goes in v3:
time: 556 us; the launch traced here: 548 us
  waiting for transfers between devices  134 us (24%)
  Pallas kernels  133 us (24%)
  matrix products  101 us (18%)
  other arithmetic  67.3 us (12%)
  starting transfers between devices  66.5 us (12%)
  local copies, waits for them, and re-layouts  42.7 us (8%)
    ppermute x43, waiting for transfers between devices, swap_group(): return lax.ppermute(values, 'fsdp', [(i, i ^ bit) for i in range(8)])  109 us
    dot_general x20, matrix products, dot(): return lax.dot_general(left, right, dims, preferred_element_type=F32)  101 us
    pallas_call x4, Pallas kernels, attend_back(): pl.pallas_call(attend_back_kernel, grid=(1,), in_specs=in_specs, out_spec...  73.6 us
    ppermute x43, starting transfers between devices, swap_group(): return lax.ppermute(values, 'fsdp', [(i, i ^ bit) for i in range(8)])  52 us
    pallas_call x4, Pallas kernels, attend(): pl.pallas_call(attend_kernel, grid=(1,), in_specs=in_specs, out_specs=[ti...  41.4 us
    ppermute x10, waiting for transfers between devices, swap_chip(): return lax.ppermute(values, 'seq', [(0, 2), (2, 0), (1, 3), (3, 1)])  22.1 us
    convert_element_type x20, other arithmetic, add_low(): return (left.astype(F32) + right.astype(F32)).astype(BF16)  17.7 us
    unnamed x182, local copies, waits for them, and re-layouts  16.6 us
  transfers between devices with their start and end apart: 68, of which 32 were waited for; matrix products, arithmetic and copies ran while one was open for 24% of the time, Pallas kernels for 24%

profile of v3, /device:TPU:0, one launch (start us, length us, event | category | flops | bytes accessed | tf_op | source)
XLA Modules:
  0.0 547.9 jit_solution(6307555389289550257)
XLA Ops:
  43.5 4.4 in_order.4
  58.3 4.4 multiply_convert_fusion.3.q_ref.k_ref.v_ref
  66.2 10.1 %attend.4 = (bf16[1568,512]{1,0:T(8,128)(2,1)}, bf16[2,1568,128]{2,1,0:T(8,128)(2,1)}) custom-call(bf16[1568,768]{1,0:T(8,128)(2,1)} %multiply_convert_fusion.3.q_ref.k_ref.v_ref, bf16[1568,768]{1,0:T(8,128)(2,1)} %multiply_convert_fusion.3.q_ref.k_ref.v_ref, bf16[1568,768]{1,0:T(8,128)(2,1)} %multiply_convert_fusion.3.q_ref.k_ref.v_ref, ...), custom_call_target="tpu_custom_call" | custom-call | flops 10000000 | bytes 1048576 | tf_op jit(solution)/shard_map/attend/pallas_call | solution.py:89
  86.3 4.3 collective-permute-done.15.refs_7_
  104.9 10.0 %attend.5 = (bf16[1568,512]{1,0:T(8,128)(2,1)}, bf16[2,1568,128]{2,1,0:T(8,128)(2,1)}) custom-call(bf16[1568,768]{1,0:T(8,128)(2,1)} %multiply_convert_fusion.3.q_ref.k_ref.v_ref, bf16[1568,768]{1,0:T(8,128)(2,1)} %multiply_convert_fusion.3.q_ref.k_ref.v_ref, ...), custom_call_target="tpu_custom_call", output_to_operand_aliasing={{0}: (4, {})} | custom-call | flops 10000000 | bytes 1048576 | tf_op jit(solution)/shard_map/attend/pallas_call | solution.py:89
  120.1 10.6 %attend.6 = (bf16[1568,512]{1,0:T(8,128)(2,1)}, bf16[2,1568,128]{2,1,0:T(8,128)(2,1)}) custom-call(bf16[1568,768]{1,0:T(8,128)(2,1)} %multiply_convert_fusion.2.q_ref.k_ref.v_ref, bf16[1568,768]{1,0:T(8,128)(2,1)} %multiply_convert_fusion.2.q_ref.k_ref.v_ref, ...), custom_call_target="tpu_custom_call", output_to_operand_aliasing={{0}: (4, {})} | custom-call | flops 10000000 | bytes 1048576 | tf_op jit(solution)/shard_map/attend/pallas_call | solution.py:89
  130.8 10.9 %collective-permute-done.22.refs_5_ = bf16[128,2048]{1,0:T(8,128)(2,1)} collective-permute-done((bf16[128,2048]{1,0:T(8,128)(2,1)}, bf16[128,2048]{1,0:T(8,128)(2,1)}, u32[]{:S(2)}, u32[]{:S(2)}) %collective-permute-start.22) | collective-permute-done | bytes 524320 | tf_op jit(solution)/shard_map/ppermute | solution.py:239
  149.8 10.7 %attend.7 = (bf16[1568,512]{1,0:T(8,128)(2,1)}, bf16[2,1568,128]{2,1,0:T(8,128)(2,1)}) custom-call(bf16[1568,768]{1,0:T(8,128)(2,1)} %multiply_convert_fusion.2.q_ref.k_ref.v_ref, bf16[1568,768]{1,0:T(8,128)(2,1)} %multiply_convert_fusion.2.q_ref.k_ref.v_ref, ...), custom_call_target="tpu_custom_call", output_to_operand_aliasing={{0}: (4, {})} | custom-call | flops 10000000 | bytes 1048576 | tf_op jit(solution)/shard_map/attend/pallas_call | solution.py:89
  162.5 5.5 %collective-permute-done.24.refs_4_ = bf16[256,1024]{1,0:T(8,128)(2,1)S(1)} collective-permute-done((bf16[256,1024]{1,0:T(8,128)(2,1)S(1)}, bf16[256,1024]{1,0:T(8,128)(2,1)S(1)}, u32[]{:S(2)}, u32[]{:S(2)}) %collective-permute-start.24) | collective-permute-done | bytes 524320 | tf_op jit(solution)/shard_map/ppermute | solution.py:239
  174.0 4.3 fusion.57
  187.7 8.0 %collective-permute-done.29.refs_1_ = bf16[256,1024]{1,0:T(8,128)(2,1)} collective-permute-done((bf16[256,1024]{1,0:T(8,128)(2,1)S(1)}, bf16[256,1024]{1,0:T(8,128)(2,1)}, u32[]{:S(2)}, u32[]{:S(2)}) %collective-permute-start.29) | collective-permute-done | bytes 524320 | tf_op jit(solution)/shard_map/ppermute | solution.py:239
  195.6 10.7 %collective-permute-done.30.refs_3_ = bf16[256,1024]{1,0:T(8,128)(2,1)} collective-permute-done((bf16[256,1024]{1,0:T(8,128)(2,1)S(1)}, bf16[256,1024]{1,0:T(8,128)(2,1)}, u32[]{:S(2)}, u32[]{:S(2)}) %collective-permute-start.30) | collective-permute-done | bytes 524320 | tf_op jit(solution)/shard_map/ppermute | solution.py:239
  206.8 10.5 %multiply_convert_fusion.1 = (bf16[1568,2048]{1,0:T(8,128)(2,1)S(1)}, f32[1568,2048]{1,0:T(8,128)}) fusion(f32[2048]{0:T(1024)S(1)} %bitcast.149, bf16[1568,1024]{1,0:T(8,128)(2,1)S(1)} %pad_maximum_fusion.1, bf16[1024,2048]{1,0:T(8,128)(2,1)S(1)} %in_order.6), kind=kOutput, calls=%fused_computation.8 | convolution fusion | flops 6595936256 | bytes 26681344 | tf_op jit(solution)/shard_map/dot_general | solution.py:25
  220.2 8.3 %convolution_convert_fusion.1.full_ref = bf16[2048,1024]{1,0:T(8,128)(2,1)S(1)} fusion(bf16[1568,2048]{1,0:T(8,128)(2,1)S(1)} %get-tuple-element.172, bf16[1568,1024]{1,0:T(8,128)(2,1)S(1)} %constant_dynamic-update-slice_fusion), kind=kOutput, calls=%fused_computation.33 | convolution fusion | flops 6578765824 | bytes 13828096 | tf_op jit(solution)/shard_map/dot_general | solution.py:25
  234.0 13.4 %convert_reduce_fusion = (bf16[2048]{0:T(1024)(128)(2,1)S(1)}, bf16[1568,2048]{1,0:T(8,128)(2,1)S(1)}) fusion(f32[1568,2048]{1,0:T(8,128)} %get-tuple-element.341, f32[2048]{0:T(1024)S(1)} %bitcast.150, bf16[1568,1024]{1,0:T(8,128)(2,1)S(1)} %constant_dynamic-update-slice_fusion, bf16[2048,1024]{1,0:T(8,128)(2,1)S(1)} %in_order.7), kind=kOutput, calls=%fused_computation.6 | convolution fusion | flops 6624835584 | bytes 26685440 | tf_op jit(solution)/shard_map/dot_general | solution.py:25
  247.3 8.6 %convolution_convert_fusion = bf16[1024,2048]{1,0:T(8,128)(2,1)S(1)} fusion(bf16[1568,1024]{1,0:T(8,128)(2,1)S(1)} %pad_maximum_fusion.1, bf16[1568,2048]{1,0:T(8,128)(2,1)S(1)} %get-tuple-element.174), kind=kOutput, calls=%fused_computation.32 | convolution fusion | flops 6578765824 | bytes 13828096 | tf_op jit(solution)/shard_map/dot_general | solution.py:25
  257.7 5.8 %fusion.32 = bf16[784,1024]{1,0:T(8,128)(2,1)S(1)} fusion(bf16[2048,1024]{1,0:T(8,128)(2,1)S(1)} %in_order.7, bf16[1568,2048]{1,0:T(8,128)(2,1)} %copy-done.54), kind=kOutput, calls=%fused_computation.71 | convolution fusion | flops 3289137152 | bytes 9011200 | tf_op jit(solution)/shard_map/dot_general | solution.py:25
  267.0 7.8 %fusion.23 = (bf16[]{:T(256)}, bf16[]{:T(256)}, bf16[]{:T(256)}, bf16[784,1024]{1,0:T(8,128)(2,1)}) fusion(f32[784]{0:T(1024)S(1)} %add_convert_fusion.32, f32[1024]{0:T(1024)S(1)} %bitcast.189, f32[784,1024]{1,0:T(8,128)} %get-tuple-element.339, bf16[784,1024]{1,0:T(8,128)(2,1)S(1)} %copy-done.83, f32[1024]{0:T(1024)S(1)} %bitcast.187, ...), kind=kOutput, calls=%fused_computation.41 | convolution fusion | flops 3301982208 | bytes 18656326 | tf_op jit(solution)/shard_map/dot_general | solution.py:25
  281.9 5.0 multiply_reduce_fusion
  286.9 4.4 fusion.56
  296.3 5.1 convolution_convert_fusion.2.grad_ref
  301.3 18.4 %attend_back.4 = (bf16[1568,768]{1,0:T(8,128)(2,1)}, f32[2,128]{1,0:T(2,128)}) custom-call(bf16[2,1568,128]{2,1,0:T(8,128)(2,1)} %get-tuple-element.135.query_ref, bf16[1568,768]{1,0:T(8,128)(2,1)} %multiply_convert_fusion.3.q_ref.k_ref.v_ref, bf16[1568,768]{1,0:T(8,128)(2,1)} %multiply_convert_fusion.3.q_ref.k_ref.v_ref, ...), custom_call_target="tpu_custom_call" | custom-call | flops 10000000 | bytes 1048576 | tf_op jit(solution)/shard_map/attend_back/pallas_call | solution.py:174
  319.7 7.0 %collective-permute-done.39 = bf16[1024,1024]{1,0:T(8,128)(2,1)} collective-permute-done((bf16[1024,1024]{1,0:T(8,128)(2,1)}, bf16[1024,1024]{1,0:T(8,128)(2,1)}, u32[]{:S(2)}, u32[]{:S(2)}) %collective-permute-start.39) | collective-permute-done | bytes 2097184 | tf_op jit(solution)/shard_map/ppermute | solution.py:239
  340.2 18.6 %attend_back.5 = (bf16[1568,768]{1,0:T(8,128)(2,1)}, f32[2,128]{1,0:T(2,128)}) custom-call(bf16[2,1568,128]{2,1,0:T(8,128)(2,1)} %get-tuple-element.139.query_ref, bf16[1568,768]{1,0:T(8,128)(2,1)} %multiply_convert_fusion.3.q_ref.k_ref.v_ref, bf16[1568,768]{1,0:T(8,128)(2,1)} %multiply_convert_fusion.3.q_ref.k_ref.v_ref, ...), custom_call_target="tpu_custom_call", output_to_operand_aliasing={{0}: (6, {})} | custom-call | flops 10000000 | bytes 1048576 | tf_op jit(solution)/shard_map/attend_back/pallas_call | solution.py:174
  358.8 4.9 convolution_convert_fusion.5
  376.8 18.2 %attend_back.6 = (bf16[1568,768]{1,0:T(8,128)(2,1)}, f32[2,128]{1,0:T(2,128)}) custom-call(bf16[2,1568,128]{2,1,0:T(8,128)(2,1)} %get-tuple-element.145.query_ref, bf16[1568,768]{1,0:T(8,128)(2,1)} %multiply_convert_fusion.2.q_ref.k_ref.v_ref, bf16[1568,768]{1,0:T(8,128)(2,1)} %multiply_convert_fusion.2.q_ref.k_ref.v_ref, ...), custom_call_target="tpu_custom_call" | custom-call | flops 10000000 | bytes 1048576 | tf_op jit(solution)/shard_map/attend_back/pallas_call | solution.py:174
  401.7 18.5 %attend_back.7 = (bf16[1568,768]{1,0:T(8,128)(2,1)}, f32[2,128]{1,0:T(2,128)}) custom-call(bf16[2,1568,128]{2,1,0:T(8,128)(2,1)} %get-tuple-element.154.query_ref, bf16[1568,768]{1,0:T(8,128)(2,1)} %multiply_convert_fusion.2.q_ref.k_ref.v_ref, bf16[1568,768]{1,0:T(8,128)(2,1)} %multiply_convert_fusion.2.q_ref.k_ref.v_ref, ...), custom_call_target="tpu_custom_call", output_to_operand_aliasing={{0}: (6, {})} | custom-call | flops 10000000 | bytes 1048576 | tf_op jit(solution)/shard_map/attend_back/pallas_call | solution.py:174
  426.8 6.4 %collective-permute-done.46 = bf16[128,1024]{1,0:T(8,128)(2,1)S(1)} collective-permute-done((bf16[128,1024]{1,0:T(8,128)(2,1)S(1)}, bf16[128,1024]{1,0:T(8,128)(2,1)S(1)}, u32[]{:S(2)}, u32[]{:S(2)}) %collective-permute-start.46) | collective-permute-done | bytes 262176 | tf_op jit(solution)/shard_map/ppermute | solution.py:239
  452.5 5.2 collective-permute-done.50
  464.9 9.9 %collective-permute-done.52 = bf16[256,768]{1,0:T(8,128)(2,1)} collective-permute-done((bf16[256,768]{1,0:T(8,128)(2,1)S(1)}, bf16[256,768]{1,0:T(8,128)(2,1)}, u32[]{:S(2)}, u32[]{:S(2)}) %collective-permute-start.52) | collective-permute-done | bytes 393248 | tf_op jit(solution)/shard_map/ppermute | solution.py:239
  488.9 14.5 %collective-permute-done.55 = bf16[16,128]{1,0:T(8,128)(2,1)S(1)} collective-permute-done((bf16[16,128]{1,0:T(8,128)(2,1)S(1)}, bf16[16,128]{1,0:T(8,128)(2,1)S(1)}, u32[]{:S(2)}, u32[]{:S(2)}) %collective-permute-start.55) | collective-permute-done | bytes 4128 | tf_op jit(solution)/shard_map/ppermute | solution.py:239
  517.3 14.1 %collective-permute-done.51 = bf16[392,1024]{1,0:T(8,128)(2,1)S(1)} collective-permute-done((bf16[392,1024]{1,0:T(8,128)(2,1)S(1)}, bf16[392,1024]{1,0:T(8,128)(2,1)S(1)}, u32[]{:S(2)}, u32[]{:S(2)}) %collective-permute-start.51) | collective-permute-done | bytes 802848 | tf_op jit(solution)/shard_map/ppermute | solution.py:222
  (457 shorter events, 246.7 us)
Async XLA Ops:
  5.6 27.2 %collective-permute-start = (bf16[392,1024]{1,0:T(8,128)(2,1)}, bf16[392,1024]{1,0:T(8,128)(2,1)}, u32[]{:S(2)}, u32[]{:S(2)}) collective-permute-start(bf16[392,1024]{1,0:T(8,128)(2,1)} %get-tuple-element.119), channel_id=1, source_target_pairs={{0,16},{16,0},{8,24},{24,8},{1,17},{17,1},{9,25},{25,9},{2,18},{18... | collective-permute-start | bytes 2408456 | tf_op jit(solution)/shard_map/ppermute | solution.py:222
  37.5 25.2 %collective-permute-start.11 = (bf16[128,1280]{1,0:T(8,128)(2,1)S(1)}, bf16[128,1280]{1,0:T(8,128)(2,1)S(1)}, u32[]{:S(2)}, u32[]{:S(2)}) collective-permute-start(bf16[128,1280]{1,0:T(8,128)(2,1)S(1)} %copy-done.13), channel_id=1, source_target_pairs={{0,4},{1,5},{2,6},{3,7},{4,0},{5,1},{6,2},{7,3},{8,12},{9,13},{10,... | collective-permute-start | bytes 983048 | tf_op jit(solution)/shard_map/ppermute | solution.py:239
  40.8 21.9 %collective-permute-start.10 = (bf16[128,1280]{1,0:T(8,128)(2,1)S(1)}, bf16[128,1280]{1,0:T(8,128)(2,1)S(1)}, u32[]{:S(2)}, u32[]{:S(2)}) collective-permute-start(bf16[128,1280]{1,0:T(8,128)(2,1)S(1)} %copy-done.13), channel_id=1, source_target_pairs={{0,2},{1,3},{2,0},{3,1},{4,6},{5,7},{6,4},{7,5},{8,10},{9,11},{10,... | collective-permute-start | bytes 983048 | tf_op jit(solution)/shard_map/ppermute | solution.py:239
  41.1 21.6 %collective-permute-start.9 = (bf16[128,1280]{1,0:T(8,128)(2,1)S(1)}, bf16[128,1280]{1,0:T(8,128)(2,1)S(1)}, u32[]{:S(2)}, u32[]{:S(2)}) collective-permute-start(bf16[128,1280]{1,0:T(8,128)(2,1)S(1)} %copy-done.13), channel_id=1, source_target_pairs={{0,1},{1,0},{2,3},{3,2},{4,5},{5,4},{6,7},{7,6},{8,9},{9,8},{10,11... | collective-permute-start | bytes 983048 | tf_op jit(solution)/shard_map/ppermute | solution.py:239
  82.2 32.7 %collective-permute-start.16 = (bf16[128,2048]{1,0:T(8,128)(2,1)S(1)}, bf16[128,2048]{1,0:T(8,128)(2,1)}, u32[]{:S(2)}, u32[]{:S(2)}) collective-permute-start(bf16[128,2048]{1,0:T(8,128)(2,1)S(1)} %bitcast.145), channel_id=1, source_target_pairs={{0,4},{1,5},{2,6},{3,7},{4,0},{5,1},{6,2},{7,3},{8,12},{9,13},{10,... | collective-permute-start | bytes 1572872 | tf_op jit(solution)/shard_map/ppermute | solution.py:239
  85.4 29.5 %collective-permute-start.17 = (bf16[128,2048]{1,0:T(8,128)(2,1)S(1)}, bf16[128,2048]{1,0:T(8,128)(2,1)}, u32[]{:S(2)}, u32[]{:S(2)}) collective-permute-start(bf16[128,2048]{1,0:T(8,128)(2,1)S(1)} %bitcast.146), channel_id=1, source_target_pairs={{0,2},{1,3},{2,0},{3,1},{4,6},{5,7},{6,4},{7,5},{8,10},{9,11},{10,... | collective-permute-start | bytes 1572872 | tf_op jit(solution)/shard_map/ppermute | solution.py:239
  85.8 29.1 %collective-permute-start.18 = (bf16[128,2048]{1,0:T(8,128)(2,1)S(1)}, bf16[128,2048]{1,0:T(8,128)(2,1)S(1)}, u32[]{:S(2)}, u32[]{:S(2)}) collective-permute-start(bf16[128,2048]{1,0:T(8,128)(2,1)S(1)} %bitcast.147), channel_id=1, source_target_pairs={{0,1},{1,0},{2,3},{3,2},{4,5},{5,4},{6,7},{7,6},{8,9},{9,8},{10,11... | collective-permute-start | bytes 1572872 | tf_op jit(solution)/shard_map/ppermute | solution.py:239
  117.4 24.2 %collective-permute-start.22 = (bf16[128,2048]{1,0:T(8,128)(2,1)}, bf16[128,2048]{1,0:T(8,128)(2,1)}, u32[]{:S(2)}, u32[]{:S(2)}) collective-permute-start(bf16[128,2048]{1,0:T(8,128)(2,1)} %collective-permute-done.16.refs_4_), channel_id=1, source_target_pairs={{0,1},{1,0},{2,3},{3,2},{4,5},{5,4},{6,7},{7,6},{8,9},{9,8},{10,11... | collective-permute-start | bytes 1572872 | tf_op jit(solution)/shard_map/ppermute | solution.py:239
  141.6 19.5 %collective-permute-start.23 = (bf16[392,1024]{1,0:T(8,128)(2,1)S(1)}, bf16[392,1024]{1,0:T(8,128)(2,1)S(1)}, u32[]{:S(2)}, u32[]{:S(2)}) collective-permute-start(bf16[392,1024]{1,0:T(8,128)(2,1)S(1)} %get-tuple-element.153), channel_id=1, source_target_pairs={{0,16},{16,0},{8,24},{24,8},{1,17},{17,1},{9,25},{25,9},{2,18},{18... | collective-permute-start | bytes 2408456 | tf_op jit(solution)/shard_map/ppermute | solution.py:222
  142.1 25.9 %collective-permute-start.24 = (bf16[256,1024]{1,0:T(8,128)(2,1)S(1)}, bf16[256,1024]{1,0:T(8,128)(2,1)S(1)}, u32[]{:S(2)}, u32[]{:S(2)}) collective-permute-start(bf16[256,1024]{1,0:T(8,128)(2,1)S(1)} %copy-done.4), channel_id=1, source_target_pairs={{0,4},{1,5},{2,6},{3,7},{4,0},{5,1},{6,2},{7,3},{8,12},{9,13},{10,... | collective-permute-start | bytes 1572872 | tf_op jit(solution)/shard_map/ppermute | solution.py:239
  145.5 22.6 %collective-permute-start.26 = (bf16[128,2048]{1,0:T(8,128)(2,1)}, bf16[128,2048]{1,0:T(8,128)(2,1)S(1)}, u32[]{:S(2)}, u32[]{:S(2)}) collective-permute-start(bf16[128,2048]{1,0:T(8,128)(2,1)} %collective-permute-done.20.refs_6_), channel_id=1, source_target_pairs={{0,1},{1,0},{2,3},{3,2},{4,5},{5,4},{6,7},{7,6},{8,9},{9,8},{10,11... | collective-permute-start | bytes 1572872 | tf_op jit(solution)/shard_map/ppermute | solution.py:239
  147.0 22.4 %collective-permute-start.25 = (bf16[256,1024]{1,0:T(8,128)(2,1)S(1)}, bf16[256,1024]{1,0:T(8,128)(2,1)S(1)}, u32[]{:S(2)}, u32[]{:S(2)}) collective-permute-start(bf16[256,1024]{1,0:T(8,128)(2,1)S(1)} %copy-done.4), channel_id=1, source_target_pairs={{0,2},{1,3},{2,0},{3,1},{4,6},{5,7},{6,4},{7,5},{8,10},{9,11},{10,... | collective-permute-start | bytes 1572872 | tf_op jit(solution)/shard_map/ppermute | solution.py:239
  181.3 25.0 %collective-permute-start.30 = (bf16[256,1024]{1,0:T(8,128)(2,1)S(1)}, bf16[256,1024]{1,0:T(8,128)(2,1)}, u32[]{:S(2)}, u32[]{:S(2)}) collective-permute-start(bf16[256,1024]{1,0:T(8,128)(2,1)S(1)} %collective-permute-done.25.refs_2_), channel_id=1, source_target_pairs={{0,1},{1,0},{2,3},{3,2},{4,5},{5,4},{6,7},{7,6},{8,9},{9,8},{10,11... | collective-permute-start | bytes 1572872 | tf_op jit(solution)/shard_map/ppermute | solution.py:239
  182.8 23.5 %collective-permute-start.31 = (bf16[256,1024]{1,0:T(8,128)(2,1)S(1)}, bf16[256,1024]{1,0:T(8,128)(2,1)}, u32[]{:S(2)}, u32[]{:S(2)}) collective-permute-start(bf16[256,1024]{1,0:T(8,128)(2,1)S(1)} %collective-permute-done.24.refs_4_), channel_id=1, source_target_pairs={{0,2},{1,3},{2,0},{3,1},{4,6},{5,7},{6,4},{7,5},{8,10},{9,11},{10,... | collective-permute-start | bytes 1572872 | tf_op jit(solution)/shard_map/ppermute | solution.py:239
  185.3 32.0 %collective-permute-start.33 = (bf16[784,1024]{1,0:T(8,128)(2,1)S(1)}, bf16[784,1024]{1,0:T(8,128)(2,1)S(1)}, u32[]{:S(2)}, u32[]{:S(2)}) collective-permute-start(bf16[784,1024]{1,0:T(8,128)(2,1)S(1)} %copy-done.45), channel_id=1, source_target_pairs={{0,8},{8,0},{16,24},{24,16},{1,9},{9,1},{17,25},{25,17},{2,10},{10... | collective-permute-start | bytes 4816904 | tf_op jit(solution)/shard_map/ppermute | solution.py:218
  278.8 47.9 %collective-permute-start.39 = (bf16[1024,1024]{1,0:T(8,128)(2,1)}, bf16[1024,1024]{1,0:T(8,128)(2,1)}, u32[]{:S(2)}, u32[]{:S(2)}) collective-permute-start(bf16[1024,1024]{1,0:T(8,128)(2,1)} %get-tuple-element.178), channel_id=1, source_target_pairs={{0,1},{1,0},{2,3},{3,2},{4,5},{5,4},{6,7},{7,6},{8,9},{9,8},{10,11... | collective-permute-start | bytes 6291464 | tf_op jit(solution)/shard_map/ppermute | solution.py:239
  279.3 47.6 %collective-permute-start.38 = (bf16[1024,1024]{1,0:T(8,128)(2,1)}, bf16[1024,1024]{1,0:T(8,128)(2,1)}, u32[]{:S(2)}, u32[]{:S(2)}) collective-permute-start(bf16[1024,1024]{1,0:T(8,128)(2,1)} %constant_dynamic-slice_fusion.1), channel_id=1, source_target_pairs={{0,16},{16,0},{8,24},{24,8},{1,17},{17,1},{9,25},{25,9},{2,18},{18... | collective-permute-start | bytes 6291464 | tf_op jit(solution)/shard_map/ppermute | solution.py:222
  338.4 27.0 %collective-permute-start.41 = (bf16[512,512]{1,0:T(8,128)(2,1)}, bf16[512,512]{1,0:T(8,128)(2,1)}, u32[]{:S(2)}, u32[]{:S(2)}) collective-permute-start(bf16[512,512]{1,0:T(8,128)(2,1)} %constant_dynamic-slice_fusion), channel_id=1, source_target_pairs={{0,8},{8,0},{16,24},{24,16},{1,9},{9,1},{17,25},{25,17},{2,10},{10... | collective-permute-start | bytes 1572872 | tf_op jit(solution)/shard_map/ppermute | solution.py:218
  338.4 31.3 %collective-permute-start.43 = (bf16[512,1024]{1,0:T(8,128)(2,1)S(1)}, bf16[512,1024]{1,0:T(8,128)(2,1)}, u32[]{:S(2)}, u32[]{:S(2)}) collective-permute-start(bf16[512,1024]{1,0:T(8,128)(2,1)S(1)} %get-tuple-element.187), channel_id=1, source_target_pairs={{0,1},{1,0},{2,3},{3,2},{4,5},{5,4},{6,7},{7,6},{8,9},{9,8},{10,11... | collective-permute-start | bytes 3145736 | tf_op jit(solution)/shard_map/ppermute | solution.py:239
  339.9 29.8 %collective-permute-start.42 = (bf16[512,1024]{1,0:T(8,128)(2,1)}, bf16[512,1024]{1,0:T(8,128)(2,1)}, u32[]{:S(2)}, u32[]{:S(2)}) collective-permute-start(bf16[512,1024]{1,0:T(8,128)(2,1)} %get-tuple-element.271), channel_id=1, source_target_pairs={{0,2},{1,3},{2,0},{3,1},{4,6},{5,7},{6,4},{7,5},{8,10},{9,11},{10,... | collective-permute-start | bytes 3145736 | tf_op jit(solution)/shard_map/ppermute | solution.py:239
  363.8 31.3 %collective-permute-start.40 = (bf16[392,1024]{1,0:T(8,128)(2,1)S(1)}, bf16[392,1024]{1,0:T(8,128)(2,1)S(1)}, u32[]{:S(2)}, u32[]{:S(2)}) collective-permute-start(bf16[392,1024]{1,0:T(8,128)(2,1)S(1)} %slice.315), channel_id=1, source_target_pairs={{0,16},{16,0},{8,24},{24,8},{1,17},{17,1},{9,25},{25,9},{2,18},{18... | collective-permute-start | bytes 2408456 | tf_op jit(solution)/shard_map/ppermute | solution.py:222
  372.9 24.8 %collective-permute-start.44 = (bf16[256,1024]{1,0:T(8,128)(2,1)S(1)}, bf16[256,1024]{1,0:T(8,128)(2,1)S(1)}, u32[]{:S(2)}, u32[]{:S(2)}) collective-permute-start(bf16[256,1024]{1,0:T(8,128)(2,1)S(1)} %get-tuple-element.279), channel_id=1, source_target_pairs={{0,2},{1,3},{2,0},{3,1},{4,6},{5,7},{6,4},{7,5},{8,10},{9,11},{10,... | collective-permute-start | bytes 1572872 | tf_op jit(solution)/shard_map/ppermute | solution.py:239
  374.7 25.4 %collective-permute-start.45 = (bf16[256,1024]{1,0:T(8,128)(2,1)S(1)}, bf16[256,1024]{1,0:T(8,128)(2,1)S(1)}, u32[]{:S(2)}, u32[]{:S(2)}) collective-permute-start(bf16[256,1024]{1,0:T(8,128)(2,1)S(1)} %get-tuple-element.281), channel_id=1, source_target_pairs={{0,4},{1,5},{2,6},{3,7},{4,0},{5,1},{6,2},{7,3},{8,12},{9,13},{10,... | collective-permute-start | bytes 1572872 | tf_op jit(solution)/shard_map/ppermute | solution.py:239
  375.8 57.3 %collective-permute-start.48 = (bf16[512,1280]{1,0:T(8,128)(2,1)}, bf16[512,1280]{1,0:T(8,128)(2,1)}, u32[]{:S(2)}, u32[]{:S(2)}) collective-permute-start(bf16[512,1280]{1,0:T(8,128)(2,1)} %get-tuple-element.201), channel_id=1, source_target_pairs={{0,1},{1,0},{2,3},{3,2},{4,5},{5,4},{6,7},{7,6},{8,9},{9,8},{10,11... | collective-permute-start | bytes 3932168 | tf_op jit(solution)/shard_map/ppermute | solution.py:239
  400.2 32.9 %collective-permute-start.47 = (bf16[256,1024]{1,0:T(8,128)(2,1)S(1)}, bf16[256,1024]{1,0:T(8,128)(2,1)}, u32[]{:S(2)}, u32[]{:S(2)}) collective-permute-start(bf16[256,1024]{1,0:T(8,128)(2,1)S(1)} %add_convert_fusion.8), channel_id=1, source_target_pairs={{0,16},{16,0},{8,24},{24,8},{1,17},{17,1},{9,25},{25,9},{2,18},{18... | collective-permute-start | bytes 1572872 | tf_op jit(solution)/shard_map/ppermute | solution.py:222
  433.2 42.2 %collective-permute-start.65 = (bf16[128,1024]{1,0:T(8,128)(2,1)S(1)}, bf16[128,1024]{1,0:T(8,128)(2,1)}, u32[]{:S(2)}, u32[]{:S(2)}) collective-permute-start(bf16[128,1024]{1,0:T(8,128)(2,1)S(1)} %add_convert_fusion.19), channel_id=1, source_target_pairs={{0,16},{16,0},{8,24},{24,8},{1,17},{17,1},{9,25},{25,9},{2,18},{18... | collective-permute-start | bytes 786440 | tf_op jit(solution)/shard_map/ppermute | solution.py:222
  449.3 27.6 %collective-permute-start.58 = (bf16[256,1280]{1,0:T(8,128)(2,1)}, bf16[256,1280]{1,0:T(8,128)(2,1)S(1)}, u32[]{:S(2)}, u32[]{:S(2)}) collective-permute-start(bf16[256,1280]{1,0:T(8,128)(2,1)} %get-tuple-element.273), channel_id=1, source_target_pairs={{0,2},{1,3},{2,0},{3,1},{4,6},{5,7},{6,4},{7,5},{8,10},{9,11},{10,... | collective-permute-start | bytes 1966088 | tf_op jit(solution)/shard_map/ppermute | solution.py:239
  476.8 40.0 %collective-permute-start.66 = (bf16[128,2048]{1,0:T(8,128)(2,1)S(1)}, bf16[128,2048]{1,0:T(8,128)(2,1)S(1)}, u32[]{:S(2)}, u32[]{:S(2)}) collective-permute-start(bf16[128,2048]{1,0:T(8,128)(2,1)S(1)} %pad_maximum_fusion.12), channel_id=1, source_target_pairs={{0,8},{8,0},{16,24},{24,16},{1,9},{9,1},{17,25},{25,17},{2,10},{10... | collective-permute-start | bytes 1572872 | tf_op jit(solution)/shard_map/ppermute | solution.py:218
  477.0 37.1 %collective-permute-start.59 = (bf16[128,1280]{1,0:T(8,128)(2,1)S(1)}, bf16[128,1280]{1,0:T(8,128)(2,1)S(1)}, u32[]{:S(2)}, u32[]{:S(2)}) collective-permute-start(bf16[128,1280]{1,0:T(8,128)(2,1)S(1)} %add_convert_fusion.17), channel_id=1, source_target_pairs={{0,4},{1,5},{2,6},{3,7},{4,0},{5,1},{6,2},{7,3},{8,12},{9,13},{10,... | collective-permute-start | bytes 983048 | tf_op jit(solution)/shard_map/ppermute | solution.py:239
  481.1 51.6 %collective-permute-start.61 = (bf16[128,768]{1,0:T(8,128)(2,1)S(1)}, bf16[128,768]{1,0:T(8,128)(2,1)S(1)}, u32[]{:S(2)}, u32[]{:S(2)}) collective-permute-start(bf16[128,768]{1,0:T(8,128)(2,1)S(1)} %add_convert_fusion.24), channel_id=1, source_target_pairs={{0,4},{1,5},{2,6},{3,7},{4,0},{5,1},{6,2},{7,3},{8,12},{9,13},{10,... | collective-permute-start | bytes 589832 | tf_op jit(solution)/shard_map/ppermute | solution.py:239
  510.6 20.8 %collective-permute-start.51 = (bf16[392,1024]{1,0:T(8,128)(2,1)S(1)}, bf16[392,1024]{1,0:T(8,128)(2,1)S(1)}, u32[]{:S(2)}, u32[]{:S(2)}) collective-permute-start(bf16[392,1024]{1,0:T(8,128)(2,1)S(1)} %slice.403), channel_id=1, source_target_pairs={{0,16},{16,0},{8,24},{24,8},{1,17},{17,1},{9,25},{25,9},{2,18},{18... | collective-permute-start | bytes 2408456 | tf_op jit(solution)/shard_map/ppermute | solution.py:222
  515.2 23.2 %collective-permute-start.60 = (bf16[128,1280]{1,0:T(8,128)(2,1)S(1)}, bf16[128,1280]{1,0:T(8,128)(2,1)S(1)}, u32[]{:S(2)}, u32[]{:S(2)}) collective-permute-start(bf16[128,1280]{1,0:T(8,128)(2,1)S(1)} %add_convert_fusion.16), channel_id=1, source_target_pairs={{0,16},{16,0},{8,24},{24,8},{1,17},{17,1},{9,25},{25,9},{2,18},{18... | collective-permute-start | bytes 983048 | tf_op jit(solution)/shard_map/ppermute | solution.py:222
  (120 other events, 1149.1 us)

commit v4 on v3

--- a/solution.py
+++ b/solution.py
@@ -12,7 +12,7 @@
 PAIR = 2 * HEAD
 EPS = 1e-06
 MASKED = -1e30
-VMEM_BYTES = 56 * 2**20
+VMEM_BYTES = 28 * 2**20
 BF16 = jnp.bfloat16
 F32 = jnp.float32
 NN = (((1,), (0,)), ((), ()))
@@ -410,8 +410,45 @@
     )(values)
 
 
+def pack_kernel(*refs):
+    line_refs, sum_refs, squares_ref, packed_ref = refs[:7], refs[7:11], refs[11], refs[12]
+    group = lax.axis_index("fsdp")
+    core = lax.rem(lax.axis_index("seq"), 2)
+    for n in range(8):
+        far, near, side = n % 2, (n // 2) % 2, n // 4
+        target = group ^ (4 * far + 2 * near + side)
+        columns = pl.ds(pl.multiple_of(target * PAIR, PAIR), PAIR)
+        mine = (target // 4) == core
+        pair = lax.rem(target, 4)
+        head_sums = jnp.zeros((2, PAIR), F32)
+        for k in range(4):
+            head_sums = jnp.where(jnp.logical_and(mine, pair == k), sum_refs[k][...], head_sums)
+        rows = [ref[:, columns] for ref in line_refs[:6]]
+        rows = rows[:2] + [head_sums] + rows[2:]
+        hidden = [
+            line_refs[6][:, pl.ds(pl.multiple_of(target * 2 * PAIR + k * PAIR, PAIR), PAIR)]
+            for k in range(2)
+        ]
+        empty = jnp.zeros((1, PAIR), F32)
+        rows += [jnp.where(core == 0, part, empty) for part in hidden]
+        rows += [jnp.where(core == 0, empty, part) for part in hidden]
+        rows.append(squares_ref[...])
+        packed_ref[16 * n : 16 * (n + 1), :] = jnp.concatenate(rows, axis=0).astype(BF16)
+
+
+def pack_lines(lines, sums, squares):
+    return pl.pallas_call(
+        pack_kernel,
+        in_specs=[pl.BlockSpec(memory_space=pltpu.VMEM)] * 12,
+        out_specs=pl.BlockSpec(memory_space=pltpu.VMEM),
+        out_shape=jax.ShapeDtypeStruct((128, PAIR), BF16),
+        cost_estimate=SMALL_COST,
+        name="pack_lines",
+    )(*lines, *sums, squares)
+
+
 class Scatter:
-    def __init__(self, values, *ready, halves=None):
+    def __init__(self, values, *ready, halves=None, ordered=False):
         self.grouped = lax.axis_size("fsdp") == 8
         self.halved = halves is not None
         values = values.astype(BF16)
@@ -419,7 +456,9 @@
             self.kept, self.sent = halves
             self.crossed = swap_chip(self.sent)
         elif self.grouped:
-            self.keep, self.side_send = split_blocks(values)
+            middle = values.shape[0] // 2
+            split = (values[:middle], values[middle:]) if ordered else split_blocks(values)
+            self.keep, self.side_send = split
             self.side = swap_group(after(self.side_send, *ready), 1)
         else:
             self.sums = lax.psum_scatter(values, "fsdp", scatter_dimension=0, tiled=True)
@@ -465,11 +504,10 @@
             self.total = add_low(self.sums, other_chip)
         self.other_core = swap_core(self.total)
 
-    def finish(self):
-        self.near()
-        self.far()
-        self.chips()
-        self.cores()
+    def last(self):
+        if not self.grouped:
+            return self.sums.astype(F32)
+        return self.keep.astype(F32) + self.far_sums.astype(F32)
 
 
 def take(values, index):
@@ -533,6 +571,7 @@
         own_first = by_head[:, 0]
         own_second = jnp.concatenate([by_head[:, 1], out_columns], axis=1)
 
+    fc1_weight, fc2_weight = lax.optimization_barrier((fc1_weight, fc2_weight, own_first))[:2]
     own_fc1 = lax.dynamic_index_in_dim(
         fc1_weight.reshape(own_width, groups, 2, half_rows), core, 2, keepdims=False
     ).reshape(own_width, groups * half_rows)
@@ -541,7 +580,7 @@
     qkv_a, qkv_b = Gather(own_first), Gather(own_second)
     fc1_gather, fc2_gather = Gather(own_fc1), Gather(own_fc2)
     qkv_a.send(4, 2, 1)
-    other_inputs = swap_chip(after(take(inputs, 1 - chip), own_first))
+    other_inputs = swap_chip(take(after(inputs, own_fc1), 1 - chip))
     qkv_a.send(6, 3, 5, ready=qkv_a.got(4, 2, 1) + (own_fc1, own_fc2))
     qkv_b.send(4, ready=qkv_a.got(4, 2, 1))
     qkv_a.send(7, ready=qkv_a.got(6, 3, 5))
@@ -596,42 +635,41 @@
     qkv_b.send(6, 3, 5, ready=ready)
     fc1_gather.send(4, ready=ready)
     attend_pair(0, *ready)
-    ready = (queries[0],) + qkv_b.got(6, 3, 5)
+    ready = (queries[0],) + qkv_b.got(6, 3, 5) + fc1_gather.got(4)
     qkv_b.send(7, ready=ready)
-    fc1_gather.send(2, 1, ready=ready)
+    fc1_gather.send(2, 1, 6, 5, ready=ready)
     attend_pair(1, *ready)
     second_columns = qkv_b.result()
     mixed.append(project(second_columns[:, :row_width], 1))
-    ready = (queries[1], mixed[1]) + fc1_gather.got(4, 2, 1)
-    fc1_gather.send(6, 3, 5, ready=ready)
-    fc2_gather.send(4, ready=ready)
+    ready = (queries[1], mixed[1]) + fc1_gather.got(2, 1, 6, 5)
+    fc1_gather.send(3, 7, ready=ready)
+    fc2_gather.send(4, 2, ready=ready)
     kept = lax.dynamic_slice(second_columns, (core * half, row_width), (half, half))
     received = lax.dynamic_slice(second_columns, ((1 - core) * half, row_width), (half, half))
     received = swap_core(after(received, mixed[1]))
     attend_pair(2, kept, *ready)
-    ready = (queries[2], received) + fc1_gather.got(6, 3, 5)
-    fc1_gather.send(7, ready=ready)
-    fc2_gather.send(2, ready=ready)
+    ready = (queries[2], received) + fc1_gather.got(3, 7) + fc2_gather.got(2)
+    fc2_gather.send(1, ready=ready)
+    fc2_gather.send(3, ready=ready)
     other_grads = swap_chip(after(take(cotangent, 1 - chip), *ready))
     attend_pair(3, *ready)
     own_grads = jnp.concatenate([take(cotangent, chip), after(other_grads, queries[3])], axis=0)
     full_out = jnp.concatenate(in_core_order(kept, received, core, 1), axis=1)
     full_qkv = (qkv_first, second_columns[:, :row_width])
-    ready = (own_grads, queries[3]) + fc2_gather.got(4, 2) + fc1_gather.got(7)
+    ready = (own_grads, queries[3]) + fc2_gather.got(4, 1)
     all_context = after(context[3], *ready)
-    fc2_gather.send(1, 3, 6, ready=ready)
+    fc2_gather.send(5, 6, ready=ready)
     attn_branch = sum_partner([(all_context, full_out)], NN) + bias_out
     residual_mid = own_inputs.astype(F32) + attn_branch
     normal_two, scale_two = normalize(residual_mid)
-    h_two = with_partner((normal_two * gain_two + bias_two).astype(BF16))
+    h_two = (normal_two * gain_two + bias_two).astype(BF16)
+    h_two = with_partner(after(h_two, *fc2_gather.got(3)))
     all_grads = with_partner(after(own_grads, residual_mid))
     full_fc1 = fc1_gather.result()
-    h_two = after(h_two, *fc2_gather.got(1, 3, 6))
-    fc2_gather.send(5, ready=(h_two,))
+    h_two = after(h_two, *fc2_gather.got(5, 6))
+    fc2_gather.send(7, ready=(h_two,))
     active, slope = gelu_both(dot(h_two, full_fc1) + bias_fc1)
     active, slope = active.astype(BF16), slope.astype(BF16)
-    active = after(active, *fc2_gather.got(5))
-    fc2_gather.send(7, ready=(active,))
     fc2_product = dot(active, all_grads, TN).astype(BF16)
     fc2_scatter = Scatter(fc2_product)
 
@@ -645,19 +683,7 @@
         for part in (chip, 1 - chip)
     ]
     fc1_scatter = Scatter(fc1_product, halves=fc1_halves)
-    mlp_branch = sum_partner([(after(active, fc1_scatter.sent), full_fc2)], NN) + bias_fc2
-    residual_out = residual_mid + mlp_branch
-    counted = own_valid.astype(F32)[:, None]
-    squares = jnp.stack(
-        [
-            jnp.sum(counted * residual_out * residual_out),
-            jnp.sum(counted * attn_branch * attn_branch),
-            jnp.sum(counted * mlp_branch * mlp_branch),
-            jnp.sum(counted),
-        ]
-    )
-    low_output = residual_out.astype(BF16)
-    grad_h_two = sum_partner([(after(grad_hidden, residual_out), full_fc1)], NT)
+    grad_h_two = sum_partner([(after(grad_hidden, fc1_scatter.sent), full_fc1)], NT)
     grad_residual = own_grads.astype(F32) + normalize_back(
         normal_two, scale_two, grad_h_two, gain_two
     )
@@ -690,7 +716,6 @@
     ready = (sums[0], fc1_scatter.crossed) + fc2_scatter.got("side")
     fc2_scatter.near(*ready)
     fc1_scatter.cross(*ready)
-    low_output = after(low_output, *ready)
     back_pair(1, grad_out, *ready, *fc2_scatter.got("keep"), *fc1_scatter.got("keep"))
     early = jnp.concatenate([dot(h_one, halves[0], TN).astype(BF16), grad_out], axis=1)
     ready = (sums[1],) + fc2_scatter.got("near_sums") + fc1_scatter.got("side")
@@ -699,7 +724,6 @@
     early_scatter = Scatter(early, *ready)
     ready += fc2_scatter.got("keep") + fc1_scatter.got("keep") + early_scatter.got("keep")
     back_pair(2, *ready)
-    output = all_clips(low_output, sums[2])
     ready = (sums[2],) + fc2_scatter.got("far_sums") + fc1_scatter.got("near_sums")
     fc2_scatter.chips(*ready)
     fc1_scatter.far(*ready)
@@ -710,54 +734,65 @@
     fc2_scatter.cores(*ready)
     early_scatter.near(*ready)
     late_scatter = Scatter(dot(after(h_one, fc1_scatter.sums, *ready), halves[1], TN))
+    mlp_branch = sum_partner([(after(active, *late_scatter.got("keep")), full_fc2)], NN) + bias_fc2
+    residual_out = residual_mid + mlp_branch
+    low_output = residual_out.astype(BF16)
+    counted = own_valid.astype(F32)[:, None]
+    squares = [
+        jnp.sum(column_sum(counted * part * part).reshape(-1, PAIR), axis=0)
+        for part in (residual_out, attn_branch, mlp_branch)
+    ]
+    squares.append(jnp.sum(jnp.pad(own_valid.astype(F32), (0, -own_rows % PAIR)).reshape(-1, PAIR), axis=0))
+    late_scatter.near(low_output)
+    early_scatter.far(low_output)
     ready = late_scatter.got("keep")
     grad_h_one = sum_partner(
-        [(after(halves[0], *ready), full_qkv[0]), (halves[1], full_qkv[1])], NT
+        [(after(halves[n], *ready), full_qkv[n]) for n in range(2)], NT
     )
-    late_scatter.near()
+    late_scatter.far(grad_h_one)
     grad_h_one = after(grad_h_one, *late_scatter.got("keep"))
     own_normal, own_scale = normalize(own_inputs.astype(F32))
     low_input_grad = (
         grad_residual + normalize_back(own_normal, own_scale, grad_h_one, gain_one)
     ).astype(BF16)
-    input_grad = all_clips(low_input_grad)
-
-    def by_core(values):
-        full = jnp.zeros((2, values.shape[0]), F32)
-        return lax.dynamic_update_index_in_dim(full, values, core, 0).reshape(-1)
-
-    vector_grads = [
+
+    lines = [
         column_sum(grad_h_one * own_normal),
         column_sum(grad_h_one),
-        by_core(jnp.concatenate([part[0] for part in sums])),
-        by_core(jnp.concatenate([part[1] for part in sums])),
         column_sum(own_grad_attn),
         column_sum(grad_h_two * normal_two),
         column_sum(grad_h_two),
         column_sum(own_grads),
+        column_sum(grad_hidden),
     ]
-    hidden_sums = jnp.zeros((groups, 2, half_rows), F32)
-    hidden_sums = lax.dynamic_update_index_in_dim(
-        hidden_sums, column_sum(grad_hidden).reshape(groups, half_rows), core, 1
-    )
-    by_group = [part.reshape(groups, own_width) for part in vector_grads]
-    by_group.append(hidden_sums.reshape(groups, hidden_rows))
-    by_group.append(jnp.broadcast_to(squares, (groups, 4)))
-    by_group = jnp.concatenate(by_group, axis=1).astype(BF16)
-    by_group = jnp.pad(by_group, ((0, 0), (0, 16 * PAIR - by_group.shape[1])))
-    by_group = after(by_group, *late_scatter.got("near_sums"))
-    vector_scatter = Scatter(by_group.reshape(groups * 16, PAIR))
-    ready = vector_scatter.got("keep")
-    early_scatter.far(*ready)
-    late_scatter.far(*ready)
+    if groups == 8:
+        packed = pack_lines([line[None] for line in lines], sums, jnp.stack(squares))
+    else:
+        def by_core(values):
+            full = jnp.zeros((2, values.shape[0]), F32)
+            return lax.dynamic_update_index_in_dim(full, values, core, 0).reshape(-1)
+
+        wide = lines[:2] + [by_core(jnp.concatenate([part[n] for part in sums])) for n in range(2)]
+        wide = [line.reshape(groups, own_width) for line in wide + lines[2:6]]
+        hidden_sums = jnp.zeros((groups, 2, half_rows), F32)
+        hidden_sums = lax.dynamic_update_index_in_dim(
+            hidden_sums, lines[6].reshape(groups, half_rows), core, 1
+        )
+        wide.append(hidden_sums.reshape(groups, hidden_rows))
+        wide.append(jnp.zeros((groups, 12 * PAIR - used)))
+        wide.append(jnp.broadcast_to(jnp.concatenate(squares), (groups, 4 * PAIR)))
+        packed = jnp.concatenate(wide, axis=1).astype(BF16).reshape(groups * 16, PAIR)
+    packed = add_low(packed, swap_chip(packed))
+    packed = add_low(packed, swap_core(packed))
+    vector_scatter = Scatter(packed, ordered=True)
     vector_scatter.near()
-    fc1_scatter.cores(*ready)
+    early_scatter.chips(packed)
+    late_scatter.chips(packed)
+    input_grad = all_clips(after(low_input_grad, packed))
+    output = all_clips(low_output, packed)
     vector_scatter.far()
-    early_scatter.chips()
-    vector_scatter.chips()
-    late_scatter.chips(input_grad)
-    early_scatter.cores()
-    vector_scatter.cores()
+    fc1_scatter.cores(packed)
+    early_scatter.cores(input_grad)
     late_scatter.cores()
 
     def in_columns(values, other, blocks):
@@ -780,11 +815,11 @@
         return both.reshape(own_width, 3 * half)
 
     qkv_grad = in_columns(both_halves(early, late), both_halves(early_other, late_other), 3)
-    flat = vector_scatter.total.astype(F32) + vector_scatter.other_core.astype(F32)
-    flat = flat.reshape(-1)
+    lines = vector_scatter.last()
+    flat = lines[:12].reshape(-1)
     own_vectors = [flat[i * own_width : (i + 1) * own_width] for i in range(8)]
     own_hidden = flat[8 * own_width : used]
-    totals = flat[used : used + 4]
+    totals = jnp.sum(lines[12:], axis=1)
     branch_rms = jnp.sqrt(totals[:3] / (totals[3] * width))
     return (
         output,

time: 556 us -> 519 us (0.933)
  Pallas kernels: 133 us -> 113 us
  starting transfers between devices: 66.5 us -> 54.1 us
  other arithmetic: 67.3 us -> 58.8 us
  local copies, waits for them, and re-layouts: 42.7 us -> 48.8 us
    ppermute x43, starting transfers between devices: 52 us -> 39.7 us  [swap_group(): return lax.ppermute(values, 'fsdp', [(i, i ^ bit) for i in range(8)])]
    pallas_call x4, Pallas kernels: 73.6 us -> 63.2 us  [attend_back(): pl.pallas_call(attend_back_kernel, grid=(1,), in_specs=in_specs, out_spec...]
    pallas_call x4, Pallas kernels: 41.4 us -> 31.8 us  [attend(): pl.pallas_call(attend_kernel, grid=(1,), in_specs=in_specs, out_specs=[ti...]
    reduce_sum x4 -> x1, other arithmetic: 11.3 us -> 4.14 us  [column_sum(): return jnp.sum(values, axis=0, dtype=F32)]
    unnamed x182 -> x220, local copies, waits for them, and re-layouts: 16.6 us -> 23.6 us
    convert_element_type x20, other arithmetic: 17.7 us -> 11 us  [add_low(): return (left.astype(F32) + right.astype(F32)).astype(BF16)]
  transfers between devices with their start and end apart: 68 -> 68, of which waited for: 32 -> 31; matrix products, arithmetic and copies ran while one was open for 24% -> 25% of each run, Pallas kernels for 24% -> 21%
where the time goes in v4:
time: 519 us; the launch traced here: 512 us
  waiting for transfers between devices  137 us (26%)
  Pallas kernels  113 us (22%)
  matrix products  95.6 us (18%)
  other arithmetic  58.8 us (11%)
  starting transfers between devices  54.1 us (10%)
  local copies, waits for them, and re-layouts  48.8 us (9%)
    ppermute x43, waiting for transfers between devices, swap_group(): return lax.ppermute(values, 'fsdp', [(i, i ^ bit) for i in range(8)])  105 us
    dot_general x20, matrix products, dot(): return lax.dot_general(left, right, dims, preferred_element_type=F32)  95.6 us
    pallas_call x4, Pallas kernels, attend_back(): pl.pallas_call(attend_back_kernel, grid=(1,), in_specs=in_specs, out_spec...  63.2 us
    ppermute x43, starting transfers between devices, swap_group(): return lax.ppermute(values, 'fsdp', [(i, i ^ bit) for i in range(8)])  39.7 us
    pallas_call x4, Pallas kernels, attend(): pl.pallas_call(attend_kernel, grid=(1,), in_specs=in_specs, out_specs=[ti...  31.8 us
    ppermute x10, waiting for transfers between devices, swap_chip(): return lax.ppermute(values, 'seq', [(0, 2), (2, 0), (1, 3), (3, 1)])  26 us
    unnamed x220, local copies, waits for them, and re-layouts  23.6 us
    ppermute x10, starting transfers between devices, swap_chip(): return lax.ppermute(values, 'seq', [(0, 2), (2, 0), (1, 3), (3, 1)])  13.3 us
  transfers between devices with their start and end apart: 68, of which 31 were waited for; matrix products, arithmetic and copies ran while one was open for 25% of the time, Pallas kernels for 21%

profile of v4, /device:TPU:0, one launch (start us, length us, event | category | flops | bytes accessed | tf_op | source)
XLA Modules:
  0.0 511.6 jit_solution(1553829208087391299)
XLA Ops:
  19.6 4.7 collective-permute-done.2.refs_2_
  56.3 4.2 fusion.10
  69.2 7.8 %attend.4 = (bf16[1568,512]{1,0:T(8,128)(2,1)S(1)}, bf16[2,1568,128]{2,1,0:T(8,128)(2,1)S(1)}) custom-call(bf16[1568,768]{1,0:T(8,128)(2,1)S(1)} %multiply_convert_fusion.3.q_ref.k_ref.v_ref, bf16[1568,768]{1,0:T(8,128)(2,1)S(1)} %multiply_convert_fusion.3.q_ref.k_ref.v_ref, bf16[1568,768]{1,0:T(8,128)(2,1)S(1)} %multiply_convert_fusion.3.q_ref.k_ref.v_ref, ...), custom_call_target="tpu_custom_call" | custom-call | flops 10000000 | bytes 1048576 | tf_op jit(solution)/shard_map/attend/pallas_call | solution.py:89
  83.8 5.5 %collective-permute-done.15.refs_4_ = bf16[128,2048]{1,0:T(8,128)(2,1)} collective-permute-done((bf16[128,2048]{1,0:T(8,128)(2,1)S(1)}, bf16[128,2048]{1,0:T(8,128)(2,1)}, u32[]{:S(2)}, u32[]{:S(2)}) %collective-permute-start.15) | collective-permute-done | bytes 524320 | tf_op jit(solution)/shard_map/ppermute | solution.py:239
  93.8 6.4 %collective-permute-done.16.refs_7_ = bf16[128,1280]{1,0:T(8,128)(2,1)} collective-permute-done((bf16[128,1280]{1,0:T(8,128)(2,1)}, bf16[128,1280]{1,0:T(8,128)(2,1)}, u32[]{:S(2)}, u32[]{:S(2)}) %collective-permute-start.16) | collective-permute-done | bytes 327712 | tf_op jit(solution)/shard_map/ppermute | solution.py:239
  105.5 4.2 multiply_convert_fusion.2.q_ref.k_ref.v_ref
  110.6 7.8 %attend.5 = (bf16[1568,512]{1,0:T(8,128)(2,1)S(1)}, bf16[2,1568,128]{2,1,0:T(8,128)(2,1)S(1)}) custom-call(bf16[1568,768]{1,0:T(8,128)(2,1)S(1)} %multiply_convert_fusion.3.q_ref.k_ref.v_ref, bf16[1568,768]{1,0:T(8,128)(2,1)S(1)} %multiply_convert_fusion.3.q_ref.k_ref.v_ref, ...), custom_call_target="tpu_custom_call", output_to_operand_aliasing={{0}: (4, {})} | custom-call | flops 10000000 | bytes 1048576 | tf_op jit(solution)/shard_map/attend/pallas_call | solution.py:89
  127.4 8.1 %attend.6 = (bf16[1568,512]{1,0:T(8,128)(2,1)S(1)}, bf16[2,1568,128]{2,1,0:T(8,128)(2,1)S(1)}) custom-call(bf16[1568,768]{1,0:T(8,128)(2,1)S(1)} %copy-done.2, bf16[1568,768]{1,0:T(8,128)(2,1)S(1)} %copy-done.2, bf16[1568,768]{1,0:T(8,128)(2,1)S(1)} %copy-done.2, ...), custom_call_target="tpu_custom_call", output_to_operand_aliasing={{0}: (4, {})} | custom-call | flops 10000000 | bytes 1048576 | tf_op jit(solution)/shard_map/attend/pallas_call | solution.py:89
  137.2 10.9 %collective-permute-done.23.refs_7_ = bf16[128,2048]{1,0:T(8,128)(2,1)} collective-permute-done((bf16[128,2048]{1,0:T(8,128)(2,1)}, bf16[128,2048]{1,0:T(8,128)(2,1)}, u32[]{:S(2)}, u32[]{:S(2)}) %collective-permute-start.23) | collective-permute-done | bytes 524320 | tf_op jit(solution)/shard_map/ppermute | solution.py:239
  150.2 8.1 %attend.7 = (bf16[1568,512]{1,0:T(8,128)(2,1)S(1)}, bf16[2,1568,128]{2,1,0:T(8,128)(2,1)S(1)}) custom-call(bf16[1568,768]{1,0:T(8,128)(2,1)S(1)} %copy-done.2, bf16[1568,768]{1,0:T(8,128)(2,1)S(1)} %copy-done.2, bf16[1568,768]{1,0:T(8,128)(2,1)S(1)} %copy-done.2, ...), custom_call_target="tpu_custom_call", output_to_operand_aliasing={{0}: (4, {})} | custom-call | flops 10000000 | bytes 1048576 | tf_op jit(solution)/shard_map/attend/pallas_call | solution.py:89
  158.3 9.2 %collective-permute-done.25 = bf16[392,1024]{1,0:T(8,128)(2,1)S(1)} collective-permute-done((bf16[392,1024]{1,0:T(8,128)(2,1)S(1)}, bf16[392,1024]{1,0:T(8,128)(2,1)S(1)}, u32[]{:S(2)}, u32[]{:S(2)}) %collective-permute-start.25) | collective-permute-done | bytes 802848 | tf_op jit(solution)/shard_map/ppermute | solution.py:222
  168.9 5.2 %collective-permute-done.26.refs_4_ = bf16[256,1024]{1,0:T(8,128)(2,1)} collective-permute-done((bf16[256,1024]{1,0:T(8,128)(2,1)}, bf16[256,1024]{1,0:T(8,128)(2,1)}, u32[]{:S(2)}, u32[]{:S(2)}) %collective-permute-start.26) | collective-permute-done | bytes 524320 | tf_op jit(solution)/shard_map/ppermute | solution.py:239
  178.7 4.7 fusion.53
  185.7 5.8 %collective-permute-done.29.refs_3_ = bf16[256,1024]{1,0:T(8,128)(2,1)S(1)} collective-permute-done((bf16[256,1024]{1,0:T(8,128)(2,1)}, bf16[256,1024]{1,0:T(8,128)(2,1)S(1)}, u32[]{:S(2)}, u32[]{:S(2)}) %collective-permute-start.29) | collective-permute-done | bytes 524320 | tf_op jit(solution)/shard_map/ppermute | solution.py:239
  199.8 7.3 %collective-permute-done.31.refs_5_ = bf16[256,1024]{1,0:T(8,128)(2,1)} collective-permute-done((bf16[256,1024]{1,0:T(8,128)(2,1)}, bf16[256,1024]{1,0:T(8,128)(2,1)}, u32[]{:S(2)}, u32[]{:S(2)}) %collective-permute-start.31) | collective-permute-done | bytes 524320 | tf_op jit(solution)/shard_map/ppermute | solution.py:239
  208.8 10.5 %multiply_convert_fusion.1 = (bf16[1568,2048]{1,0:T(8,128)(2,1)S(1)}, f32[1568,2048]{1,0:T(8,128)}) fusion(f32[2048]{0:T(1024)S(1)} %bitcast.129, bf16[1568,1024]{1,0:T(8,128)(2,1)S(1)} %pad_maximum_fusion.1, bf16[1024,2048]{1,0:T(8,128)(2,1)S(1)} %in_order.6), kind=kOutput, calls=%fused_computation.8 | convolution fusion | flops 6595936256 | bytes 26681344 | tf_op jit(solution)/shard_map/dot_general | solution.py:25
  219.4 8.3 %convolution_convert_fusion.1.full_ref = bf16[2048,1024]{1,0:T(8,128)(2,1)S(1)} fusion(bf16[1568,2048]{1,0:T(8,128)(2,1)S(1)} %get-tuple-element.207, bf16[1568,1024]{1,0:T(8,128)(2,1)S(1)} %constant_dynamic-update-slice_fusion), kind=kOutput, calls=%fused_computation.35 | convolution fusion | flops 6578765824 | bytes 13828096 | tf_op jit(solution)/shard_map/dot_general | solution.py:25
  232.7 15.2 %convert_reduce_fusion = (f32[2048]{0:T(1024)}, bf16[1568,2048]{1,0:T(8,128)(2,1)S(1)}) fusion(f32[1568,2048]{1,0:T(8,128)} %get-tuple-element.355, f32[2048]{0:T(1024)S(1)} %bitcast.130, bf16[1568,1024]{1,0:T(8,128)(2,1)S(1)} %constant_dynamic-update-slice_fusion, bf16[2048,1024]{1,0:T(8,128)(2,1)S(1)} %in_order.7), kind=kOutput, calls=%fused_computation.6 | convolution fusion | flops 6624835584 | bytes 26689536 | tf_op jit(solution)/shard_map/dot_general | solution.py:25
  247.9 8.8 %convolution_convert_fusion = bf16[1024,2048]{1,0:T(8,128)(2,1)S(1)} fusion(bf16[1568,1024]{1,0:T(8,128)(2,1)S(1)} %pad_maximum_fusion.1, bf16[1568,2048]{1,0:T(8,128)(2,1)S(1)} %get-tuple-element.177), kind=kOutput, calls=%fused_computation.34 | convolution fusion | flops 6578765824 | bytes 13828096 | tf_op jit(solution)/shard_map/dot_general | solution.py:25
  267.3 4.9 multiply_reduce_fusion
  272.2 4.1 convert_reduce_fusion.4
  284.1 15.9 %attend_back.4 = (bf16[1568,768]{1,0:T(8,128)(2,1)S(1)}, f32[2,128]{1,0:T(2,128)S(1)}) custom-call(bf16[2,1568,128]{2,1,0:T(8,128)(2,1)S(1)} %copy-done.26, bf16[1568,768]{1,0:T(8,128)(2,1)S(1)} %multiply_convert_fusion.3.q_ref.k_ref.v_ref, bf16[1568,768]{1,0:T(8,128)(2,1)S(1)} %multiply_convert_fusion.3.q_ref.k_ref.v_ref, ...), custom_call_target="tpu_custom_call" | custom-call | flops 10000000 | bytes 1048576 | tf_op jit(solution)/shard_map/attend_back/pallas_call | solution.py:174
  300.6 11.6 %collective-permute-done.38 = bf16[1024,1024]{1,0:T(8,128)(2,1)} collective-permute-done((bf16[1024,1024]{1,0:T(8,128)(2,1)}, bf16[1024,1024]{1,0:T(8,128)(2,1)}, u32[]{:S(2)}, u32[]{:S(2)}) %collective-permute-start.38) | collective-permute-done | bytes 2097184 | tf_op jit(solution)/shard_map/ppermute | solution.py:239
  324.1 15.7 %attend_back.5 = (bf16[1568,768]{1,0:T(8,128)(2,1)S(1)}, f32[2,128]{1,0:T(2,128)S(1)}) custom-call(bf16[2,1568,128]{2,1,0:T(8,128)(2,1)S(1)} %copy-done.24, bf16[1568,768]{1,0:T(8,128)(2,1)S(1)} %multiply_convert_fusion.3.q_ref.k_ref.v_ref, bf16[1568,768]{1,0:T(8,128)(2,1)S(1)} %multiply_convert_fusion.3.q_ref.k_ref.v_ref, ...), custom_call_target="tpu_custom_call", output_to_operand_aliasing={{0}: (6, {})} | custom-call | flops 10000000 | bytes 1048576 | tf_op jit(solution)/shard_map/attend_back/pallas_call | solution.py:174
  348.5 15.9 %attend_back.6 = (bf16[1568,768]{1,0:T(8,128)(2,1)S(1)}, f32[2,128]{1,0:T(2,128)S(1)}) custom-call(bf16[2,1568,128]{2,1,0:T(8,128)(2,1)S(1)} %copy-done.28, bf16[1568,768]{1,0:T(8,128)(2,1)S(1)} %copy-done.3, bf16[1568,768]{1,0:T(8,128)(2,1)S(1)} %copy-done.3, bf16[1568,512]{1,0:T(8,128)(2,1)S(1)} %convolution_convert_fusion.2.grad_ref, ...), custom_call_target="tpu_custom_call" | custom-call | flops 10000000 | bytes 1048576 | tf_op jit(solution)/shard_map/attend_back/pallas_call | solution.py:174
  367.6 4.6 collective-permute-done.43
  374.2 15.7 %attend_back.7 = (bf16[1568,768]{1,0:T(8,128)(2,1)S(1)}, f32[2,128]{1,0:T(2,128)S(1)}) custom-call(bf16[2,1568,128]{2,1,0:T(8,128)(2,1)S(1)} %copy-done.22, bf16[1568,768]{1,0:T(8,128)(2,1)S(1)} %copy-done.3, bf16[1568,768]{1,0:T(8,128)(2,1)S(1)} %copy-done.3, ...), custom_call_target="tpu_custom_call", output_to_operand_aliasing={{0}: (6, {})} | custom-call | flops 10000000 | bytes 1048576 | tf_op jit(solution)/shard_map/attend_back/pallas_call | solution.py:174
  396.4 4.8 fusion.35
  409.5 6.4 %fusion.23 = (f32[1024]{0:T(1024)S(1)}, f32[1024]{0:T(1024)S(1)}, f32[1024]{0:T(1024)S(1)}, bf16[784,1024]{1,0:T(8,128)(2,1)S(1)}) fusion(f32[784]{0:T(1024)S(1)} %add_convert_fusion.32, f32[784,1024]{1,0:T(8,128)S(1)} %copy-done.55, f32[1024]{0:T(1024)S(1)} %bitcast.169, bf16[784,1024]{1,0:T(8,128)(2,1)} %collective-permute-done.47, ...), kind=kOutput, calls=%fused_computation.43 | convolution fusion | flops 3301979136 | bytes 18668608 | tf_op jit(solution)/shard_map/dot_general | solution.py:25
  416.0 8.1 %collective-permute-done.49 = bf16[512,768]{1,0:T(8,128)(2,1)S(1)} collective-permute-done((bf16[512,768]{1,0:T(8,128)(2,1)S(1)}, bf16[512,768]{1,0:T(8,128)(2,1)S(1)}, u32[]{:S(2)}, u32[]{:S(2)}) %collective-permute-start.49) | collective-permute-done | bytes 786464 | tf_op jit(solution)/shard_map/ppermute | solution.py:239
  438.4 10.2 %collective-permute-done.51 = bf16[256,768]{1,0:T(8,128)(2,1)S(1)} collective-permute-done((bf16[256,768]{1,0:T(8,128)(2,1)S(1)}, bf16[256,768]{1,0:T(8,128)(2,1)S(1)}, u32[]{:S(2)}, u32[]{:S(2)}) %collective-permute-start.51) | collective-permute-done | bytes 393248 | tf_op jit(solution)/shard_map/ppermute | solution.py:239
  482.0 13.6 %collective-permute-done.62 = bf16[128,768]{1,0:T(8,128)(2,1)S(1)} collective-permute-done((bf16[128,768]{1,0:T(8,128)(2,1)S(1)}, bf16[128,768]{1,0:T(8,128)(2,1)S(1)}, u32[]{:S(2)}, u32[]{:S(2)}) %collective-permute-start.62) | collective-permute-done | bytes 196640 | tf_op jit(solution)/shard_map/ppermute | solution.py:222
  (481 shorter events, 233.6 us)
Async XLA Ops:
  9.1 25.7 %collective-permute-start = (bf16[392,1024]{1,0:T(8,128)(2,1)}, bf16[392,1024]{1,0:T(8,128)(2,1)}, u32[]{:S(2)}, u32[]{:S(2)}) collective-permute-start(bf16[392,1024]{1,0:T(8,128)(2,1)} %dynamic-slice_bitcast_fusion.2), channel_id=1, source_target_pairs={{0,16},{16,0},{8,24},{24,8},{1,17},{17,1},{9,25},{25,9},{2,18},{18... | collective-permute-start | bytes 2408456 | tf_op jit(solution)/shard_map/ppermute | solution.py:222
  38.8 24.8 %collective-permute-start.11 = (bf16[128,1280]{1,0:T(8,128)(2,1)S(1)}, bf16[128,1280]{1,0:T(8,128)(2,1)}, u32[]{:S(2)}, u32[]{:S(2)}) collective-permute-start(bf16[128,1280]{1,0:T(8,128)(2,1)S(1)} %copy-done.37), channel_id=1, source_target_pairs={{0,4},{1,5},{2,6},{3,7},{4,0},{5,1},{6,2},{7,3},{8,12},{9,13},{10,... | collective-permute-start | bytes 983048 | tf_op jit(solution)/shard_map/ppermute | solution.py:239
  40.9 22.7 %collective-permute-start.9 = (bf16[128,1280]{1,0:T(8,128)(2,1)S(1)}, bf16[128,1280]{1,0:T(8,128)(2,1)}, u32[]{:S(2)}, u32[]{:S(2)}) collective-permute-start(bf16[128,1280]{1,0:T(8,128)(2,1)S(1)} %copy-done.37), channel_id=1, source_target_pairs={{0,1},{1,0},{2,3},{3,2},{4,5},{5,4},{6,7},{7,6},{8,9},{9,8},{10,11... | collective-permute-start | bytes 983048 | tf_op jit(solution)/shard_map/ppermute | solution.py:239
  42.4 21.2 %collective-permute-start.10 = (bf16[128,1280]{1,0:T(8,128)(2,1)S(1)}, bf16[128,1280]{1,0:T(8,128)(2,1)}, u32[]{:S(2)}, u32[]{:S(2)}) collective-permute-start(bf16[128,1280]{1,0:T(8,128)(2,1)S(1)} %copy-done.37), channel_id=1, source_target_pairs={{0,2},{1,3},{2,0},{3,1},{4,6},{5,7},{6,4},{7,5},{8,10},{9,11},{10,... | collective-permute-start | bytes 983048 | tf_op jit(solution)/shard_map/ppermute | solution.py:239
  63.6 25.6 %collective-permute-start.15 = (bf16[128,2048]{1,0:T(8,128)(2,1)S(1)}, bf16[128,2048]{1,0:T(8,128)(2,1)}, u32[]{:S(2)}, u32[]{:S(2)}) collective-permute-start(bf16[128,2048]{1,0:T(8,128)(2,1)S(1)} %bitcast.125), channel_id=1, source_target_pairs={{0,4},{1,5},{2,6},{3,7},{4,0},{5,1},{6,2},{7,3},{8,12},{9,13},{10,... | collective-permute-start | bytes 1572872 | tf_op jit(solution)/shard_map/ppermute | solution.py:239
  89.7 30.8 %collective-permute-start.17 = (bf16[128,2048]{1,0:T(8,128)(2,1)S(1)}, bf16[128,2048]{1,0:T(8,128)(2,1)}, u32[]{:S(2)}, u32[]{:S(2)}) collective-permute-start(bf16[128,2048]{1,0:T(8,128)(2,1)S(1)} %bitcast.126), channel_id=1, source_target_pairs={{0,2},{1,3},{2,0},{3,1},{4,6},{5,7},{6,4},{7,5},{8,10},{9,11},{10,... | collective-permute-start | bytes 1572872 | tf_op jit(solution)/shard_map/ppermute | solution.py:239
  89.7 30.8 %collective-permute-start.18 = (bf16[128,2048]{1,0:T(8,128)(2,1)S(1)}, bf16[128,2048]{1,0:T(8,128)(2,1)S(1)}, u32[]{:S(2)}, u32[]{:S(2)}) collective-permute-start(bf16[128,2048]{1,0:T(8,128)(2,1)S(1)} %bitcast.127), channel_id=1, source_target_pairs={{0,1},{1,0},{2,3},{3,2},{4,5},{5,4},{6,7},{7,6},{8,9},{9,8},{10,11... | collective-permute-start | bytes 1572872 | tf_op jit(solution)/shard_map/ppermute | solution.py:239
  91.3 30.0 %collective-permute-start.19 = (bf16[128,2048]{1,0:T(8,128)(2,1)}, bf16[128,2048]{1,0:T(8,128)(2,1)}, u32[]{:S(2)}, u32[]{:S(2)}) collective-permute-start(bf16[128,2048]{1,0:T(8,128)(2,1)} %collective-permute-done.15.refs_4_), channel_id=1, source_target_pairs={{0,2},{1,3},{2,0},{3,1},{4,6},{5,7},{6,4},{7,5},{8,10},{9,11},{10,... | collective-permute-start | bytes 1572872 | tf_op jit(solution)/shard_map/ppermute | solution.py:239
  93.3 28.0 %collective-permute-start.20 = (bf16[128,2048]{1,0:T(8,128)(2,1)}, bf16[128,2048]{1,0:T(8,128)(2,1)S(1)}, u32[]{:S(2)}, u32[]{:S(2)}) collective-permute-start(bf16[128,2048]{1,0:T(8,128)(2,1)} %collective-permute-done.15.refs_4_), channel_id=1, source_target_pairs={{0,1},{1,0},{2,3},{3,2},{4,5},{5,4},{6,7},{7,6},{8,9},{9,8},{10,11... | collective-permute-start | bytes 1572872 | tf_op jit(solution)/shard_map/ppermute | solution.py:239
  122.6 25.4 %collective-permute-start.23 = (bf16[128,2048]{1,0:T(8,128)(2,1)}, bf16[128,2048]{1,0:T(8,128)(2,1)}, u32[]{:S(2)}, u32[]{:S(2)}) collective-permute-start(bf16[128,2048]{1,0:T(8,128)(2,1)} %collective-permute-done.19.refs_6_), channel_id=1, source_target_pairs={{0,1},{1,0},{2,3},{3,2},{4,5},{5,4},{6,7},{7,6},{8,9},{9,8},{10,11... | collective-permute-start | bytes 1572872 | tf_op jit(solution)/shard_map/ppermute | solution.py:239
  124.1 23.9 %collective-permute-start.24 = (bf16[256,1024]{1,0:T(8,128)(2,1)}, bf16[256,1024]{1,0:T(8,128)(2,1)}, u32[]{:S(2)}, u32[]{:S(2)}) collective-permute-start(bf16[256,1024]{1,0:T(8,128)(2,1)} %constant_dynamic-slice_fusion.8.refs_0_), channel_id=1, source_target_pairs={{0,2},{1,3},{2,0},{3,1},{4,6},{5,7},{6,4},{7,5},{8,10},{9,11},{10,... | collective-permute-start | bytes 1572872 | tf_op jit(solution)/shard_map/ppermute | solution.py:239
  148.0 19.5 %collective-permute-start.25 = (bf16[392,1024]{1,0:T(8,128)(2,1)S(1)}, bf16[392,1024]{1,0:T(8,128)(2,1)S(1)}, u32[]{:S(2)}, u32[]{:S(2)}) collective-permute-start(bf16[392,1024]{1,0:T(8,128)(2,1)S(1)} %get-tuple-element.160), channel_id=1, source_target_pairs={{0,16},{16,0},{8,24},{24,8},{1,17},{17,1},{9,25},{25,9},{2,18},{18... | collective-permute-start | bytes 2408456 | tf_op jit(solution)/shard_map/ppermute | solution.py:222
  148.5 25.6 %collective-permute-start.26 = (bf16[256,1024]{1,0:T(8,128)(2,1)}, bf16[256,1024]{1,0:T(8,128)(2,1)}, u32[]{:S(2)}, u32[]{:S(2)}) collective-permute-start(bf16[256,1024]{1,0:T(8,128)(2,1)} %constant_dynamic-slice_fusion.8.refs_0_), channel_id=1, source_target_pairs={{0,4},{1,5},{2,6},{3,7},{4,0},{5,1},{6,2},{7,3},{8,12},{9,13},{10,... | collective-permute-start | bytes 1572872 | tf_op jit(solution)/shard_map/ppermute | solution.py:239
  148.5 25.6 %collective-permute-start.27 = (bf16[256,1024]{1,0:T(8,128)(2,1)}, bf16[256,1024]{1,0:T(8,128)(2,1)S(1)}, u32[]{:S(2)}, u32[]{:S(2)}) collective-permute-start(bf16[256,1024]{1,0:T(8,128)(2,1)} %constant_dynamic-slice_fusion.8.refs_0_), channel_id=1, source_target_pairs={{0,1},{1,0},{2,3},{3,2},{4,5},{5,4},{6,7},{7,6},{8,9},{9,8},{10,11... | collective-permute-start | bytes 1572872 | tf_op jit(solution)/shard_map/ppermute | solution.py:239
  197.2 22.1 %collective-permute-start.33 = (bf16[784,1024]{1,0:T(8,128)(2,1)S(1)}, bf16[784,1024]{1,0:T(8,128)(2,1)S(1)}, u32[]{:S(2)}, u32[]{:S(2)}) collective-permute-start(bf16[784,1024]{1,0:T(8,128)(2,1)S(1)} %copy-done.58), channel_id=1, source_target_pairs={{0,8},{8,0},{16,24},{24,16},{1,9},{9,1},{17,25},{25,17},{2,10},{10... | collective-permute-start | bytes 4816904 | tf_op jit(solution)/shard_map/ppermute | solution.py:218
  207.3 23.5 %collective-permute-start.34 = (bf16[256,1024]{1,0:T(8,128)(2,1)}, bf16[256,1024]{1,0:T(8,128)(2,1)S(1)}, u32[]{:S(2)}, u32[]{:S(2)}) collective-permute-start(bf16[256,1024]{1,0:T(8,128)(2,1)} %collective-permute-done.32.refs_6_), channel_id=1, source_target_pairs={{0,1},{1,0},{2,3},{3,2},{4,5},{5,4},{6,7},{7,6},{8,9},{9,8},{10,11... | collective-permute-start | bytes 1572872 | tf_op jit(solution)/shard_map/ppermute | solution.py:239
  263.9 48.4 %collective-permute-start.38 = (bf16[1024,1024]{1,0:T(8,128)(2,1)}, bf16[1024,1024]{1,0:T(8,128)(2,1)}, u32[]{:S(2)}, u32[]{:S(2)}) collective-permute-start(bf16[1024,1024]{1,0:T(8,128)(2,1)} %get-tuple-element.181), channel_id=1, source_target_pairs={{0,1},{1,0},{2,3},{3,2},{4,5},{5,4},{6,7},{7,6},{8,9},{9,8},{10,11... | collective-permute-start | bytes 6291464 | tf_op jit(solution)/shard_map/ppermute | solution.py:239
  264.4 48.0 %collective-permute-start.35 = (bf16[1024,1024]{1,0:T(8,128)(2,1)}, bf16[1024,1024]{1,0:T(8,128)(2,1)}, u32[]{:S(2)}, u32[]{:S(2)}) collective-permute-start(bf16[1024,1024]{1,0:T(8,128)(2,1)} %constant_dynamic-slice_fusion.1), channel_id=1, source_target_pairs={{0,16},{16,0},{8,24},{24,8},{1,17},{17,1},{9,25},{25,9},{2,18},{18... | collective-permute-start | bytes 6291464 | tf_op jit(solution)/shard_map/ppermute | solution.py:222
  315.4 27.8 %collective-permute-start.39 = (bf16[512,1024]{1,0:T(8,128)(2,1)S(1)}, bf16[512,1024]{1,0:T(8,128)(2,1)S(1)}, u32[]{:S(2)}, u32[]{:S(2)}) collective-permute-start(bf16[512,1024]{1,0:T(8,128)(2,1)S(1)} %get-tuple-element.184), channel_id=1, source_target_pairs={{0,1},{1,0},{2,3},{3,2},{4,5},{5,4},{6,7},{7,6},{8,9},{9,8},{10,11... | collective-permute-start | bytes 3145736 | tf_op jit(solution)/shard_map/ppermute | solution.py:239
  319.5 24.2 %collective-permute-start.41 = (bf16[512,1024]{1,0:T(8,128)(2,1)S(1)}, bf16[512,1024]{1,0:T(8,128)(2,1)S(1)}, u32[]{:S(2)}, u32[]{:S(2)}) collective-permute-start(bf16[512,1024]{1,0:T(8,128)(2,1)S(1)} %get-tuple-element.293), channel_id=1, source_target_pairs={{0,2},{1,3},{2,0},{3,1},{4,6},{5,7},{6,4},{7,5},{8,10},{9,11},{10,... | collective-permute-start | bytes 3145736 | tf_op jit(solution)/shard_map/ppermute | solution.py:239
  344.1 23.5 %collective-permute-start.42 = (bf16[256,1024]{1,0:T(8,128)(2,1)S(1)}, bf16[256,1024]{1,0:T(8,128)(2,1)S(1)}, u32[]{:S(2)}, u32[]{:S(2)}) collective-permute-start(bf16[256,1024]{1,0:T(8,128)(2,1)S(1)} %get-tuple-element.303), channel_id=1, source_target_pairs={{0,2},{1,3},{2,0},{3,1},{4,6},{5,7},{6,4},{7,5},{8,10},{9,11},{10,... | collective-permute-start | bytes 1572872 | tf_op jit(solution)/shard_map/ppermute | solution.py:239
  345.9 26.3 %collective-permute-start.43 = (bf16[256,1024]{1,0:T(8,128)(2,1)S(1)}, bf16[256,1024]{1,0:T(8,128)(2,1)S(1)}, u32[]{:S(2)}, u32[]{:S(2)}) collective-permute-start(bf16[256,1024]{1,0:T(8,128)(2,1)S(1)} %get-tuple-element.301), channel_id=1, source_target_pairs={{0,4},{1,5},{2,6},{3,7},{4,0},{5,1},{6,2},{7,3},{8,12},{9,13},{10,... | collective-permute-start | bytes 1572872 | tf_op jit(solution)/shard_map/ppermute | solution.py:239
  347.8 42.1 %collective-permute-start.46 = (bf16[512,1280]{1,0:T(8,128)(2,1)S(1)}, bf16[512,1280]{1,0:T(8,128)(2,1)S(1)}, u32[]{:S(2)}, u32[]{:S(2)}) collective-permute-start(bf16[512,1280]{1,0:T(8,128)(2,1)S(1)} %get-tuple-element.202), channel_id=1, source_target_pairs={{0,1},{1,0},{2,3},{3,2},{4,5},{5,4},{6,7},{7,6},{8,9},{9,8},{10,11... | collective-permute-start | bytes 3932168 | tf_op jit(solution)/shard_map/ppermute | solution.py:239
  403.8 63.8 %collective-permute-start.65 = (bf16[128,1024]{1,0:T(8,128)(2,1)S(1)}, bf16[128,1024]{1,0:T(8,128)(2,1)}, u32[]{:S(2)}, u32[]{:S(2)}) collective-permute-start(bf16[128,1024]{1,0:T(8,128)(2,1)S(1)} %add_convert_fusion.19), channel_id=1, source_target_pairs={{0,16},{16,0},{8,24},{24,8},{1,17},{17,1},{9,25},{25,9},{2,18},{18... | collective-permute-start | bytes 786440 | tf_op jit(solution)/shard_map/ppermute | solution.py:222
  404.4 19.6 %collective-permute-start.49 = (bf16[512,768]{1,0:T(8,128)(2,1)S(1)}, bf16[512,768]{1,0:T(8,128)(2,1)S(1)}, u32[]{:S(2)}, u32[]{:S(2)}) collective-permute-start(bf16[512,768]{1,0:T(8,128)(2,1)S(1)} %copy-done.52), channel_id=1, source_target_pairs={{0,1},{1,0},{2,3},{3,2},{4,5},{5,4},{6,7},{7,6},{8,9},{9,8},{10,11... | collective-permute-start | bytes 2359304 | tf_op jit(solution)/shard_map/ppermute | solution.py:239
  405.6 26.2 %collective-permute-start.58 = (bf16[256,1280]{1,0:T(8,128)(2,1)S(1)}, bf16[256,1280]{1,0:T(8,128)(2,1)S(1)}, u32[]{:S(2)}, u32[]{:S(2)}) collective-permute-start(bf16[256,1280]{1,0:T(8,128)(2,1)S(1)} %get-tuple-element.295), channel_id=1, source_target_pairs={{0,2},{1,3},{2,0},{3,1},{4,6},{5,7},{6,4},{7,5},{8,10},{9,11},{10,... | collective-permute-start | bytes 1966088 | tf_op jit(solution)/shard_map/ppermute | solution.py:239
  426.8 36.2 %collective-permute-start.48 = (bf16[392,1024]{1,0:T(8,128)(2,1)}, bf16[392,1024]{1,0:T(8,128)(2,1)}, u32[]{:S(2)}, u32[]{:S(2)}) collective-permute-start(bf16[392,1024]{1,0:T(8,128)(2,1)} %slice.388), channel_id=1, source_target_pairs={{0,16},{16,0},{8,24},{24,8},{1,17},{17,1},{9,25},{25,9},{2,18},{18... | collective-permute-start | bytes 2408456 | tf_op jit(solution)/shard_map/ppermute | solution.py:222
  432.8 32.8 %collective-permute-start.59 = (bf16[128,1280]{1,0:T(8,128)(2,1)}, bf16[128,1280]{1,0:T(8,128)(2,1)}, u32[]{:S(2)}, u32[]{:S(2)}) collective-permute-start(bf16[128,1280]{1,0:T(8,128)(2,1)} %add_convert_fusion.17), channel_id=1, source_target_pairs={{0,4},{1,5},{2,6},{3,7},{4,0},{5,1},{6,2},{7,3},{8,12},{9,13},{10,... | collective-permute-start | bytes 983048 | tf_op jit(solution)/shard_map/ppermute | solution.py:239
  455.4 24.7 %collective-permute-start.61 = (bf16[128,768]{1,0:T(8,128)(2,1)}, bf16[128,768]{1,0:T(8,128)(2,1)S(1)}, u32[]{:S(2)}, u32[]{:S(2)}) collective-permute-start(bf16[128,768]{1,0:T(8,128)(2,1)} %get-tuple-element.321), channel_id=1, source_target_pairs={{0,4},{1,5},{2,6},{3,7},{4,0},{5,1},{6,2},{7,3},{8,12},{9,13},{10,... | collective-permute-start | bytes 589832 | tf_op jit(solution)/shard_map/ppermute | solution.py:239
  463.9 33.5 %collective-permute-start.54 = (bf16[392,1024]{1,0:T(8,128)(2,1)}, bf16[392,1024]{1,0:T(8,128)(2,1)}, u32[]{:S(2)}, u32[]{:S(2)}) collective-permute-start(bf16[392,1024]{1,0:T(8,128)(2,1)} %slice.335), channel_id=1, source_target_pairs={{0,16},{16,0},{8,24},{24,8},{1,17},{17,1},{9,25},{25,9},{2,18},{18... | collective-permute-start | bytes 2408456 | tf_op jit(solution)/shard_map/ppermute | solution.py:222
  466.7 33.2 %collective-permute-start.60 = (bf16[128,1280]{1,0:T(8,128)(2,1)S(1)}, bf16[128,1280]{1,0:T(8,128)(2,1)S(1)}, u32[]{:S(2)}, u32[]{:S(2)}) collective-permute-start(bf16[128,1280]{1,0:T(8,128)(2,1)S(1)} %add_convert_fusion.16), channel_id=1, source_target_pairs={{0,16},{16,0},{8,24},{24,8},{1,17},{17,1},{9,25},{25,9},{2,18},{18... | collective-permute-start | bytes 983048 | tf_op jit(solution)/shard_map/ppermute | solution.py:222
  470.9 29.3 %collective-permute-start.66 = (bf16[128,2048]{1,0:T(8,128)(2,1)}, bf16[128,2048]{1,0:T(8,128)(2,1)}, u32[]{:S(2)}, u32[]{:S(2)}) collective-permute-start(bf16[128,2048]{1,0:T(8,128)(2,1)} %pad_maximum_fusion.12), channel_id=1, source_target_pairs={{0,8},{8,0},{16,24},{24,16},{1,9},{9,1},{17,25},{25,17},{2,10},{10... | collective-permute-start | bytes 1572872 | tf_op jit(solution)/shard_map/ppermute | solution.py:218
  (143 other events, 1363.1 us)
